TPU v7x, 512 devices: a whole 4x4x16 slice. The times are simulated.
512 devices in a mesh: dp: 32 (over z, core), tensor: 16 (over x, y).
Axes of the slice: x: 4, y: 4, z: 16, core: 2. Of those that a mesh axis runs over, the one named last changes fastest.
Arguments:
- grad_query: bfloat16 [8192, 8192], P('dp', 'tensor'), may hold values from -6 to 6
- query_weight: bfloat16 [8192, 8192], P('dp', 'tensor')
- grad_resid: bfloat16 [8192, 8192], P('dp', 'tensor'), may hold values from -6 to 6
- embeds: bfloat16 [8192, 8192], P('dp', 'tensor')
- norm_gain: float32 [8192], P('tensor'), may hold values from 0.1 to 1.9
- img_pos: int32 [32, 128], P('dp'), may hold values from 0 to 255, as said below
- img_count: int32 [32], P('dp'), may hold values from 64 to 128, as said below
- img_dest: int32 [32, 128], P('dp'), may hold values from 0 to 31, as said below
- merge_weight: bfloat16 [5120, 8192], P('dp', 'tensor'), may hold values from -0.0625 to 0.0625
- merge_pre: bfloat16 [6144, 5120], P('dp', 'tensor'), may hold values from -5 to 5
Outputs:
- grad_pre: float32 [6144, 5120], P('dp', 'tensor')
Inputs may be any that keep to these rules, and one draw needn't show every extreme that they name: `img_pos`: positions of one device are distinct. `img_count`: at least 64 on every device; some device has 128. `img_dest`: among the rows of one device no encoder device is named more than 6 times; the first 6 rows of every device name one common encoder device, which so receives 6 live rows from every device.
All inputs are finite; a program needn't handle non-finite values.
Results may differ from a plain program's by a relative error of at most 0.034.
Values may be sent and summed in bfloat16 or wider, within the bound.
No kernel may reach another device: no remote copies, remote signals or barrier semaphores. Data moves between devices by JAX's collectives and lax.ppermute only.
A program may use at most 64 MiB of HBM per device.

v0:
```python
import jax
import jax.numpy as jnp
from jax import lax
from jax.sharding import PartitionSpec as P

D = 8192


NORM_EPS = 1e-06


def gelu_slope(pre):
    value = pre.astype(jnp.float32)
    cdf_part = 0.5 * (1.0 + lax.erf(value * 0.7071067811865476))
    pdf_part = jnp.exp(-0.5 * value * value) * 0.3989422804014327
    return cdf_part + value * pdf_part


def transposed_product(left, right):
    return lax.dot_general(
        left, right, (((1,), (1,)), ((), ())), preferred_element_type=jnp.float32
    )


def local(
    grad_query,
    query_weight,
    grad_resid,
    embeds,
    norm_gain,
    img_pos,
    img_count,
    img_dest,
    merge_weight,
    merge_pre,
):
    groups = lax.axis_size("dp")
    capacity = merge_pre.shape[0] // groups
    positions = img_pos[0]
    image_count = positions.shape[0]
    picked = jnp.take(grad_query, positions, axis=0)
    partial_value = transposed_product(
        picked, lax.all_gather(query_weight, "dp", axis=0, tiled=True)
    )
    normal_grad = lax.psum_scatter(
        partial_value.astype(jnp.bfloat16), "tensor", scatter_dimension=1, tiled=True
    ).astype(jnp.float32)
    inputs = jnp.take(embeds, positions, axis=0).astype(jnp.float32)
    residual = jnp.take(grad_resid, positions, axis=0).astype(jnp.float32)
    scaled = norm_gain[None, :] * normal_grad
    squares, inner_sum = lax.psum(
        (jnp.sum(inputs * inputs, axis=1), jnp.sum(scaled * inputs, axis=1)), "tensor"
    )
    inverse = lax.rsqrt(squares / D + NORM_EPS)
    handoff = residual + inverse[:, None] * scaled - inputs * (inverse**3 * inner_sum / D)[:, None]
    handoff = handoff.astype(jnp.bfloat16)
    is_live = jnp.arange(image_count, dtype=jnp.int32) < img_count[0]
    target_dev = img_dest[0]
    dest_hot = (
        (target_dev[:, None] == jnp.arange(groups, dtype=jnp.int32)[None, :]) & is_live[:, None]
    ).astype(jnp.int32)
    earlier = jnp.cumsum(dest_hot, axis=0) - dest_hot
    slot_index = jnp.sum(earlier * dest_hot, axis=1)
    target = jnp.where(is_live, target_dev * capacity + slot_index, -1)
    placing = jnp.arange(groups * capacity, dtype=jnp.int32)[:, None] == target[None, :]
    merge_full = lax.all_gather(merge_weight, "dp", axis=0, tiled=True)
    outbox = jnp.dot(
        placing.astype(jnp.bfloat16), handoff, preferred_element_type=jnp.float32
    ).astype(jnp.bfloat16)
    outbox = outbox.reshape(groups, capacity, handoff.shape[1])
    partial_hidden = jnp.einsum(
        "sjd,hd->sjh",
        lax.all_to_all(outbox, "dp", split_axis=0, concat_axis=0, tiled=True),
        merge_full,
        preferred_element_type=jnp.float32,
    )
    hidden_grad = lax.psum_scatter(
        partial_hidden.astype(jnp.bfloat16), "tensor", scatter_dimension=2, tiled=True
    ).astype(jnp.float32)
    hidden_grad = hidden_grad.reshape(groups * capacity, hidden_grad.shape[2])
    return hidden_grad * gelu_slope(merge_pre)


def solution(mesh):
    in_specs = (
        P("dp", "tensor"),
        P("dp", "tensor"),
        P("dp", "tensor"),
        P("dp", "tensor"),
        P("tensor"),
        P("dp", None),
        P("dp"),
        P("dp", None),
        P("dp", "tensor"),
        P("dp", "tensor"),
    )
    out_specs = P("dp", "tensor")
    return jax.shard_map(local, mesh=mesh, in_specs=in_specs, out_specs=out_specs, check_vma=False)
```

profile of v0, /device:TPU:1, one launch (start us, length us, event | category | flops | bytes accessed | tf_op | source)
XLA Modules:
  0.0 393.7 jit_solution(10084197249841985198)
XLA Ops:
  6.5 0.0 copy-start
  6.5 0.0 all-gather.3.cloned.1.call-start
  6.5 0.7 all-gather.3.cloned.1.call-update
  7.3 0.0 reduce-scatter.5.cloned.1.call-start
  7.3 0.7 compare_select_fusion
  8.0 0.0 copy-done
  8.0 0.8 gather_fusion.2
  8.8 0.7 compare_and_fusion
  9.5 0.0 copy-start.1
  9.5 0.0 copy-start.2
  9.5 0.0 copy-start.4
  9.5 0.0 copy-start.5
  9.5 85.3 %all-gather.3.cloned.1.call-done = bf16[8192,512]{1,0:T(8,128)(2,1)} async-done(((bf16[256,512]{1,0:T(8,128)(2,1)}), bf16[8192,512]{1,0:T(8,128)(2,1)}) %all-gather.3.cloned.1.call-update) | async-done | bytes 8388624 | tf_op jit(solution)/shard_map/all_gather | solution.py:43
  94.8 7.6 %convolution_convert_fusion = bf16[128,8192]{1,0:T(8,128)(2,1)} fusion(bf16[8192,512]{1,0:T(8,128)(2,1)} %all-gather.3.cloned.1.call-done, bf16[128,512]{1,0:T(8,128)(2,1)S(1)} %gather_fusion.2, pred[128]{0:T(512)(128)(4,1)S(1)} %compare_and_fusion), kind=kOutput, calls=%fused_computation.3 | convolution fusion | flops 1074855936 | bytes 10616960 | tf_op jit(solution)/shard_map/dot_general | solution.py:20
  102.4 0.0 reduce-scatter.5.cloned.1.call-update
  102.4 0.0 all-gather.5.cloned.1.call-start
  102.5 0.7 all-gather.5.cloned.1.call-update
  103.1 0.0 copy-done.1
  103.2 0.8 gather_fusion.1
  104.7 0.0 copy-done.2
  104.7 0.8 gather_fusion
  105.5 0.0 copy-done.4
  105.5 0.1 fusion.24
  105.6 0.2 reduce_window_sum.11
  105.8 0.2 select_reduce_fusion
  106.0 80.7 %reduce-scatter.5.cloned.1.call-done = bf16[128,512]{1,0:T(8,128)(2,1)} async-done(((bf16[128,8192]{1,0:T(8,128)(2,1)}), bf16[128,512]{1,0:T(8,128)(2,1)}) %reduce-scatter.5.cloned.1.call-update) | async-done | bytes 131088 | tf_op jit(solution)/shard_map/reduce_scatter | solution.py:45
  186.7 0.0 copy-done.5
  186.7 1.1 fusion.8
  187.8 30.9 %all-reduce = (f32[128]{0:T(128)S(1)}, f32[128]{0:T(128)S(1)}) all-reduce(f32[128]{0:T(128)S(1)} %get-tuple-element.7, f32[128]{0:T(128)S(1)} %get-tuple-element.6), channel_id=1, replica_groups=mesh['dp'=32,'tensor'=16] {'tensor'}, use_global_device_ids=true, to_apply=%region_6.8 | all-reduce | flops 256 | bytes 2048 | tf_op jit(solution)/shard_map/psum | solution.py:51
  218.7 1.2 convolution_convert_fusion.2
  220.0 0.8 reshape.30
  220.7 21.9 %all-to-all-start = ((bf16[32,6,512]{2,1,0:T(8,128)(2,1)}), bf16[32,6,512]{2,1,0:T(8,128)(2,1)S(1)}, u32[]{:S(2)}, u32[]{:S(2)}) async-start(bf16[32,6,512]{2,1,0:T(8,128)(2,1)} %reshape.30), calls=%async_computation.1 | async-start | bytes 524288 | tf_op jit(solution)/shard_map/all_to_all | solution.py:73
  242.7 0.0 reduce-scatter.7.cloned.1.call-start
  242.7 31.5 %all-gather.5.cloned.1.call-done = bf16[5120,512]{1,0:T(8,128)(2,1)} async-done(((bf16[160,512]{1,0:T(8,128)(2,1)}), bf16[5120,512]{1,0:T(8,128)(2,1)}) %all-gather.5.cloned.1.call-update) | async-done | bytes 5242896 | tf_op jit(solution)/shard_map/all_gather | solution.py:66
  274.2 0.0 all-to-all-done
  274.2 4.3 %convolution_convert_fusion.1 = bf16[32,6,5120]{2,0,1:T(8,128)(2,1)S(1)} fusion(bf16[5120,512]{1,0:T(8,128)(2,1)} %all-gather.5.cloned.1.call-done, bf16[32,6,512]{2,1,0:T(8,128)(2,1)S(1)} %all-to-all-done), kind=kOutput, calls=%fused_computation.4 | convolution fusion | flops 1007616000 | bytes 7405568 | tf_op jit(solution)/shard_map/sjd,hd->sjh/dot_general | solution.py:71
  278.6 8.2 %copy.16 = bf16[32,6,5120]{0,1,2:T(8,128)(2,1)} copy(bf16[32,6,5120]{2,0,1:T(8,128)(2,1)S(1)} %convolution_convert_fusion.1) | data formatting | bytes 3932160
  286.8 12.7 %reshape.69 = bf16[5120,192]{1,0:T(8,128)(2,1)} reshape(bf16[5120,6,32]{2,1,0:T(8,128)(2,1)} %bitcast.21) | data formatting | bytes 3932160
  299.5 0.0 copy-start.3
  299.5 0.0 reduce-scatter.7.cloned.1.call-update
  299.5 85.0 %reduce-scatter.7.cloned.1.call-done = bf16[320,192]{1,0:T(8,128)(2,1)} async-done(((bf16[5120,192]{1,0:T(8,128)(2,1)}), bf16[320,192]{1,0:T(8,128)(2,1)}) %reduce-scatter.7.cloned.1.call-update) | async-done | bytes 122896
  384.5 1.2 reshape.70
  385.8 0.4 copy.17
  386.2 0.1 copy.15
  386.3 0.0 copy-done.3
  386.3 0.8 fusion.5
  (5 shorter events, 0.1 us)
Async XLA Ops:
  6.5 1.4 copy-start
  6.5 88.3 %all-gather.3.cloned.1.call-start = ((), (), s32[]{:S(2)}) async-start(), calls=%async_computation.3 | async-start | bytes 8650752 | tf_op jit(solution)/shard_map/all_gather | solution.py:43
  7.3 179.4 %reduce-scatter.5.cloned.1.call-start = ((), (), s32[]{:S(2)}) async-start(), calls=%async_computation.4 | async-start | bytes 2228224 | tf_op jit(solution)/shard_map/reduce_scatter | solution.py:45
  9.5 93.7 %copy-start.1 = (bf16[256,512]{1,0:T(8,128)(2,1)S(1)}, bf16[256,512]{1,0:T(8,128)(2,1)}, u32[]{:S(2)}) copy-start(bf16[256,512]{1,0:T(8,128)(2,1)} %param.15) | copy-start | bytes 786436
  9.5 95.2 %copy-start.2 = (bf16[256,512]{1,0:T(8,128)(2,1)S(1)}, bf16[256,512]{1,0:T(8,128)(2,1)}, u32[]{:S(2)}) copy-start(bf16[256,512]{1,0:T(8,128)(2,1)} %param.14) | copy-start | bytes 786436
  9.5 96.0 %copy-start.4 = (s32[1,128]{1,0:T(1,128)S(1)}, s32[1,128]{1,0:T(1,128)}, u32[]{:S(2)}) copy-start(s32[1,128]{1,0:T(1,128)} %param.19) | copy-start | bytes 1540
  9.5 177.2 %copy-start.5 = (f32[512]{0:T(512)S(1)}, f32[512]{0:T(512)}, u32[]{:S(2)}) copy-start(f32[512]{0:T(512)} %param.16) | copy-start | bytes 6148
  102.4 171.8 %all-gather.5.cloned.1.call-start = ((), (), s32[]{:S(2)}) async-start(), calls=%async_computation.5 | async-start | bytes 5406720 | tf_op jit(solution)/shard_map/all_gather | solution.py:66
  220.7 53.5 %all-to-all-start = ((bf16[32,6,512]{2,1,0:T(8,128)(2,1)}), bf16[32,6,512]{2,1,0:T(8,128)(2,1)S(1)}, u32[]{:S(2)}, u32[]{:S(2)}) async-start(bf16[32,6,512]{2,1,0:T(8,128)(2,1)} %reshape.30), calls=%async_computation.1 | async-start | bytes 524288 | tf_op jit(solution)/shard_map/all_to_all | solution.py:73
  242.7 141.8 %reduce-scatter.7.cloned.1.call-start = ((), (), s32[]{:S(2)}) async-start(), calls=%async_computation.6 | async-start | bytes 2785280
  299.5 86.8 %copy-start.3 = (bf16[192,320]{1,0:T(8,128)(2,1)S(1)}, bf16[192,320]{1,0:T(8,128)(2,1)}, u32[]{:S(2)}) copy-start(bf16[192,320]{1,0:T(8,128)(2,1)} %param.21) | copy-start | bytes 368644
Sparse Core Ops, SparseCore 0:
  9.5 85.2 all-gather.2
  102.5 84.1 reduce-scatter.4
  189.1 85.1 all-gather.4
  299.6 84.8 reduce-scatter.6
where the time goes:
time: 395 us; the launch traced here: 394 us
  waiting for transfers between devices  284 us (72%)
  blocking collectives  30.9 us (8%)
  local copies, waits for them, and re-layouts  26 us (7%)
  starting transfers between devices  22 us (6%)
  between operations  13.9 us (4%)
  matrix products  13.2 us (3%)
    unnamed x5, waiting for transfers between devices  86.5 us
    all_gather x1, waiting for transfers between devices, local(): lax.all_gather(query_weight, 'dp', axis=0, tiled=True)  85.3 us
    reduce_scatter x1, waiting for transfers between devices, local(): lax.psum_scatter(partial_value.astype(jnp.bfloat16), 'tensor', scatter_di...  80.7 us
    all_gather x1, waiting for transfers between devices, local(): merge_full = lax.all_gather(merge_weight, 'dp', axis=0, tiled=True)  31.5 us
    psum x1, blocking collectives, local(): lax.psum((jnp.sum(inputs * inputs, axis=1), jnp.sum(scaled * inputs, axis...  30.9 us
    unnamed x16, local copies, waits for them, and re-layouts  22.6 us
    all_to_all x1, starting transfers between devices, local(): lax.all_to_all(outbox, 'dp', split_axis=0, concat_axis=0, tiled=True)  21.9 us
  transfers between devices with their start and end apart: 5, of which 4 were waited for; matrix products, arithmetic and copies ran while one was open for 2% of the time, Pallas kernels for 0%

commit v1 on v0

v1 whole, which is shorter than its diff:
```python
import jax
import jax.numpy as jnp
from jax import lax
from jax.experimental import pallas as pl
from jax.experimental.pallas import tpu as pltpu
from jax.sharding import PartitionSpec as P

D = 8192
NORM_EPS = 1e-06
VMEM_BYTES = 40 * 1024 * 1024


def gelu_slope(pre):
    value = pre.astype(jnp.float32)
    cdf_part = 0.5 * (1.0 + lax.erf(value * 0.7071067811865476))
    pdf_part = jnp.exp(-0.5 * value * value) * 0.3989422804014327
    return cdf_part + value * pdf_part


def product_kernel(left_ref, right_ref, out_ref):
    right = right_ref[...].reshape(-1, right_ref.shape[-1])
    out_ref[0] = lax.dot_general(
        left_ref[...], right, (((1,), (1,)), ((), ())), preferred_element_type=jnp.float32
    ).astype(out_ref.dtype)


def block_products(left, gathered, first, count, shares):
    rows, depth = left.shape
    per_share = gathered.shape[0] // shares
    return pl.pallas_call(
        product_kernel,
        grid=(shares,),
        in_specs=[
            pl.BlockSpec((rows, depth), lambda i: (0, 0)),
            pl.BlockSpec(
                (pl.Element(per_share), pl.Element(count), pl.Element(depth)),
                lambda i: (i * per_share, first, 0),
            ),
        ],
        out_specs=pl.BlockSpec((1, rows, per_share * count), lambda i: (i, 0, 0)),
        out_shape=jax.ShapeDtypeStruct((shares, rows, per_share * count), jnp.bfloat16),
        compiler_params=pltpu.CompilerParams(vmem_limit_bytes=VMEM_BYTES),
    )(left, gathered)


def local(
    grad_query,
    query_weight,
    grad_resid,
    embeds,
    norm_gain,
    img_pos,
    img_count,
    img_dest,
    merge_weight,
    merge_pre,
):
    groups = lax.axis_size("dp")
    shares = lax.axis_size("tensor")
    capacity = merge_pre.shape[0] // groups
    query_rows = query_weight.shape[0]
    merge_rows = merge_weight.shape[0]
    positions = img_pos[0]
    image_count = positions.shape[0]
    weights = lax.all_gather(jnp.concatenate([query_weight, merge_weight], axis=0), "dp", axis=0)
    picked = jnp.take(grad_query, positions, axis=0)
    inputs = jnp.take(embeds, positions, axis=0).astype(jnp.float32)
    residual = jnp.take(grad_resid, positions, axis=0).astype(jnp.float32)
    is_live = jnp.arange(image_count, dtype=jnp.int32) < img_count[0]
    target_dev = img_dest[0]
    dest_hot = (
        (target_dev[:, None] == jnp.arange(groups, dtype=jnp.int32)[None, :]) & is_live[:, None]
    ).astype(jnp.int32)
    earlier = jnp.cumsum(dest_hot, axis=0) - dest_hot
    slot_index = jnp.sum(earlier * dest_hot, axis=1)
    target = jnp.where(is_live, target_dev * capacity + slot_index, -1)
    placing = jnp.arange(groups * capacity, dtype=jnp.int32)[:, None] == target[None, :]

    partial_value = block_products(picked, weights, 0, query_rows, shares)
    normal_grad = jnp.sum(
        lax.all_to_all(partial_value, "tensor", 0, 0, tiled=True).astype(jnp.float32), axis=0
    )
    scaled = norm_gain[None, :] * normal_grad
    stats = jnp.stack([jnp.sum(inputs * inputs, axis=1), jnp.sum(scaled * inputs, axis=1)])
    stats = lax.all_to_all(
        jnp.broadcast_to(stats[None], (shares,) + stats.shape), "tensor", 0, 0, tiled=True
    )
    squares, inner_sum = jnp.sum(stats, axis=0)
    inverse = lax.rsqrt(squares / D + NORM_EPS)
    handoff = residual + inverse[:, None] * scaled - inputs * (inverse**3 * inner_sum / D)[:, None]
    handoff = handoff.astype(jnp.bfloat16)
    outbox = jnp.dot(
        placing.astype(jnp.bfloat16), handoff, preferred_element_type=jnp.float32
    ).astype(jnp.bfloat16)
    outbox = outbox.reshape(groups, capacity, handoff.shape[1])
    received = lax.all_to_all(outbox, "dp", split_axis=0, concat_axis=0, tiled=True)
    received = received.reshape(groups * capacity, handoff.shape[1])
    partial_hidden = block_products(received, weights, query_rows, merge_rows, shares)
    hidden_grad = jnp.sum(
        lax.all_to_all(partial_hidden, "tensor", 0, 0, tiled=True).astype(jnp.float32), axis=0
    )
    return hidden_grad * gelu_slope(merge_pre)


def solution(mesh):
    in_specs = (
        P("dp", "tensor"),
        P("dp", "tensor"),
        P("dp", "tensor"),
        P("dp", "tensor"),
        P("tensor"),
        P("dp", None),
        P("dp"),
        P("dp", None),
        P("dp", "tensor"),
        P("dp", "tensor"),
    )
    out_specs = P("dp", "tensor")
    return jax.shard_map(local, mesh=mesh, in_specs=in_specs, out_specs=out_specs, check_vma=False)
```

time: 395 us -> 254 us (0.64)
  waiting for transfers between devices: 284 us -> 129 us
  blocking collectives: 30.9 us -> 65.4 us
  Pallas kernels: 0 us -> 23.6 us
  local copies, waits for them, and re-layouts: 26 us -> 3.87 us
  matrix products: 13.2 us -> 0.34 us
  starting transfers between devices: 22 us -> 11.7 us
    unnamed x5 -> x1, waiting for transfers between devices: 86.5 us -> 0.02 us
    reduce_scatter x1 -> x0, waiting for transfers between devices: 80.7 us -> none  [local(): lax.psum_scatter(partial_value.astype(jnp.bfloat16), 'tensor', scatter_di...]
    all_to_all x0 -> x2, blocking collectives: none -> 65.4 us  [the longest x1 33.5 us: local(): lax.all_to_all(outbox, 'dp', split_axis=0, concat_axis=0, tiled=True)]
    all_to_all x1 -> x2, waiting for transfers between devices: 0.01 us -> 32.7 us  [the longest x1 27.2 us: local(): lax.all_to_all(partial_value, 'tensor', 0, 0, tiled=True)]
    psum x1 -> x0, blocking collectives: 30.9 us -> none  [local(): lax.psum((jnp.sum(inputs * inputs, axis=1), jnp.sum(scaled * inputs, axis...]
    pallas_call x0 -> x2, Pallas kernels: none -> 23.6 us  [block_products(): pl.pallas_call(product_kernel, grid=(shares,), in_specs=[pl.BlockSpec((ro...]
    unnamed x16 -> x14, local copies, waits for them, and re-layouts: 22.6 us -> 0.56 us
    all_gather x2 -> x1, waiting for transfers between devices: 117 us -> 96.1 us  [local(): lax.all_gather(jnp.concatenate([query_weight, merge_weight], axis=0), 'dp...]
  transfers between devices with their start and end apart: 5 -> 3, of which waited for: 4 -> 3; matrix products, arithmetic and copies ran while one was open for 2% -> 1% of each run, Pallas kernels for 0% -> 0%
where the time goes in v1:
time: 254 us; the launch traced here: 253 us
  waiting for transfers between devices  129 us (51%)
  blocking collectives  65.4 us (26%)
  Pallas kernels  23.6 us (9%)
  between operations  14.2 us (6%)
  starting transfers between devices  11.7 us (5%)
  other arithmetic  4.85 us (2%)
  local copies, waits for them, and re-layouts  3.87 us (2%)
    all_gather x1, waiting for transfers between devices, local(): lax.all_gather(jnp.concatenate([query_weight, merge_weight], axis=0), 'dp...  96.1 us
    all_to_all x1, blocking collectives, local(): lax.all_to_all(outbox, 'dp', split_axis=0, concat_axis=0, tiled=True)  33.5 us
    all_to_all x1, blocking collectives, local(): lax.all_to_all(partial_hidden, 'tensor', 0, 0, tiled=True)  31.9 us
    all_to_all x1, waiting for transfers between devices, local(): lax.all_to_all(partial_value, 'tensor', 0, 0, tiled=True)  27.2 us
    pallas_call x2, Pallas kernels, block_products(): pl.pallas_call(product_kernel, grid=(shares,), in_specs=[pl.BlockSpec((ro...  23.6 us
    all_to_all x1, starting transfers between devices, local(): lax.all_to_all(partial_value, 'tensor', 0, 0, tiled=True)  6.67 us
    all_to_all x1, waiting for transfers between devices, local(): lax.all_to_all(jnp.broadcast_to(stats[None], (shares,) + stats.shape), 't...  5.57 us
  transfers between devices with their start and end apart: 3, of which 3 were waited for; matrix products, arithmetic and copies ran while one was open for 1% of the time, Pallas kernels for 0%

profile of v1, /device:TPU:1, one launch (start us, length us, event | category | flops | bytes accessed | tf_op | source)
XLA Modules:
  0.0 252.9 jit_solution(7539892717023070264)
XLA Ops:
  6.5 0.0 copy-start
  6.5 0.0 copy-start.6
  6.5 0.0 all-gather.3.cloned.1.call-start
  6.5 1.9 pad_maximum_fusion
  8.4 0.0 all-gather.3.cloned.1.call-update
  8.4 0.7 compare_select_fusion
  9.1 0.0 copy-done
  9.1 0.8 gather_fusion.2
  10.0 0.0 copy-done.6
  10.0 0.1 broadcast_select_fusion.left_ref
  10.1 96.1 %all-gather.3.cloned.1.call-done = bf16[13312,512]{1,0:T(8,128)(2,1)} async-done(((bf16[416,512]{1,0:T(8,128)(2,1)}), bf16[13312,512]{1,0:T(8,128)(2,1)}) %all-gather.3.cloned.1.call-update) | async-done | bytes 13631504 | tf_op jit(solution)/shard_map/all_gather | solution.py:65
  106.2 12.8 %shard_map.100 = bf16[16,128,512]{2,1,0:T(8,128)(2,1)} custom-call(bf16[128,512]{1,0:T(8,128)(2,1)S(1)} %broadcast_select_fusion.left_ref, bf16[32,416,512]{2,1,0:T(8,128)(2,1)} %bitcast.25), custom_call_target="tpu_custom_call" | custom-call | tf_op jit(solution)/shard_map/pallas_call | solution.py:30
  119.0 0.0 copy-start.1
  119.0 0.0 copy-start.4
  119.0 6.7 %all-to-all-start = ((bf16[16,128,512]{2,1,0:T(8,128)(2,1)}), bf16[16,128,512]{2,1,0:T(8,128)(2,1)S(1)}, u32[]{:S(2)}, u32[]{:S(2)}) async-start(bf16[16,128,512]{2,1,0:T(8,128)(2,1)} %shard_map.100), calls=%async_computation | async-start | bytes 4194304 | tf_op jit(solution)/shard_map/all_to_all | solution.py:81
  125.6 0.0 copy-done.1
  125.7 0.0 copy-start.5
  125.7 0.0 copy-start.2
  125.7 0.8 gather_fusion.1
  127.2 0.0 copy-done.4
  127.2 0.1 fusion.19
  127.3 0.2 reduce_window_sum.11
  127.5 0.2 select_reduce_fusion
  127.7 27.2 %all-to-all-done = bf16[16,128,512]{2,1,0:T(8,128)(2,1)S(1)} async-done(((bf16[16,128,512]{2,1,0:T(8,128)(2,1)}), bf16[16,128,512]{2,1,0:T(8,128)(2,1)S(1)}, u32[]{:S(2)}, u32[]{:S(2)}) %all-to-all-start) | async-done | bytes 2097184 | tf_op jit(solution)/shard_map/all_to_all | solution.py:81
  154.8 0.3 convert_reduce_fusion.1
  155.1 0.0 copy-done.5
  155.1 0.2 fusion.7
  155.4 0.6 broadcast_in_dim.16
  156.0 5.1 %all-to-all-start.1 = ((f32[16,2,128]{2,1,0:T(2,128)}), f32[16,2,128]{2,1,0:T(2,128)S(1)}, u32[]{:S(2)}, u32[]{:S(2)}) async-start(f32[16,2,128]{2,1,0:T(2,128)} %broadcast_in_dim.16), calls=%async_computation.1 | async-start | bytes 32768 | tf_op jit(solution)/shard_map/all_to_all | solution.py:85
  161.1 0.0 copy-done.2
  161.1 0.8 gather_fusion
  161.9 5.6 %all-to-all-done.1 = f32[16,2,128]{2,1,0:T(2,128)S(1)} async-done(((f32[16,2,128]{2,1,0:T(2,128)}), f32[16,2,128]{2,1,0:T(2,128)S(1)}, u32[]{:S(2)}, u32[]{:S(2)}) %all-to-all-start.1) | async-done | bytes 16416 | tf_op jit(solution)/shard_map/all_to_all | solution.py:85
  167.5 0.3 convolution_convert_fusion
  167.9 0.1 reshape.49
  168.0 33.5 %all_to_all.20 = bf16[32,6,512]{2,1,0:T(8,128)(2,1)S(1)} all-to-all(bf16[32,6,512]{2,1,0:T(8,128)(2,1)S(1)} %reshape.49), channel_id=1, replica_groups=mesh['dp'=32,'tensor'=16] {'dp'}, dimensions={0} | all-to-all | bytes 393216 | tf_op jit(solution)/shard_map/all_to_all | solution.py:96
  201.5 0.1 reshape.50.left_ref
  201.5 10.8 %shard_map.101 = bf16[16,192,320]{2,1,0:T(8,128)(2,1)S(1)} custom-call(bf16[192,512]{1,0:T(8,128)(2,1)S(1)} %reshape.50.left_ref, bf16[32,416,512]{2,1,0:T(8,128)(2,1)} %bitcast.26), custom_call_target="tpu_custom_call" | custom-call | tf_op jit(solution)/shard_map/pallas_call | solution.py:30
  212.4 31.9 %all_to_all.21 = bf16[16,192,320]{2,1,0:T(8,128)(2,1)S(1)} all-to-all(bf16[16,192,320]{2,1,0:T(8,128)(2,1)S(1)} %shard_map.101), channel_id=1, replica_groups=mesh['dp'=32,'tensor'=16] {'tensor'}, dimensions={0} | all-to-all | bytes 3932160 | tf_op jit(solution)/shard_map/all_to_all | solution.py:100
  244.3 0.0 copy-start.3
  244.3 0.4 convert_reduce_fusion
  244.7 0.5 copy-done.3
  245.2 0.8 fusion.4
  (8 shorter events, 0.1 us)
Async XLA Ops:
  6.5 2.6 %copy-start = (bf16[256,512]{1,0:T(8,128)(2,1)S(1)}, bf16[256,512]{1,0:T(8,128)(2,1)}, u32[]{:S(2)}) copy-start(bf16[256,512]{1,0:T(8,128)(2,1)} %param.12) | copy-start | bytes 786436
  6.5 3.4 %copy-start.6 = (s32[1,128]{1,0:T(1,128)S(1)}, s32[1,128]{1,0:T(1,128)}, u32[]{:S(2)}) copy-start(s32[1,128]{1,0:T(1,128)} %param.17) | copy-start | bytes 1540
  6.5 99.7 %all-gather.3.cloned.1.call-start = ((), (), s32[]{:S(2)}) async-start(), calls=%async_computation.4 | async-start | bytes 14057472 | tf_op jit(solution)/shard_map/all_gather | solution.py:65
  119.0 6.7 %copy-start.1 = (bf16[256,512]{1,0:T(8,128)(2,1)S(1)}, bf16[256,512]{1,0:T(8,128)(2,1)}, u32[]{:S(2)}) copy-start(bf16[256,512]{1,0:T(8,128)(2,1)} %param.15) | copy-start | bytes 786436
  119.0 8.2 %copy-start.4 = (s32[1,128]{1,0:T(1,128)S(1)}, s32[1,128]{1,0:T(1,128)}, u32[]{:S(2)}) copy-start(s32[1,128]{1,0:T(1,128)} %param.19) | copy-start | bytes 1540
  119.0 35.9 %all-to-all-start = ((bf16[16,128,512]{2,1,0:T(8,128)(2,1)}), bf16[16,128,512]{2,1,0:T(8,128)(2,1)S(1)}, u32[]{:S(2)}, u32[]{:S(2)}) async-start(bf16[16,128,512]{2,1,0:T(8,128)(2,1)} %shard_map.100), calls=%async_computation | async-start | bytes 4194304 | tf_op jit(solution)/shard_map/all_to_all | solution.py:81
  125.7 29.5 %copy-start.5 = (f32[512]{0:T(512)S(1)}, f32[512]{0:T(512)}, u32[]{:S(2)}) copy-start(f32[512]{0:T(512)} %param.16) | copy-start | bytes 6148
  125.7 35.4 %copy-start.2 = (bf16[256,512]{1,0:T(8,128)(2,1)S(1)}, bf16[256,512]{1,0:T(8,128)(2,1)}, u32[]{:S(2)}) copy-start(bf16[256,512]{1,0:T(8,128)(2,1)} %param.14) | copy-start | bytes 786436
  156.0 11.5 %all-to-all-start.1 = ((f32[16,2,128]{2,1,0:T(2,128)}), f32[16,2,128]{2,1,0:T(2,128)S(1)}, u32[]{:S(2)}, u32[]{:S(2)}) async-start(f32[16,2,128]{2,1,0:T(2,128)} %broadcast_in_dim.16), calls=%async_computation.1 | async-start | bytes 32768 | tf_op jit(solution)/shard_map/all_to_all | solution.py:85
  244.3 0.9 copy-start.3
Sparse Core Ops, SparseCore 0:
  9.5 96.6 all-gather.2

commit v2 on v0

v2 whole, which is shorter than its diff:
```python
import jax
import jax.numpy as jnp
from jax import lax
from jax.experimental import pallas as pl
from jax.experimental.pallas import tpu as pltpu
from jax.sharding import Mesh
from jax.sharding import PartitionSpec as P

D = 8192
NORM_EPS = 1e-06
VMEM_BYTES = 24 * 1024 * 1024
LANES = 128
DP = ("zh", "zl", "core")
TP = ("x", "y")


def gelu_slope(pre):
    value = pre.astype(jnp.float32)
    cdf_part = 0.5 * (1.0 + lax.erf(value * 0.7071067811865476))
    pdf_part = jnp.exp(-0.5 * value * value) * 0.3989422804014327
    return cdf_part + value * pdf_part


def query_kernel(rows_ref, weight_ref, out_ref, turned):
    parts, count, depth = rows_ref.shape

    @pl.when(pl.program_id(0) == 0)
    def _():
        turned[...] = rows_ref[...].reshape(parts * count, depth).T

    weight = weight_ref[...].reshape(-1, depth)
    product = jnp.dot(weight, turned[...], preferred_element_type=jnp.float32)
    product = product.astype(out_ref.dtype)
    for part in range(parts):
        out_ref[part] = product[:, part * count : (part + 1) * count]


def query_products(rows, weights):
    parts, count, depth = rows.shape
    blocks, height, _ = weights.shape
    steps = blocks // 2
    return pl.pallas_call(
        query_kernel,
        grid=(steps,),
        in_specs=[
            pl.BlockSpec((parts, count, depth), lambda i: (0, 0, 0)),
            pl.BlockSpec((2, height, depth), lambda i: (i, 0, 0)),
        ],
        out_specs=pl.BlockSpec((parts, 2 * height, count), lambda i: (i, 0, 0)),
        out_shape=jax.ShapeDtypeStruct((steps * parts, 2 * height, count), jnp.bfloat16),
        scratch_shapes=[pltpu.VMEM((depth, parts * count), jnp.bfloat16)],
        compiler_params=pltpu.CompilerParams(vmem_limit_bytes=VMEM_BYTES),
    )(rows, weights)


def handoff_kernel(capacity, grad_ref, input_ref, resid_ref, gain_ref, stat_ref, target_ref, out_ref):
    width, count = grad_ref.shape
    stats = jnp.sum(stat_ref[...], axis=0)
    inverse = lax.rsqrt(stats[0:1] / D + NORM_EPS)
    factor = inverse * inverse * inverse * stats[1:2] / D
    scaled = gain_ref[...] * grad_ref[...].astype(jnp.float32)
    handoff = (
        resid_ref[...].astype(jnp.float32)
        + inverse * scaled
        - input_ref[...].astype(jnp.float32) * factor
    ).astype(jnp.bfloat16)
    place = lax.broadcasted_iota(jnp.int32, (out_ref.shape[0], count), 0) - target_ref[...]
    total = jnp.zeros(out_ref.shape, jnp.float32)
    for block in range(width // LANES):
        hot = (place == block * capacity).astype(jnp.bfloat16)
        total += lax.dot_general(
            hot,
            handoff[block * LANES : (block + 1) * LANES],
            (((1,), (1,)), ((), ())),
            preferred_element_type=jnp.float32,
        )
    out_ref[...] = total.astype(out_ref.dtype)


def merge_kernel(capacity, box_ref, weight_ref, out_ref, turned):
    width, rows = turned.shape
    chunks = width // LANES

    @pl.when(pl.program_id(0) == 0)
    def _():
        box = box_ref[...]
        row = lax.broadcasted_iota(jnp.int32, (rows, box.shape[0]), 0)
        spot = lax.broadcasted_iota(jnp.int32, (rows, box.shape[0]), 1)
        source = (row * 10923) >> 16
        ahead = spot - (row + source * (capacity * (chunks - 1)))
        for block in range(chunks):
            hot = (ahead == block * capacity).astype(jnp.bfloat16)
            piece = jnp.dot(hot, box, preferred_element_type=jnp.float32)
            turned[block * LANES : (block + 1) * LANES] = piece.T.astype(jnp.bfloat16)

    height = weight_ref.shape[1]
    for part in range(out_ref.shape[0]):
        for half in range(2):
            product = jnp.dot(
                weight_ref[2 * part + half], turned[...], preferred_element_type=jnp.float32
            )
            out_ref[part, :, half * rows : (half + 1) * rows] = product.astype(out_ref.dtype)


def merge_products(box, weights, capacity, shares, steps):
    blocks, height, width = weights.shape
    rows = box.shape[0] * box.shape[1] // width
    per_step = shares // steps
    return pl.pallas_call(
        lambda *refs: merge_kernel(capacity, *refs),
        grid=(steps,),
        in_specs=[
            pl.BlockSpec(box.shape, lambda i: (0, 0)),
            pl.BlockSpec((blocks // steps, height, width), lambda i: (i, 0, 0)),
        ],
        out_specs=pl.BlockSpec((per_step, height, 2 * rows), lambda i: (i, 0, 0)),
        out_shape=jax.ShapeDtypeStruct((shares, height, 2 * rows), jnp.bfloat16),
        scratch_shapes=[pltpu.VMEM((width, rows), jnp.bfloat16)],
        compiler_params=pltpu.CompilerParams(vmem_limit_bytes=VMEM_BYTES),
    )(box, weights)


def local(
    grad_query,
    query_weight,
    grad_resid,
    embeds,
    norm_gain,
    img_pos,
    img_count,
    img_dest,
    merge_weight,
    merge_pre,
):
    groups = lax.axis_size(DP)
    shares = lax.axis_size(TP)
    side = lax.axis_size("zl")
    capacity = merge_pre.shape[0] // groups
    positions = img_pos[0]
    image_count = positions.shape[0]
    width = embeds.shape[1]

    query_full = lax.all_gather(query_weight, ("zh", "core"), axis=0)
    merge_weight, query_full = lax.optimization_barrier((merge_weight, query_full))
    merge_full = lax.all_gather(merge_weight, DP, axis=0)
    picked = lax.all_gather(jnp.take(grad_query, positions, axis=0), "zl", axis=0)
    inputs = jnp.take(embeds, positions, axis=0).T
    residual = jnp.take(grad_resid, positions, axis=0).T
    gain = norm_gain[:, None]
    wide = inputs.astype(jnp.float32)
    squares = jnp.sum(wide * wide, axis=0)
    is_live = jnp.arange(image_count, dtype=jnp.int32) < img_count[0]
    target_dev = img_dest[0]
    dest_hot = (
        (target_dev[:, None] == jnp.arange(groups, dtype=jnp.int32)[None, :]) & is_live[:, None]
    ).astype(jnp.int32)
    earlier = jnp.cumsum(dest_hot, axis=0) - dest_hot
    slot_index = jnp.sum(earlier * dest_hot, axis=1)
    pitch = capacity * (width // LANES)
    target = jnp.where(is_live, target_dev * pitch + slot_index, -groups * pitch)

    partial_value = query_products(picked, query_full)
    swapped = lax.all_to_all(partial_value, TP, 0, 0, tiled=True)
    normal_grad = jnp.sum(swapped.astype(jnp.float32), axis=0).astype(jnp.bfloat16)
    exchange = [(b * side + a, a * side + b) for a in range(side) for b in range(side)]
    normal_grad = lax.ppermute(normal_grad, ("zl", "y"), exchange)
    inner = jnp.sum(gain * normal_grad.astype(jnp.float32) * wide, axis=0)
    stats = jnp.stack([squares, inner])
    stats = lax.all_to_all(
        jnp.broadcast_to(stats[None], (shares,) + stats.shape), TP, 0, 0, tiled=True
    )
    outbox = pl.pallas_call(
        lambda *refs: handoff_kernel(capacity, *refs),
        out_shape=jax.ShapeDtypeStruct((groups * pitch, LANES), jnp.bfloat16),
        compiler_params=pltpu.CompilerParams(vmem_limit_bytes=VMEM_BYTES),
    )(normal_grad, inputs, residual, gain, stats, target[None])
    received = lax.all_to_all(outbox.reshape(groups, pitch, LANES), DP, 0, 0, tiled=True)
    partial_hidden = merge_products(
        received.reshape(groups * pitch, LANES), merge_full, capacity, shares, 4
    )
    hidden = lax.all_to_all(partial_hidden, TP, 0, 0, tiled=True)
    hidden = jnp.sum(hidden.astype(jnp.float32), axis=0)
    rows = merge_pre.shape[0]
    hidden = jnp.concatenate([hidden[:, :rows].T, hidden[:, rows:].T], axis=1)
    return hidden * gelu_slope(merge_pre)


def solution(mesh):
    split = Mesh(mesh.devices.reshape(4, 4, 2, 4, 4), DP + TP)
    in_specs = (
        P(DP, TP),
        P(DP, TP),
        P(DP, TP),
        P(DP, TP),
        P(TP),
        P(DP, None),
        P(DP),
        P(DP, None),
        P(DP, TP),
        P(DP, TP),
    )
    out_specs = P(DP, TP)
    return jax.shard_map(local, mesh=split, in_specs=in_specs, out_specs=out_specs, check_vma=False)
```

time: 395 us -> 229 us (0.58)
  waiting for transfers between devices: 284 us -> 102 us
  blocking collectives: 30.9 us -> 68.2 us
  local copies, waits for them, and re-layouts: 26 us -> 6.65 us
  matrix products: 13.2 us -> 0 us
  Pallas kernels: 0 us -> 6.57 us
  starting transfers between devices: 22 us -> 26.3 us
    unnamed x5 -> x2, waiting for transfers between devices: 86.5 us -> 0.73 us
    reduce_scatter x1 -> x0, waiting for transfers between devices: 80.7 us -> none  [local(): lax.psum_scatter(partial_value.astype(jnp.bfloat16), 'tensor', scatter_di...]
    all_to_all x0 -> x2, blocking collectives: none -> 54.9 us  [the longest x1 28.2 us: local(): lax.all_to_all(outbox.reshape(groups, pitch, LANES), DP, 0, 0, tiled=True)]
    all_gather x2, waiting for transfers between devices: 117 us -> 71.2 us  [the longest x1 71.2 us: local(): query_full = lax.all_gather(query_weight, ('zh', 'core'), axis=0)]
    psum x1 -> x0, blocking collectives: 30.9 us -> none  [local(): lax.psum((jnp.sum(inputs * inputs, axis=1), jnp.sum(scaled * inputs, axis...]
    all_to_all x1 -> x2, waiting for transfers between devices: 0.01 us -> 30 us  [the longest x1 23.7 us: local(): swapped = lax.all_to_all(partial_value, TP, 0, 0, tiled=True)]
    unnamed x16 -> x18, local copies, waits for them, and re-layouts: 22.6 us -> 3.02 us
    all_gather x0 -> x1, blocking collectives: none -> 13.3 us  [local(): lax.all_gather(jnp.take(grad_query, positions, axis=0), 'zl', axis=0)]
  transfers between devices with their start and end apart: 5 -> 5, of which waited for: 4 -> 3; matrix products, arithmetic and copies ran while one was open for 2% -> 3% of each run, Pallas kernels for 0% -> 2%
where the time goes in v2:
time: 229 us; the launch traced here: 228 us
  waiting for transfers between devices  102 us (45%)
  blocking collectives  68.2 us (30%)
  starting transfers between devices  26.3 us (11%)
  between operations  14.3 us (6%)
  local copies, waits for them, and re-layouts  6.65 us (3%)
  Pallas kernels  6.57 us (3%)
  other arithmetic  3.66 us (2%)
    all_gather x1, waiting for transfers between devices, local(): query_full = lax.all_gather(query_weight, ('zh', 'core'), axis=0)  71.2 us
    all_to_all x1, blocking collectives, local(): lax.all_to_all(outbox.reshape(groups, pitch, LANES), DP, 0, 0, tiled=True)  28.2 us
    all_to_all x1, blocking collectives, local(): hidden = lax.all_to_all(partial_hidden, TP, 0, 0, tiled=True)  26.7 us
    all_to_all x1, waiting for transfers between devices, local(): swapped = lax.all_to_all(partial_value, TP, 0, 0, tiled=True)  23.7 us
    all_to_all x1, starting transfers between devices, local(): lax.all_to_all(jnp.broadcast_to(stats[None], (shares,) + stats.shape), TP...  19.3 us
    all_gather x1, blocking collectives, local(): lax.all_gather(jnp.take(grad_query, positions, axis=0), 'zl', axis=0)  13.3 us
    all_to_all x1, starting transfers between devices, local(): swapped = lax.all_to_all(partial_value, TP, 0, 0, tiled=True)  6.29 us
    all_to_all x1, waiting for transfers between devices, local(): lax.all_to_all(jnp.broadcast_to(stats[None], (shares,) + stats.shape), TP...  6.28 us
  transfers between devices with their start and end apart: 5, of which 3 were waited for; matrix products, arithmetic and copies ran while one was open for 3% of the time, Pallas kernels for 2%

profile of v2, /device:TPU:1, one launch (start us, length us, event | category | flops | bytes accessed | tf_op | source)
XLA Modules:
  0.0 227.6 jit_solution(14476723743691576514)
XLA Ops:
  6.5 0.0 copy-start
  6.5 0.0 all-gather.6.cloned.1.call-start
  6.5 0.7 all-gather.6.cloned.1.call-update
  7.3 0.0 all-gather.8.cloned.1.call-start
  7.3 71.2 %all-gather.6.cloned.1.call-done = bf16[2048,512]{1,0:T(8,128)(2,1)} async-done(((bf16[256,512]{1,0:T(8,128)(2,1)}), bf16[2048,512]{1,0:T(8,128)(2,1)}) %all-gather.6.cloned.1.call-update) | async-done | bytes 2097168 | tf_op jit(solution)/shard_map/all_gather | solution.py:143
  78.5 0.0 copy-start.2
  78.5 0.0 all-gather.8.cloned.1.call-update
  78.6 0.8 compare_select_fusion
  79.4 0.0 copy-done
  79.4 0.8 gather_fusion
  80.2 0.7 compare_and_fusion
  80.9 0.1 broadcast_select_fusion
  81.0 13.3 %all-gather = bf16[512,512]{1,0:T(8,128)(2,1)S(1)} all-gather(bf16[128,512]{1,0:T(8,128)(2,1)S(1)} %broadcast_select_fusion), channel_id=2, replica_groups=mesh['zh'=4,'zl'=4,'core'=2,'x'=4,'y'=4] {'zl'}, dimensions={0}, use_global_device_ids=true | all-gather | bytes 655360 | tf_op jit(solution)/shard_map/all_gather | solution.py:146
  94.3 0.0 copy-done.2
  94.3 3.1 %shard_map.100 = bf16[16,512,128]{2,1,0:T(8,128)(2,1)} custom-call(bf16[4,128,512]{2,1,0:T(8,128)(2,1)S(1)} %bitcast.28, bf16[8,256,512]{2,1,0:T(8,128)(2,1)S(1)} %bitcast.29), custom_call_target="tpu_custom_call" | custom-call | tf_op jit(solution)/shard_map/pallas_call | solution.py:42
  97.4 0.0 copy-start.3
  97.4 6.3 %all-to-all-start = ((bf16[16,512,128]{2,1,0:T(8,128)(2,1)}), bf16[16,512,128]{2,1,0:T(8,128)(2,1)S(1)}, u32[]{:S(2)}, u32[]{:S(2)}) async-start(bf16[16,512,128]{2,1,0:T(8,128)(2,1)} %shard_map.100), calls=%async_computation | async-start | bytes 4194304 | tf_op jit(solution)/shard_map/all_to_all | solution.py:163
  103.7 0.0 copy-start.7
  103.7 0.0 copy-start.4
  104.4 0.0 copy-done.3
  104.4 0.8 gather_fusion.2
  105.3 0.1 copy.22
  105.4 0.0 copy-start.6
  105.5 23.7 %all-to-all-done = bf16[16,512,128]{2,1,0:T(8,128)(2,1)S(1)} async-done(((bf16[16,512,128]{2,1,0:T(8,128)(2,1)}), bf16[16,512,128]{2,1,0:T(8,128)(2,1)S(1)}, u32[]{:S(2)}, u32[]{:S(2)}) %all-to-all-start) | async-done | bytes 2097184 | tf_op jit(solution)/shard_map/all_to_all | solution.py:163
  129.1 0.3 reduce_sum.50
  129.4 0.7 collective-permute-start
  130.1 0.0 copy-done.7
  130.1 0.1 fusion.10
  130.2 0.0 copy-done.4
  130.2 0.8 gather_fusion.1
  131.1 0.1 copy.21
  131.2 0.2 reduce_window_sum.11
  131.4 0.2 select_reduce_fusion
  131.6 0.0 collective-permute-done.refs_0_
  131.6 0.0 copy-done.6
  131.6 0.2 fusion.7
  131.7 0.6 broadcast_in_dim.26
  132.4 19.3 %all-to-all-start.1 = ((f32[16,2,128]{2,1,0:T(2,128)}), f32[16,2,128]{2,1,0:T(2,128)S(1)}, u32[]{:S(2)}, u32[]{:S(2)}) async-start(f32[16,2,128]{2,1,0:T(2,128)} %broadcast_in_dim.26), calls=%async_computation.1 | async-start | bytes 32768 | tf_op jit(solution)/shard_map/all_to_all | solution.py:169
  151.6 0.1 copy.23.refs_3_
  151.8 6.3 %all-to-all-done.1.refs_4_ = f32[16,2,128]{2,1,0:T(2,128)S(1)} async-done(((f32[16,2,128]{2,1,0:T(2,128)}), f32[16,2,128]{2,1,0:T(2,128)S(1)}, u32[]{:S(2)}, u32[]{:S(2)}) %all-to-all-start.1) | async-done | bytes 16416 | tf_op jit(solution)/shard_map/all_to_all | solution.py:169
  158.1 0.5 shard_map.101
  158.6 28.2 %all_to_all.20 = bf16[32,24,128]{2,1,0:T(8,128)(2,1)S(1)} all-to-all(bf16[32,24,128]{2,1,0:T(8,128)(2,1)S(1)} %bitcast.30), channel_id=1, replica_groups=mesh['zh'=4,'zl'=4,'core'=2,'x'=4,'y'=4] {'zh','zl','core'}, dimensions={0} | all-to-all | bytes 393216 | tf_op jit(solution)/shard_map/all_to_all | solution.py:177
  186.8 0.0 all-gather.8.cloned.1.call-done
  186.8 0.0 copy-start.1
  186.8 2.5 %copy-done.1 = bf16[5120,512]{1,0:T(8,128)(2,1)S(1)} copy-done((bf16[5120,512]{1,0:T(8,128)(2,1)S(1)}, bf16[5120,512]{1,0:T(8,128)(2,1)}, u32[]{:S(2)}) %copy-start.1) | copy-done | bytes 5242904
  189.3 2.9 %shard_map.102 = bf16[16,160,384]{2,1,0:T(8,128)(2,1)S(1)} custom-call(bf16[768,128]{1,0:T(8,128)(2,1)S(1)} %bitcast.31, bf16[32,160,512]{2,1,0:T(8,128)(2,1)S(1)} %bitcast.27), custom_call_target="tpu_custom_call" | custom-call | tf_op jit(solution)/shard_map/pallas_call | solution.py:109
  192.2 26.7 %all_to_all.21 = bf16[16,160,384]{2,1,0:T(8,128)(2,1)S(1)} all-to-all(bf16[16,160,384]{2,1,0:T(8,128)(2,1)S(1)} %shard_map.102), channel_id=1, replica_groups=mesh['zh'=4,'zl'=4,'core'=2,'x'=4,'y'=4] {'x','y'}, dimensions={0} | all-to-all | bytes 3932160 | tf_op jit(solution)/shard_map/all_to_all | solution.py:181
  218.9 0.0 copy-start.5
  218.9 0.3 convert_reduce_fusion
  219.2 0.1 fusion.11
  219.3 0.1 copy.26
  219.5 0.1 copy.27
  219.6 0.3 copy-done.5
  219.9 0.9 fusion.4
  (5 shorter events, 0.0 us)
Async XLA Ops:
  6.5 72.8 %copy-start = (bf16[256,512]{1,0:T(8,128)(2,1)S(1)}, bf16[256,512]{1,0:T(8,128)(2,1)}, u32[]{:S(2)}) copy-start(bf16[256,512]{1,0:T(8,128)(2,1)} %param.12) | copy-start | bytes 786436
  6.5 72.0 %all-gather.6.cloned.1.call-start = ((), (), s32[]{:S(2)}) async-start(), calls=%async_computation.4 | async-start | bytes 2359296 | tf_op jit(solution)/shard_map/all_gather | solution.py:143
  7.3 179.5 %all-gather.8.cloned.1.call-start = ((), (), s32[]{:S(2)}) async-start(), calls=%async_computation.5 | async-start | bytes 5406720 | tf_op jit(solution)/shard_map/all_gather | solution.py:145
  78.5 15.7 %copy-start.2 = (bf16[2048,512]{1,0:T(8,128)(2,1)S(1)}, bf16[2048,512]{1,0:T(8,128)(2,1)}, u32[]{:S(2)}) copy-start(bf16[2048,512]{1,0:T(8,128)(2,1)} %all-gather.6.cloned.1.call-done) | copy-start | bytes 6291460
  97.4 7.0 %copy-start.3 = (bf16[256,512]{1,0:T(8,128)(2,1)S(1)}, bf16[256,512]{1,0:T(8,128)(2,1)}, u32[]{:S(2)}) copy-start(bf16[256,512]{1,0:T(8,128)(2,1)} %param.14) | copy-start | bytes 786436
  97.4 31.7 %all-to-all-start = ((bf16[16,512,128]{2,1,0:T(8,128)(2,1)}), bf16[16,512,128]{2,1,0:T(8,128)(2,1)S(1)}, u32[]{:S(2)}, u32[]{:S(2)}) async-start(bf16[16,512,128]{2,1,0:T(8,128)(2,1)} %shard_map.100), calls=%async_computation | async-start | bytes 4194304 | tf_op jit(solution)/shard_map/all_to_all | solution.py:163
  103.7 26.4 %copy-start.7 = (s32[1,128]{1,0:T(1,128)S(1)}, s32[1,128]{1,0:T(1,128)}, u32[]{:S(2)}) copy-start(s32[1,128]{1,0:T(1,128)} %param.19) | copy-start | bytes 1540
  103.7 26.5 %copy-start.4 = (bf16[256,512]{1,0:T(8,128)(2,1)S(1)}, bf16[256,512]{1,0:T(8,128)(2,1)}, u32[]{:S(2)}) copy-start(bf16[256,512]{1,0:T(8,128)(2,1)} %param.15) | copy-start | bytes 786436
  105.4 26.1 %copy-start.6 = (f32[512]{0:T(512)S(1)}, f32[512]{0:T(512)}, u32[]{:S(2)}) copy-start(f32[512]{0:T(512)} %param.16) | copy-start | bytes 6148
  129.4 2.1 collective-permute-start
  132.4 25.7 %all-to-all-start.1 = ((f32[16,2,128]{2,1,0:T(2,128)}), f32[16,2,128]{2,1,0:T(2,128)S(1)}, u32[]{:S(2)}, u32[]{:S(2)}) async-start(f32[16,2,128]{2,1,0:T(2,128)} %broadcast_in_dim.26), calls=%async_computation.1 | async-start | bytes 32768 | tf_op jit(solution)/shard_map/all_to_all | solution.py:169
  186.8 2.5 %copy-start.1 = (bf16[5120,512]{1,0:T(8,128)(2,1)S(1)}, bf16[5120,512]{1,0:T(8,128)(2,1)}, u32[]{:S(2)}) copy-start(bf16[5120,512]{1,0:T(8,128)(2,1)} %all-gather.8.cloned.1.call-done) | copy-start | bytes 15728644
  218.9 0.9 copy-start.5
Sparse Core Ops, SparseCore 0:
  9.5 68.9 all-gather.5
  80.7 74.5 all-gather.7

commit v3 on v2

v3 whole, which is shorter than its diff:
```python
import jax
import jax.numpy as jnp
from jax import lax
from jax.experimental import pallas as pl
from jax.experimental.pallas import tpu as pltpu
from jax.sharding import Mesh
from jax.sharding import PartitionSpec as P

D = 8192
NORM_EPS = 1e-06
MIB = 1024 * 1024
LANES = 128
SLOT_PITCH = 8
DP = ("zh", "zl", "core")
TP = ("x", "y")


def gelu_slope(pre):
    value = pre.astype(jnp.float32)
    cdf_part = 0.5 * (1.0 + lax.erf(value * 0.7071067811865476))
    pdf_part = jnp.exp(-0.5 * value * value) * 0.3989422804014327
    return cdf_part + value * pdf_part


def query_kernel(core_ref, rows_ref, own_ref, other_ref, out_ref, turned):
    parts, count, depth = rows_ref.shape
    height = own_ref.shape[1]
    core = core_ref[0]

    @pl.when(pl.program_id(0) == 0)
    def _():
        turned[...] = rows_ref[...].reshape(parts * count, depth).T

    for weight_ref, place in ((own_ref, core), (other_ref, 1 - core)):
        product = jnp.dot(weight_ref[0], turned[...], preferred_element_type=jnp.float32)
        product = product.astype(out_ref.dtype)
        spot = pl.ds(pl.multiple_of(place * height, height), height)
        for part in range(parts):
            out_ref[part, 0, spot] = product[:, part * count : (part + 1) * count]


def query_products(core, rows, own, other):
    parts, count, depth = rows.shape
    steps, height, _ = own.shape
    weight_spec = pl.BlockSpec((1, height, depth), lambda i, _: (i, 0, 0))
    return pl.pallas_call(
        query_kernel,
        grid_spec=pltpu.PrefetchScalarGridSpec(
            num_scalar_prefetch=1,
            grid=(steps,),
            in_specs=[
                pl.BlockSpec((parts, count, depth), lambda i, _: (0, 0, 0)),
                weight_spec,
                weight_spec,
            ],
            out_specs=pl.BlockSpec((parts, 1, 2 * height, count), lambda i, _: (0, i, 0, 0)),
            scratch_shapes=[pltpu.VMEM((depth, parts * count), jnp.bfloat16)],
        ),
        out_shape=jax.ShapeDtypeStruct((parts, steps, 2 * height, count), jnp.bfloat16),
        compiler_params=pltpu.CompilerParams(vmem_limit_bytes=24 * MIB),
    )(core, rows, own, other)


def merge_kernel(grad_ref, input_ref, resid_ref, gain_ref, stat_ref, weight_ref, out_ref, handoff):
    count = grad_ref.shape[1]

    @pl.when(pl.program_id(0) == 0)
    def _():
        stats = jnp.sum(stat_ref[...], axis=0)
        inverse = lax.rsqrt(stats[0:1] / D + NORM_EPS)
        factor = inverse * inverse * inverse * stats[1:2] / D
        scaled = gain_ref[...] * grad_ref[...].astype(jnp.float32)
        handoff[...] = (
            resid_ref[...].astype(jnp.float32)
            + inverse * scaled
            - input_ref[...].astype(jnp.float32) * factor
        ).astype(jnp.bfloat16)

    for part in range(out_ref.shape[0]):
        for half in range(2):
            product = jnp.dot(
                weight_ref[2 * part + half], handoff[...], preferred_element_type=jnp.float32
            )
            out_ref[part, :, half * count : (half + 1) * count] = product.astype(out_ref.dtype)


def merge_products(grad, inputs, residual, gain, stats, weights, shares, steps):
    blocks, height, width = weights.shape
    count = grad.shape[1]
    whole = [grad, inputs, residual, gain, stats]
    return pl.pallas_call(
        merge_kernel,
        grid=(steps,),
        in_specs=[
            pl.BlockSpec(a.shape, lambda i, rank=a.ndim: (0,) * rank) for a in whole
        ]
        + [pl.BlockSpec((blocks // steps, height, width), lambda i: (i, 0, 0))],
        out_specs=pl.BlockSpec((shares // steps, height, 2 * count), lambda i: (i, 0, 0)),
        out_shape=jax.ShapeDtypeStruct((shares, height, 2 * count), jnp.bfloat16),
        scratch_shapes=[pltpu.VMEM((width, count), jnp.bfloat16)],
        compiler_params=pltpu.CompilerParams(vmem_limit_bytes=56 * MIB),
    )(*whole, weights)


def send_kernel(hidden_ref, target_ref, out_ref):
    count = target_ref.shape[1]
    total = jnp.sum(hidden_ref[...].astype(jnp.float32), axis=0).astype(jnp.bfloat16)
    spare = out_ref.shape[1] - 2 * total.shape[0]
    columns = jnp.concatenate(
        [total[:, :count], total[:, count:], jnp.zeros((spare, count), jnp.bfloat16)], axis=0
    )
    row = lax.broadcasted_iota(jnp.int32, (out_ref.shape[0], count), 0)
    hot = (row == target_ref[...]).astype(jnp.bfloat16)
    out_ref[...] = lax.dot_general(
        hot, columns, (((1,), (1,)), ((), ())), preferred_element_type=jnp.float32
    ).astype(out_ref.dtype)


def finish_kernel(box_ref, spot_ref, slope_ref, out_ref):
    rows, columns = out_ref.shape
    spot = lax.broadcasted_iota(jnp.int32, (rows, box_ref.shape[0]), 1)
    hot = (spot == spot_ref[...]).astype(jnp.bfloat16)
    hidden = jnp.dot(hot, box_ref[...], preferred_element_type=jnp.float32)
    out_ref[...] = hidden[:, :columns] * slope_ref[...]


def local(
    grad_query,
    query_weight,
    grad_resid,
    embeds,
    norm_gain,
    img_pos,
    img_count,
    img_dest,
    merge_weight,
    merge_pre,
):
    groups = lax.axis_size(DP)
    shares = lax.axis_size(TP)
    side = lax.axis_size("zh")
    rows, columns = merge_pre.shape
    capacity = rows // groups
    positions = img_pos[0]
    image_count = positions.shape[0]

    own = lax.all_gather(query_weight, "zl", axis=0)
    picked = lax.all_gather(jnp.take(grad_query, positions, axis=0), "zh", axis=0)
    merge_weight, picked = lax.optimization_barrier((merge_weight, picked))
    merge_full = lax.all_gather(merge_weight, DP, axis=0)
    inputs = jnp.take(embeds, positions, axis=0).T
    residual = jnp.take(grad_resid, positions, axis=0).T
    gain = norm_gain[:, None]
    wide = inputs.astype(jnp.float32)
    squares = jnp.sum(wide * wide, axis=0)
    is_live = jnp.arange(image_count, dtype=jnp.int32) < img_count[0]
    target_dev = img_dest[0]
    dest_hot = (
        (target_dev[:, None] == jnp.arange(groups, dtype=jnp.int32)[None, :]) & is_live[:, None]
    ).astype(jnp.int32)
    earlier = jnp.cumsum(dest_hot, axis=0) - dest_hot
    slot_index = jnp.sum(earlier * dest_hot, axis=1)
    target = jnp.where(is_live, target_dev * SLOT_PITCH + slot_index, -1)
    number = jnp.arange(rows, dtype=jnp.int32)
    spot = number // capacity * SLOT_PITCH + number % capacity
    slope = gelu_slope(merge_pre)

    other = lax.ppermute(own, "core", [(0, 1), (1, 0)])
    core = lax.axis_index("core").astype(jnp.int32)[None]
    partial_value = query_products(core, picked, own, other)
    partial_value = partial_value.reshape((shares,) + partial_value.shape[2:])
    swapped = lax.all_to_all(partial_value, TP, 0, 0, tiled=True)
    normal_grad = jnp.sum(swapped.astype(jnp.float32), axis=0).astype(jnp.bfloat16)
    exchange = [(b * side + a, a * side + b) for a in range(side) for b in range(side)]
    normal_grad = lax.ppermute(normal_grad, ("zh", "x"), exchange)
    inner = jnp.sum(gain * normal_grad.astype(jnp.float32) * wide, axis=0)
    stats = jnp.stack([squares, inner])
    stats = lax.all_to_all(
        jnp.broadcast_to(stats[None], (shares,) + stats.shape), TP, 0, 0, tiled=True
    )
    partial_hidden = merge_products(
        normal_grad, inputs, residual, gain, stats, merge_full, shares, 4
    )
    hidden = lax.all_to_all(partial_hidden, TP, 0, 0, tiled=True)
    lanes = -(-columns // LANES) * LANES
    outbox = pl.pallas_call(
        send_kernel,
        out_shape=jax.ShapeDtypeStruct((groups * SLOT_PITCH, lanes), jnp.bfloat16),
        compiler_params=pltpu.CompilerParams(vmem_limit_bytes=24 * MIB),
    )(hidden, target[None])
    received = lax.all_to_all(outbox.reshape(groups, SLOT_PITCH, lanes), DP, 0, 0, tiled=True)
    return pl.pallas_call(
        finish_kernel,
        out_shape=jax.ShapeDtypeStruct((rows, columns), jnp.float32),
        compiler_params=pltpu.CompilerParams(vmem_limit_bytes=24 * MIB),
    )(received.reshape(groups * SLOT_PITCH, lanes), spot[:, None], slope)


def solution(mesh):
    split = Mesh(mesh.devices.reshape(4, 4, 2, 4, 4), DP + TP)
    in_specs = (
        P(DP, TP),
        P(DP, TP),
        P(DP, TP),
        P(DP, TP),
        P(TP),
        P(DP, None),
        P(DP),
        P(DP, None),
        P(DP, TP),
        P(DP, TP),
    )
    out_specs = P(DP, TP)
    return jax.shard_map(local, mesh=split, in_specs=in_specs, out_specs=out_specs, check_vma=False)
```

time: 229 us -> 216 us (0.943)
  waiting for transfers between devices: 102 us -> 68.4 us
  starting transfers between devices: 26.3 us -> 47.5 us
  Pallas kernels: 6.57 us -> 9.61 us
    all_gather x1, waiting for transfers between devices: 71.2 us -> 16.7 us  [local(): own = lax.all_gather(query_weight, 'zl', axis=0)]
    all_to_all x2 -> x1, blocking collectives: 54.9 us -> 33.8 us  [local(): swapped = lax.all_to_all(partial_value, TP, 0, 0, tiled=True)]
    all_gather x1, blocking collectives: 13.3 us -> 32.9 us  [local(): lax.all_gather(jnp.take(grad_query, positions, axis=0), 'zh', axis=0)]
    all_to_all x1 -> x2, waiting for transfers between devices: 23.7 us -> 36.3 us  [the longest x1 18.4 us: local(): lax.all_to_all(outbox.reshape(groups, SLOT_PITCH, lanes), DP, 0, 0, tiled...]
    all_to_all x1 -> x2, starting transfers between devices: 6.29 us -> 16.1 us  [the longest x1 9.56 us: local(): lax.all_to_all(outbox.reshape(groups, SLOT_PITCH, lanes), DP, 0, 0, tiled...]
    all_to_all x1, starting transfers between devices: 19.3 us -> 28.2 us  [local(): lax.all_to_all(jnp.broadcast_to(stats[None], (shares,) + stats.shape), TP...]
    all_gather x1, waiting for transfers between devices: 0.01 us -> 7.23 us  [local(): merge_full = lax.all_gather(merge_weight, DP, axis=0)]
    pallas_call x3 -> x4, Pallas kernels: 6.57 us -> 9.61 us  [the longest x1 5.47 us: merge_products(): pl.pallas_call(merge_kernel, grid=(steps,), in_specs=[pl.BlockSpec(a.shap...]
  transfers between devices with their start and end apart: 5 -> 7, of which waited for: 3 -> 6; matrix products, arithmetic and copies ran while one was open for 3% -> 4% of each run, Pallas kernels for 2% -> 1%
where the time goes in v3:
time: 216 us
  waiting for transfers between devices  68.4 us (32%)
  blocking collectives  66.6 us (31%)
  starting transfers between devices  47.5 us (22%)
  between operations  14.2 us (7%)
  Pallas kernels  9.61 us (4%)
  local copies, waits for them, and re-layouts  5.5 us (3%)
  other arithmetic  3.74 us (2%)
    all_to_all x1, blocking collectives, local(): swapped = lax.all_to_all(partial_value, TP, 0, 0, tiled=True)  33.8 us
    all_gather x1, blocking collectives, local(): lax.all_gather(jnp.take(grad_query, positions, axis=0), 'zh', axis=0)  32.9 us
    all_to_all x1, starting transfers between devices, local(): lax.all_to_all(jnp.broadcast_to(stats[None], (shares,) + stats.shape), TP...  28.2 us
    all_to_all x1, waiting for transfers between devices, local(): lax.all_to_all(outbox.reshape(groups, SLOT_PITCH, lanes), DP, 0, 0, tiled...  18.4 us
    all_to_all x1, waiting for transfers between devices, local(): hidden = lax.all_to_all(partial_hidden, TP, 0, 0, tiled=True)  17.9 us
    all_gather x1, waiting for transfers between devices, local(): own = lax.all_gather(query_weight, 'zl', axis=0)  16.7 us
    all_to_all x1, starting transfers between devices, local(): lax.all_to_all(outbox.reshape(groups, SLOT_PITCH, lanes), DP, 0, 0, tiled...  9.56 us
    all_gather x1, waiting for transfers between devices, local(): merge_full = lax.all_gather(merge_weight, DP, axis=0)  7.23 us
  transfers between devices with their start and end apart: 7, of which 6 were waited for; matrix products, arithmetic and copies ran while one was open for 4% of the time, Pallas kernels for 1%

profile of v3, /device:TPU:1, one launch (start us, length us, event | category | flops | bytes accessed | tf_op | source)
XLA Modules:
  0.0 215.6 jit_solution(3937884030836235449)
XLA Ops:
  6.5 0.0 copy-start
  6.5 0.0 all-gather.6.cloned.1.call-start
  6.5 0.7 all-gather.6.cloned.1.call-update
  7.3 0.0 all-gather.8.cloned.1.call-start
  7.3 0.7 compare_select_fusion
  8.0 0.0 copy-done
  8.0 0.8 gather_fusion
  8.8 0.7 compare_and_fusion
  9.5 0.1 broadcast_select_fusion
  9.6 32.9 %all-gather = bf16[512,512]{1,0:T(8,128)(2,1)S(1)} all-gather(bf16[128,512]{1,0:T(8,128)(2,1)S(1)} %broadcast_select_fusion), channel_id=2, replica_groups=mesh['zh'=4,'zl'=4,'core'=2,'x'=4,'y'=4] {'zh'}, dimensions={0}, use_global_device_ids=true | all-gather | bytes 655360 | tf_op jit(solution)/shard_map/all_gather | solution.py:148
  42.5 0.0 all-gather.8.cloned.1.call-update
  42.5 16.7 %all-gather.6.cloned.1.call-done = bf16[1024,512]{1,0:T(8,128)(2,1)} async-done(((bf16[256,512]{1,0:T(8,128)(2,1)}), bf16[1024,512]{1,0:T(8,128)(2,1)}) %all-gather.6.cloned.1.call-update) | async-done | bytes 1048592 | tf_op jit(solution)/shard_map/all_gather | solution.py:147
  59.2 2.5 %collective-permute-start = (bf16[4,256,512]{2,1,0:T(8,128)(2,1)}, bf16[4,256,512]{2,1,0:T(8,128)(2,1)S(1)}, u32[]{:S(2)}, u32[]{:S(2)}) collective-permute-start(bf16[4,256,512]{2,1,0:T(8,128)(2,1)} %bitcast.29), channel_id=1, source_target_pairs={{0,16},{16,0},{1,17},{17,1},{2,18},{18,2},{3,19},{19,3},{4,20},{20... | collective-permute-start | bytes 3145736 | tf_op jit(solution)/shard_map/ppermute | solution.py:168
  61.7 2.5 %collective-permute-done.other_ref = bf16[4,256,512]{2,1,0:T(8,128)(2,1)S(1)} collective-permute-done((bf16[4,256,512]{2,1,0:T(8,128)(2,1)}, bf16[4,256,512]{2,1,0:T(8,128)(2,1)S(1)}, u32[]{:S(2)}, u32[]{:S(2)}) %collective-permute-start) | collective-permute-done | bytes 1048608 | tf_op jit(solution)/shard_map/ppermute | solution.py:168
  64.2 0.0 copy-start.1
  64.2 1.2 copy-done.1
  65.4 2.1 shard_map.100
  67.5 33.8 %all_to_all.20 = bf16[16,512,128]{2,1,0:T(8,128)(2,1)S(1)} all-to-all(bf16[16,512,128]{2,1,0:T(8,128)(2,1)S(1)} %bitcast.27), channel_id=1, replica_groups=mesh['zh'=4,'zl'=4,'core'=2,'x'=4,'y'=4] {'x','y'}, dimensions={0} | all-to-all | bytes 4194304 | tf_op jit(solution)/shard_map/all_to_all | solution.py:172
  101.3 0.0 copy-start.2
  101.3 0.0 copy-start.3
  101.3 0.0 copy-start.7
  101.3 0.3 reduce_sum.41
  101.6 0.7 collective-permute-start.1
  102.3 0.0 copy-done.2
  102.3 0.8 gather_fusion.1
  103.1 0.1 copy.13
  103.2 0.0 copy-done.3
  103.3 0.8 gather_fusion.2
  104.1 0.1 copy.14
  104.2 0.0 collective-permute-done.1.grad_ref
  104.2 0.0 copy-done.7
  104.3 0.0 copy-start.4
  104.3 0.7 fusion.6
  105.0 0.6 broadcast_in_dim.31
  105.6 28.2 %all-to-all-start.1 = ((f32[16,2,128]{2,1,0:T(2,128)}), f32[16,2,128]{2,1,0:T(2,128)S(1)}, u32[]{:S(2)}, u32[]{:S(2)}) async-start(f32[16,2,128]{2,1,0:T(2,128)} %broadcast_in_dim.31), calls=%async_computation.1 | async-start | bytes 32768 | tf_op jit(solution)/shard_map/all_to_all | solution.py:178
  133.8 0.7 select_bitcast_fusion.resid_ref
  134.5 0.9 copy.15.gain_ref
  135.4 4.9 %all-to-all-done.1.stat_ref = f32[16,2,128]{2,1,0:T(2,128)S(1)} async-done(((f32[16,2,128]{2,1,0:T(2,128)}), f32[16,2,128]{2,1,0:T(2,128)S(1)}, u32[]{:S(2)}, u32[]{:S(2)}) %all-to-all-start.1) | async-done | bytes 16416 | tf_op jit(solution)/shard_map/all_to_all | solution.py:178
  140.3 0.0 copy-start.6
  140.3 7.2 %all-gather.8.cloned.1.call-done = bf16[5120,512]{1,0:T(8,128)(2,1)} async-done(((bf16[160,512]{1,0:T(8,128)(2,1)}), bf16[5120,512]{1,0:T(8,128)(2,1)}) %all-gather.8.cloned.1.call-update) | async-done | bytes 5242896 | tf_op jit(solution)/shard_map/all_gather | solution.py:150
  147.5 0.0 copy-done.4
  147.5 0.0 copy-done.6
  147.5 5.5 %shard_map.101 = bf16[16,160,256]{2,1,0:T(8,128)(2,1)} custom-call(bf16[512,128]{1,0:T(8,128)(2,1)} %copy-done.4, bf16[512,128]{1,0:T(8,128)(2,1)} %get-tuple-element.12.input_ref, bf16[512,128]{1,0:T(8,128)(2,1)} %select_bitcast_fusion.resid_ref, f32[512,1]{1,0:T(8,128)} %copy.15.gain_ref, f32[16,2,128]{2,1,0:T(2,128)} %copy-done.6, ...), custom_call_target="tpu_custom_call" | custom-call | tf_op jit(solution)/shard_map/pallas_call | solution.py:91
  153.0 0.0 copy-start.8
  153.0 0.0 copy-start.5
  153.0 6.5 %all-to-all-start.2 = ((bf16[16,160,256]{2,1,0:T(8,128)(2,1)}), bf16[16,160,256]{2,1,0:T(8,128)(2,1)S(1)}, u32[]{:S(2)}, u32[]{:S(2)}) async-start(bf16[16,160,256]{2,1,0:T(8,128)(2,1)} %shard_map.101), calls=%async_computation.2 | async-start | bytes 2621440 | tf_op jit(solution)/shard_map/all_to_all | solution.py:184
  160.2 0.0 copy-done.8
  160.2 0.1 fusion.18
  160.3 0.2 reduce_window_sum.11
  160.5 0.2 select_reduce_fusion
  160.7 17.9 %all-to-all-done.2.hidden_ref = bf16[16,160,256]{2,1,0:T(8,128)(2,1)S(1)} async-done(((bf16[16,160,256]{2,1,0:T(8,128)(2,1)}), bf16[16,160,256]{2,1,0:T(8,128)(2,1)S(1)}, u32[]{:S(2)}, u32[]{:S(2)}) %all-to-all-start.2) | async-done | bytes 1310752 | tf_op jit(solution)/shard_map/all_to_all | solution.py:184
  178.6 1.0 shard_map.102
  179.6 9.6 %all-to-all-start.3 = ((bf16[32,8,384]{2,1,0:T(8,128)(2,1)}), bf16[32,8,384]{2,1,0:T(8,128)(2,1)S(1)}, u32[]{:S(2)}, u32[]{:S(2)}) async-start(bf16[32,8,384]{2,1,0:T(8,128)(2,1)} %bitcast.14), calls=%async_computation.3 | async-start | bytes 393216 | tf_op jit(solution)/shard_map/all_to_all | solution.py:191
  189.2 0.0 copy-done.5
  189.2 0.1 fusion.3.slope_ref
  189.4 18.4 %all-to-all-done.3 = bf16[32,8,384]{2,1,0:T(8,128)(2,1)S(1)} async-done(((bf16[32,8,384]{2,1,0:T(8,128)(2,1)}), bf16[32,8,384]{2,1,0:T(8,128)(2,1)S(1)}, u32[]{:S(2)}, u32[]{:S(2)}) %all-to-all-start.3) | async-done | bytes 196640 | tf_op jit(solution)/shard_map/all_to_all | solution.py:191
  207.8 1.0 shard_map.103
  (5 shorter events, 0.1 us)
Async XLA Ops:
  6.5 1.4 copy-start
  6.5 52.7 %all-gather.6.cloned.1.call-start = ((), (), s32[]{:S(2)}) async-start(), calls=%async_computation.4 | async-start | bytes 1310720 | tf_op jit(solution)/shard_map/all_gather | solution.py:147
  7.3 140.3 %all-gather.8.cloned.1.call-start = ((), (), s32[]{:S(2)}) async-start(), calls=%async_computation.5 | async-start | bytes 5406720 | tf_op jit(solution)/shard_map/all_gather | solution.py:150
  59.2 4.9 %collective-permute-start = (bf16[4,256,512]{2,1,0:T(8,128)(2,1)}, bf16[4,256,512]{2,1,0:T(8,128)(2,1)S(1)}, u32[]{:S(2)}, u32[]{:S(2)}) collective-permute-start(bf16[4,256,512]{2,1,0:T(8,128)(2,1)} %bitcast.29), channel_id=1, source_target_pairs={{0,16},{16,0},{1,17},{17,1},{2,18},{18,2},{3,19},{19,3},{4,20},{20... | collective-permute-start | bytes 3145736 | tf_op jit(solution)/shard_map/ppermute | solution.py:168
  64.2 1.2 copy-start.1
  101.3 1.0 copy-start.2
  101.3 2.0 copy-start.3
  101.3 3.0 %copy-start.7 = (f32[512]{0:T(512)S(1)}, f32[512]{0:T(512)}, u32[]{:S(2)}) copy-start(f32[512]{0:T(512)} %param.16) | copy-start | bytes 6148
  101.6 2.6 %collective-permute-start.1 = (bf16[512,128]{1,0:T(8,128)(2,1)S(1)}, bf16[512,128]{1,0:T(8,128)(2,1)S(1)}, u32[]{:S(2)}, u32[]{:S(2)}) collective-permute-start(bf16[512,128]{1,0:T(8,128)(2,1)S(1)} %reduce_sum.41), channel_id=1, source_target_pairs={{0,0},{128,4},{256,8},{384,12},{4,128},{132,132},{260,136},{388,14... | collective-permute-start | bytes 393224 | tf_op jit(solution)/shard_map/ppermute | solution.py:175
  104.3 43.3 %copy-start.4 = (bf16[512,128]{1,0:T(8,128)(2,1)}, bf16[512,128]{1,0:T(8,128)(2,1)S(1)}, u32[]{:S(2)}) copy-start(bf16[512,128]{1,0:T(8,128)(2,1)S(1)} %collective-permute-done.1.grad_ref) | copy-start | bytes 393220
  105.6 34.7 %all-to-all-start.1 = ((f32[16,2,128]{2,1,0:T(2,128)}), f32[16,2,128]{2,1,0:T(2,128)S(1)}, u32[]{:S(2)}, u32[]{:S(2)}) async-start(f32[16,2,128]{2,1,0:T(2,128)} %broadcast_in_dim.31), calls=%async_computation.1 | async-start | bytes 32768 | tf_op jit(solution)/shard_map/all_to_all | solution.py:178
  140.3 7.2 %copy-start.6 = (f32[16,2,128]{2,1,0:T(2,128)}, f32[16,2,128]{2,1,0:T(2,128)S(1)}, u32[]{:S(2)}) copy-start(f32[16,2,128]{2,1,0:T(2,128)S(1)} %all-to-all-done.1.stat_ref) | copy-start | bytes 49156
  153.0 7.2 %copy-start.8 = (s32[1,128]{1,0:T(1,128)S(1)}, s32[1,128]{1,0:T(1,128)}, u32[]{:S(2)}) copy-start(s32[1,128]{1,0:T(1,128)} %param.19) | copy-start | bytes 1540
  153.0 36.2 %copy-start.5 = (bf16[192,320]{1,0:T(8,128)(2,1)S(1)}, bf16[192,320]{1,0:T(8,128)(2,1)}, u32[]{:S(2)}) copy-start(bf16[192,320]{1,0:T(8,128)(2,1)} %param.21) | copy-start | bytes 368644
  153.0 25.6 %all-to-all-start.2 = ((bf16[16,160,256]{2,1,0:T(8,128)(2,1)}), bf16[16,160,256]{2,1,0:T(8,128)(2,1)S(1)}, u32[]{:S(2)}, u32[]{:S(2)}) async-start(bf16[16,160,256]{2,1,0:T(8,128)(2,1)} %shard_map.101), calls=%async_computation.2 | async-start | bytes 2621440 | tf_op jit(solution)/shard_map/all_to_all | solution.py:184
  179.6 28.2 %all-to-all-start.3 = ((bf16[32,8,384]{2,1,0:T(8,128)(2,1)}), bf16[32,8,384]{2,1,0:T(8,128)(2,1)S(1)}, u32[]{:S(2)}, u32[]{:S(2)}) async-start(bf16[32,8,384]{2,1,0:T(8,128)(2,1)} %bitcast.14), calls=%async_computation.3 | async-start | bytes 393216 | tf_op jit(solution)/shard_map/all_to_all | solution.py:191
Sparse Core Ops, SparseCore 0:
  9.5 49.7 all-gather.5
  61.3 86.1 all-gather.7

commit v4 on v3

--- a/solution.py
+++ b/solution.py
@@ -22,10 +22,10 @@
     return cdf_part + value * pdf_part
 
 
-def query_kernel(core_ref, rows_ref, own_ref, other_ref, out_ref, turned):
+def query_kernel(place_ref, rows_ref, own_ref, other_ref, out_ref, turned):
     parts, count, depth = rows_ref.shape
     height = own_ref.shape[1]
-    core = core_ref[0]
+    core, shift = place_ref[0], place_ref[1]
 
     @pl.when(pl.program_id(0) == 0)
     def _():
@@ -36,10 +36,10 @@
         product = product.astype(out_ref.dtype)
         spot = pl.ds(pl.multiple_of(place * height, height), height)
         for part in range(parts):
-            out_ref[part, 0, spot] = product[:, part * count : (part + 1) * count]
-
-
-def query_products(core, rows, own, other):
+            out_ref[lax.rem(part + shift, parts), 0, spot] = product[:, part * count : (part + 1) * count]
+
+
+def query_products(place, rows, own, other):
     parts, count, depth = rows.shape
     steps, height, _ = own.shape
     weight_spec = pl.BlockSpec((1, height, depth), lambda i, _: (i, 0, 0))
@@ -57,8 +57,8 @@
             scratch_shapes=[pltpu.VMEM((depth, parts * count), jnp.bfloat16)],
         ),
         out_shape=jax.ShapeDtypeStruct((parts, steps, 2 * height, count), jnp.bfloat16),
-        compiler_params=pltpu.CompilerParams(vmem_limit_bytes=24 * MIB),
-    )(core, rows, own, other)
+        compiler_params=pltpu.CompilerParams(vmem_limit_bytes=56 * MIB),
+    )(place, rows, own, other)
 
 
 def merge_kernel(grad_ref, input_ref, resid_ref, gain_ref, stat_ref, weight_ref, out_ref, handoff):
@@ -145,11 +145,11 @@
     image_count = positions.shape[0]
 
     own = lax.all_gather(query_weight, "zl", axis=0)
-    picked = lax.all_gather(jnp.take(grad_query, positions, axis=0), "zh", axis=0)
+    picked = lax.all_gather(jnp.take(grad_query, positions, axis=0, mode="clip"), "zh", axis=0)
     merge_weight, picked = lax.optimization_barrier((merge_weight, picked))
     merge_full = lax.all_gather(merge_weight, DP, axis=0)
-    inputs = jnp.take(embeds, positions, axis=0).T
-    residual = jnp.take(grad_resid, positions, axis=0).T
+    inputs = jnp.take(embeds, positions, axis=0, mode="clip").T
+    residual = jnp.take(grad_resid, positions, axis=0, mode="clip").T
     gain = norm_gain[:, None]
     wide = inputs.astype(jnp.float32)
     squares = jnp.sum(wide * wide, axis=0)
@@ -166,12 +166,14 @@
     slope = gelu_slope(merge_pre)
 
     other = lax.ppermute(own, "core", [(0, 1), (1, 0)])
-    core = lax.axis_index("core").astype(jnp.int32)[None]
-    partial_value = query_products(core, picked, own, other)
+    place = jnp.stack([lax.axis_index("core"), lax.axis_index("zh")]).astype(jnp.int32)
+    partial_value = query_products(place, picked, own, other)
     partial_value = partial_value.reshape((shares,) + partial_value.shape[2:])
     swapped = lax.all_to_all(partial_value, TP, 0, 0, tiled=True)
     normal_grad = jnp.sum(swapped.astype(jnp.float32), axis=0).astype(jnp.bfloat16)
-    exchange = [(b * side + a, a * side + b) for a in range(side) for b in range(side)]
+    exchange = [
+        (h * side + (a + h) % side, a * side + h) for a in range(side) for h in range(side)
+    ]
     normal_grad = lax.ppermute(normal_grad, ("zh", "x"), exchange)
     inner = jnp.sum(gain * normal_grad.astype(jnp.float32) * wide, axis=0)
     stats = jnp.stack([squares, inner])
@@ -179,7 +181,7 @@
         jnp.broadcast_to(stats[None], (shares,) + stats.shape), TP, 0, 0, tiled=True
     )
     partial_hidden = merge_products(
-        normal_grad, inputs, residual, gain, stats, merge_full, shares, 4
+        normal_grad, inputs, residual, gain, stats, merge_full, shares, 8
     )
     hidden = lax.all_to_all(partial_hidden, TP, 0, 0, tiled=True)
     lanes = -(-columns // LANES) * LANES

time: 216 us -> 213 us (0.986)
  waiting for transfers between devices: 68.4 us -> 61 us
  Pallas kernels: 9.61 us -> 15.3 us
    all_gather x1, waiting for transfers between devices: 7.23 us -> 0.29 us  [local(): merge_full = lax.all_gather(merge_weight, DP, axis=0)]
    all_to_all x1, starting transfers between devices: 28.2 us -> 22.2 us  [local(): lax.all_to_all(jnp.broadcast_to(stats[None], (shares,) + stats.shape), TP...]
    all_to_all x1, starting transfers between devices: 6.54 us -> 11.9 us  [local(): hidden = lax.all_to_all(partial_hidden, TP, 0, 0, tiled=True)]
    pallas_call x1, Pallas kernels: 2.14 us -> 5.7 us  [query_products(): pl.pallas_call(query_kernel, grid_spec=pltpu.PrefetchScalarGridSpec(num_s...]
  transfers between devices with their start and end apart: 7 -> 7, of which waited for: 6 -> 6; matrix products, arithmetic and copies ran while one was open for 4% -> 3% of each run, Pallas kernels for 1% -> 3%
where the time goes in v4:
time: 213 us; the launch traced here: 212 us
  blocking collectives  66.2 us (31%)
  waiting for transfers between devices  61 us (29%)
  starting transfers between devices  46.9 us (22%)
  Pallas kernels  15.3 us (7%)
  between operations  14.2 us (7%)
  local copies, waits for them, and re-layouts  6.27 us (3%)
  other arithmetic  2.36 us (1%)
    all_to_all x1, blocking collectives, local(): swapped = lax.all_to_all(partial_value, TP, 0, 0, tiled=True)  34 us
    all_gather x1, blocking collectives, local(): lax.all_gather(jnp.take(grad_query, positions, axis=0, mode='clip'), 'zh'...  32.3 us
    all_to_all x1, starting transfers between devices, local(): lax.all_to_all(jnp.broadcast_to(stats[None], (shares,) + stats.shape), TP...  22.2 us
    all_to_all x1, waiting for transfers between devices, local(): lax.all_to_all(outbox.reshape(groups, SLOT_PITCH, lanes), DP, 0, 0, tiled...  18.4 us
    all_to_all x1, waiting for transfers between devices, local(): hidden = lax.all_to_all(partial_hidden, TP, 0, 0, tiled=True)  18 us
    all_gather x1, waiting for transfers between devices, local(): own = lax.all_gather(query_weight, 'zl', axis=0)  17.8 us
    all_to_all x1, starting transfers between devices, local(): hidden = lax.all_to_all(partial_hidden, TP, 0, 0, tiled=True)  11.9 us
    all_to_all x1, starting transfers between devices, local(): lax.all_to_all(outbox.reshape(groups, SLOT_PITCH, lanes), DP, 0, 0, tiled...  9.72 us
  transfers between devices with their start and end apart: 7, of which 6 were waited for; matrix products, arithmetic and copies ran while one was open for 3% of the time, Pallas kernels for 3%

profile of v4, /device:TPU:1, one launch (start us, length us, event | category | flops | bytes accessed | tf_op | source)
XLA Modules:
  0.0 212.2 jit_solution(2105080535129397836)
XLA Ops:
  6.5 0.0 copy-start
  6.5 0.0 all-gather.6.cloned.1.call-start
  6.5 0.7 all-gather.6.cloned.1.call-update
  7.3 0.0 all-gather.8.cloned.1.call-start
  7.3 0.7 pad_clamp_fusion
  8.0 0.0 copy-done
  8.0 0.8 gather_fusion
  8.8 32.3 %all-gather = bf16[512,512]{1,0:T(8,128)(2,1)} all-gather(bf16[128,512]{1,0:T(8,128)(2,1)S(1)} %gather_fusion), channel_id=2, replica_groups=mesh['zh'=4,'zl'=4,'core'=2,'x'=4,'y'=4] {'zh'}, dimensions={0}, use_global_device_ids=true | all-gather | bytes 655360 | tf_op jit(solution)/shard_map/all_gather | solution.py:148
  41.1 0.0 all-gather.8.cloned.1.call-update
  41.1 17.8 %all-gather.6.cloned.1.call-done = bf16[1024,512]{1,0:T(8,128)(2,1)} async-done(((bf16[256,512]{1,0:T(8,128)(2,1)}), bf16[1024,512]{1,0:T(8,128)(2,1)}) %all-gather.6.cloned.1.call-update) | async-done | bytes 1048592 | tf_op jit(solution)/shard_map/all_gather | solution.py:147
  58.9 2.4 %collective-permute-start = (bf16[4,256,512]{2,1,0:T(8,128)(2,1)}, bf16[4,256,512]{2,1,0:T(8,128)(2,1)S(1)}, u32[]{:S(2)}, u32[]{:S(2)}) collective-permute-start(bf16[4,256,512]{2,1,0:T(8,128)(2,1)} %bitcast.29), channel_id=1, source_target_pairs={{0,16},{16,0},{1,17},{17,1},{2,18},{18,2},{3,19},{19,3},{4,20},{20... | collective-permute-start | bytes 3145736 | tf_op jit(solution)/shard_map/ppermute | solution.py:168
  61.2 0.6 pad_add_fusion.place_ref
  61.9 1.9 collective-permute-done.other_ref
  63.7 0.0 copy-start.4
  63.7 1.1 copy-done.4
  64.8 5.7 %shard_map.100 = bf16[4,4,512,128]{3,2,1,0:T(8,128)(2,1)} custom-call(s32[2]{0:T(128)} %pad_add_fusion.place_ref, bf16[4,128,512]{2,1,0:T(8,128)(2,1)} %bitcast.27, bf16[4,256,512]{2,1,0:T(8,128)(2,1)} %bitcast.30, bf16[4,256,512]{2,1,0:T(8,128)(2,1)} %copy-done.4), custom_call_target="tpu_custom_call" | custom-call | tf_op jit(solution)/shard_map/pallas_call | solution.py:46
  70.5 34.0 %all_to_all.20 = bf16[16,512,128]{2,1,0:T(8,128)(2,1)S(1)} all-to-all(bf16[16,512,128]{2,1,0:T(8,128)(2,1)} %bitcast.25), channel_id=1, replica_groups=mesh['zh'=4,'zl'=4,'core'=2,'x'=4,'y'=4] {'x','y'}, dimensions={0} | all-to-all | bytes 4194304 | tf_op jit(solution)/shard_map/all_to_all | solution.py:172
  104.4 0.0 copy-start.1
  104.4 0.0 copy-start.8
  104.4 0.0 copy-start.2
  104.4 0.3 reduce_sum.41
  104.7 0.7 collective-permute-start.1
  105.4 0.0 copy-done.1
  105.4 0.8 gather_fusion.1
  106.3 0.1 copy.13
  106.4 0.0 copy-start.3
  106.4 0.0 collective-permute-done.1.grad_ref
  106.4 0.0 copy-done.8
  106.4 0.0 copy-start.5
  106.4 0.2 fusion.6
  106.6 0.6 broadcast_in_dim.25
  107.2 22.2 %all-to-all-start.1 = ((f32[16,2,128]{2,1,0:T(2,128)}), f32[16,2,128]{2,1,0:T(2,128)S(1)}, u32[]{:S(2)}, u32[]{:S(2)}) async-start(f32[16,2,128]{2,1,0:T(2,128)} %broadcast_in_dim.25), calls=%async_computation.1 | async-start | bytes 32768 | tf_op jit(solution)/shard_map/all_to_all | solution.py:180
  129.4 0.0 copy-done.2
  129.4 0.8 gather_fusion.2
  130.3 0.7 copy.14
  131.0 0.9 copy.15.gain_ref
  131.9 4.0 %all-to-all-done.1.stat_ref = f32[16,2,128]{2,1,0:T(2,128)S(1)} async-done(((f32[16,2,128]{2,1,0:T(2,128)}), f32[16,2,128]{2,1,0:T(2,128)S(1)}, u32[]{:S(2)}, u32[]{:S(2)}) %all-to-all-start.1) | async-done | bytes 16416 | tf_op jit(solution)/shard_map/all_to_all | solution.py:180
  135.9 0.0 copy-start.7
  135.9 0.3 all-gather.8.cloned.1.call-done
  136.2 0.0 copy-done.3
  136.2 0.0 copy-done.5
  136.2 0.3 copy-done.7
  136.5 7.6 %shard_map.101 = bf16[16,160,256]{2,1,0:T(8,128)(2,1)} custom-call(bf16[512,128]{1,0:T(8,128)(2,1)} %copy-done.5, bf16[512,128]{1,0:T(8,128)(2,1)} %bitcast.28, bf16[512,128]{1,0:T(8,128)(2,1)} %bitcast.31, f32[512,1]{1,0:T(8,128)} %copy.15.gain_ref, f32[16,2,128]{2,1,0:T(2,128)} %copy-done.7, bf16[32,160,512]{2,1,0:T(8,128)(2,1)} %bitcast.26), custom_call_target="tpu_custom_call" | custom-call | tf_op jit(solution)/shard_map/pallas_call | solution.py:91
  144.0 0.0 copy-start.9
  144.1 0.0 copy-start.6
  144.1 11.9 %all-to-all-start.2 = ((bf16[16,160,256]{2,1,0:T(8,128)(2,1)}), bf16[16,160,256]{2,1,0:T(8,128)(2,1)S(1)}, u32[]{:S(2)}, u32[]{:S(2)}) async-start(bf16[16,160,256]{2,1,0:T(8,128)(2,1)} %shard_map.101), calls=%async_computation.2 | async-start | bytes 2621440 | tf_op jit(solution)/shard_map/all_to_all | solution.py:186
  156.6 0.0 copy-done.9
  156.6 0.1 fusion.18
  156.7 0.2 reduce_window_sum.11
  156.9 0.2 select_reduce_fusion
  157.1 18.0 %all-to-all-done.2.hidden_ref = bf16[16,160,256]{2,1,0:T(8,128)(2,1)S(1)} async-done(((bf16[16,160,256]{2,1,0:T(8,128)(2,1)}), bf16[16,160,256]{2,1,0:T(8,128)(2,1)S(1)}, u32[]{:S(2)}, u32[]{:S(2)}) %all-to-all-start.2) | async-done | bytes 1310752 | tf_op jit(solution)/shard_map/all_to_all | solution.py:186
  175.0 1.0 shard_map.102
  176.1 9.7 %all-to-all-start.3 = ((bf16[32,8,384]{2,1,0:T(8,128)(2,1)}), bf16[32,8,384]{2,1,0:T(8,128)(2,1)S(1)}, u32[]{:S(2)}, u32[]{:S(2)}) async-start(bf16[32,8,384]{2,1,0:T(8,128)(2,1)} %bitcast.15), calls=%async_computation.3 | async-start | bytes 393216 | tf_op jit(solution)/shard_map/all_to_all | solution.py:193
  185.9 0.0 copy-done.6
  185.9 0.1 fusion.3.slope_ref
  186.0 18.4 %all-to-all-done.3 = bf16[32,8,384]{2,1,0:T(8,128)(2,1)S(1)} async-done(((bf16[32,8,384]{2,1,0:T(8,128)(2,1)}), bf16[32,8,384]{2,1,0:T(8,128)(2,1)S(1)}, u32[]{:S(2)}, u32[]{:S(2)}) %all-to-all-start.3) | async-done | bytes 196640 | tf_op jit(solution)/shard_map/all_to_all | solution.py:193
  204.4 1.0 shard_map.103
  (4 shorter events, 0.1 us)
Async XLA Ops:
  6.5 1.4 copy-start
  6.5 52.3 %all-gather.6.cloned.1.call-start = ((), (), s32[]{:S(2)}) async-start(), calls=%async_computation.4 | async-start | bytes 1310720 | tf_op jit(solution)/shard_map/all_gather | solution.py:147
  7.3 128.9 %all-gather.8.cloned.1.call-start = ((), (), s32[]{:S(2)}) async-start(), calls=%async_computation.5 | async-start | bytes 5406720 | tf_op jit(solution)/shard_map/all_gather | solution.py:150
  58.9 4.8 %collective-permute-start = (bf16[4,256,512]{2,1,0:T(8,128)(2,1)}, bf16[4,256,512]{2,1,0:T(8,128)(2,1)S(1)}, u32[]{:S(2)}, u32[]{:S(2)}) collective-permute-start(bf16[4,256,512]{2,1,0:T(8,128)(2,1)} %bitcast.29), channel_id=1, source_target_pairs={{0,16},{16,0},{1,17},{17,1},{2,18},{18,2},{3,19},{19,3},{4,20},{20... | collective-permute-start | bytes 3145736 | tf_op jit(solution)/shard_map/ppermute | solution.py:168
  63.7 1.1 copy-start.4
  104.4 1.0 copy-start.1
  104.4 2.0 copy-start.8
  104.4 25.0 %copy-start.2 = (bf16[256,512]{1,0:T(8,128)(2,1)S(1)}, bf16[256,512]{1,0:T(8,128)(2,1)}, u32[]{:S(2)}) copy-start(bf16[256,512]{1,0:T(8,128)(2,1)} %param.12) | copy-start | bytes 786436
  104.7 1.7 collective-permute-start.1
  106.4 29.8 %copy-start.3 = (bf16[128,512]{0,1:T(8,128)(2,1)}, bf16[128,512]{0,1:T(8,128)(2,1)S(1)}, u32[]{:S(2)}) copy-start(bf16[128,512]{0,1:T(8,128)(2,1)S(1)} %copy.13) | copy-start | bytes 393220
  106.4 29.7 %copy-start.5 = (bf16[512,128]{1,0:T(8,128)(2,1)}, bf16[512,128]{1,0:T(8,128)(2,1)S(1)}, u32[]{:S(2)}) copy-start(bf16[512,128]{1,0:T(8,128)(2,1)S(1)} %collective-permute-done.1.grad_ref) | copy-start | bytes 393220
  107.2 28.7 %all-to-all-start.1 = ((f32[16,2,128]{2,1,0:T(2,128)}), f32[16,2,128]{2,1,0:T(2,128)S(1)}, u32[]{:S(2)}, u32[]{:S(2)}) async-start(f32[16,2,128]{2,1,0:T(2,128)} %broadcast_in_dim.25), calls=%async_computation.1 | async-start | bytes 32768 | tf_op jit(solution)/shard_map/all_to_all | solution.py:180
  135.9 0.6 copy-start.7
  144.0 12.5 %copy-start.9 = (s32[1,128]{1,0:T(1,128)S(1)}, s32[1,128]{1,0:T(1,128)}, u32[]{:S(2)}) copy-start(s32[1,128]{1,0:T(1,128)} %param.17) | copy-start | bytes 1540
  144.1 41.8 %copy-start.6 = (bf16[192,320]{1,0:T(8,128)(2,1)S(1)}, bf16[192,320]{1,0:T(8,128)(2,1)}, u32[]{:S(2)}) copy-start(bf16[192,320]{1,0:T(8,128)(2,1)} %param.19) | copy-start | bytes 368644
  144.1 31.0 %all-to-all-start.2 = ((bf16[16,160,256]{2,1,0:T(8,128)(2,1)}), bf16[16,160,256]{2,1,0:T(8,128)(2,1)S(1)}, u32[]{:S(2)}, u32[]{:S(2)}) async-start(bf16[16,160,256]{2,1,0:T(8,128)(2,1)} %shard_map.101), calls=%async_computation.2 | async-start | bytes 2621440 | tf_op jit(solution)/shard_map/all_to_all | solution.py:186
  176.1 28.4 %all-to-all-start.3 = ((bf16[32,8,384]{2,1,0:T(8,128)(2,1)}), bf16[32,8,384]{2,1,0:T(8,128)(2,1)S(1)}, u32[]{:S(2)}, u32[]{:S(2)}) async-start(bf16[32,8,384]{2,1,0:T(8,128)(2,1)} %bitcast.15), calls=%async_computation.3 | async-start | bytes 393216 | tf_op jit(solution)/shard_map/all_to_all | solution.py:193
Sparse Core Ops, SparseCore 0:
  9.5 49.3 all-gather.5
  61.0 75.1 all-gather.7

commit v5 on v4

v5 whole, which is shorter than its diff:
```python
import jax
import jax.numpy as jnp
from jax import lax
from jax.experimental import pallas as pl
from jax.experimental.pallas import tpu as pltpu
from jax.sharding import Mesh
from jax.sharding import PartitionSpec as P

D = 8192
NORM_EPS = 1e-06
MIB = 1024 * 1024
LANES = 128
SLOT_PITCH = 8
COPIES = 8
DP = ("zh", "zl", "core")
TP = ("x", "y")


def gelu_slope(pre):
    value = pre.astype(jnp.float32)
    cdf_part = 0.5 * (1.0 + lax.erf(value * 0.7071067811865476))
    pdf_part = jnp.exp(-0.5 * value * value) * 0.3989422804014327
    return cdf_part + value * pdf_part


def query_kernel(place_ref, rows_ref, weight_ref, *refs):
    out_ref, turned = refs[-2:]
    parts, count, depth = rows_ref.shape
    shift = place_ref[1]

    @pl.when(pl.program_id(0) == 0)
    def _():
        turned[...] = rows_ref[...].reshape(parts * count, depth).T

    product = jnp.dot(weight_ref[0], turned[...], preferred_element_type=jnp.float32)
    product = product.astype(out_ref.dtype)
    for part in range(parts):
        out_ref[lax.rem(part + shift, parts), 0, 0] = product[:, part * count : (part + 1) * count]


def query_products(place, rows, weight, flip, partly=None):
    parts, count, depth = rows.shape
    steps, height, _ = weight.shape
    out_spec = pl.BlockSpec(
        (parts, 1, 1, height, count), lambda i, place: (0, i, (place[0] + flip) % 2, 0, 0)
    )
    specs = [
        pl.BlockSpec((parts, count, depth), lambda i, _: (0, 0, 0)),
        pl.BlockSpec((1, height, depth), lambda i, _: (i, 0, 0)),
    ]
    args = [place, rows, weight]
    aliases = {}
    if partly is not None:
        specs.append(pl.BlockSpec(memory_space=pl.ANY))
        args.append(partly)
        aliases = {3: 0}
    return pl.pallas_call(
        query_kernel,
        grid_spec=pltpu.PrefetchScalarGridSpec(
            num_scalar_prefetch=1,
            grid=(steps,),
            in_specs=specs,
            out_specs=out_spec,
            scratch_shapes=[pltpu.VMEM((depth, parts * count), jnp.bfloat16)],
        ),
        out_shape=jax.ShapeDtypeStruct((parts, steps, 2, height, count), jnp.bfloat16),
        input_output_aliases=aliases,
        compiler_params=pltpu.CompilerParams(vmem_limit_bytes=16 * MIB),
    )(*args)


def reduce_kernel(place_ref, parts_ref, scaled_ref, square_ref, out_ref, stat_ref):
    total = parts_ref[0].astype(jnp.float32)
    for part in range(1, parts_ref.shape[0]):
        total += parts_ref[part].astype(jnp.float32)
    out_ref[...] = total.astype(out_ref.dtype)
    inner = jnp.sum(total * scaled_ref[...].astype(jnp.float32), axis=0, keepdims=True)
    side = stat_ref.shape[0] // 4
    for spot in range(stat_ref.shape[0]):
        plane = spot // side
        stat_ref[spot, 0:1] = jnp.where(place_ref[2] == plane, inner, 0.0)
        stat_ref[spot, 1:2] = jnp.where(place_ref[1] == plane, square_ref[...], 0.0)


def merge_kernel(
    grad_ref, input_ref, resid_ref, gain_ref, stat_ref, weight_ref, out_ref, handoff, held, sems
):
    count = grad_ref.shape[1]
    blocks, height, width = held.shape
    step = blocks // COPIES

    def copy(number):
        spot = pl.ds(number * step, step)
        return pltpu.make_async_copy(weight_ref.at[spot], held.at[spot], sems.at[number])

    for number in range(COPIES):
        copy(number).start()
    stats = jnp.sum(stat_ref[...], axis=0)
    inverse = lax.rsqrt(stats[1:2] / D + NORM_EPS)
    factor = inverse * inverse * inverse * stats[0:1] / D
    scaled = gain_ref[...] * grad_ref[...].astype(jnp.float32)
    handoff[...] = (
        resid_ref[...].astype(jnp.float32)
        + inverse * scaled
        - input_ref[...].astype(jnp.float32) * factor
    ).astype(jnp.bfloat16)
    for number in range(COPIES):
        copy(number).wait()
        weight = held[number * step : (number + 1) * step].reshape(step * height, width)
        product = jnp.dot(weight, handoff[...], preferred_element_type=jnp.float32)
        product = product.astype(out_ref.dtype)
        for block in range(step):
            share, half = divmod(number * step + block, 2)
            out_ref[share, :, half * count : (half + 1) * count] = product[
                block * height : (block + 1) * height
            ]


def merge_products(grad, inputs, residual, gain, stats, weights, shares):
    blocks, height, width = weights.shape
    count = grad.shape[1]
    local_spec = pl.BlockSpec(memory_space=pltpu.VMEM)
    return pl.pallas_call(
        merge_kernel,
        in_specs=[local_spec] * 5 + [pl.BlockSpec(memory_space=pltpu.HBM)],
        out_specs=local_spec,
        out_shape=jax.ShapeDtypeStruct((shares, height, 2 * count), jnp.bfloat16),
        scratch_shapes=[
            pltpu.VMEM((width, count), jnp.bfloat16),
            pltpu.VMEM((blocks, height, width), jnp.bfloat16),
            pltpu.SemaphoreType.DMA((COPIES,)),
        ],
        compiler_params=pltpu.CompilerParams(vmem_limit_bytes=24 * MIB),
    )(grad, inputs, residual, gain, stats, weights)


def send_kernel(hidden_ref, target_ref, out_ref):
    count = target_ref.shape[1]
    total = jnp.sum(hidden_ref[...].astype(jnp.float32), axis=0).astype(jnp.bfloat16)
    spare = out_ref.shape[1] - 2 * total.shape[0]
    columns = jnp.concatenate(
        [total[:, :count], total[:, count:], jnp.zeros((spare, count), jnp.bfloat16)], axis=0
    )
    row = lax.broadcasted_iota(jnp.int32, (out_ref.shape[0], count), 0)
    hot = (row == target_ref[...]).astype(jnp.bfloat16)
    out_ref[...] = lax.dot_general(
        hot, columns, (((1,), (1,)), ((), ())), preferred_element_type=jnp.float32
    ).astype(out_ref.dtype)


def finish_kernel(box_ref, spot_ref, slope_ref, out_ref):
    rows, columns = out_ref.shape
    spot = lax.broadcasted_iota(jnp.int32, (rows, box_ref.shape[0]), 1)
    hot = (spot == spot_ref[...]).astype(jnp.bfloat16)
    hidden = jnp.dot(hot, box_ref[...], preferred_element_type=jnp.float32)
    out_ref[...] = hidden[:, :columns] * slope_ref[...]


def local(
    grad_query,
    query_weight,
    grad_resid,
    embeds,
    norm_gain,
    img_pos,
    img_count,
    img_dest,
    merge_weight,
    merge_pre,
):
    groups = lax.axis_size(DP)
    shares = lax.axis_size(TP)
    side = lax.axis_size("zh")
    rows, columns = merge_pre.shape
    capacity = rows // groups
    positions = img_pos[0]
    image_count = positions.shape[0]
    plane = lax.axis_index("zh")
    place = jnp.stack(
        [lax.axis_index("core"), plane, (lax.axis_index("x") + side - plane) % side]
    ).astype(jnp.int32)
    forth = [(h * side + (a + h) % side, a * side + h) for a in range(side) for h in range(side)]
    back = [(target, source) for source, target in forth]

    own = lax.all_gather(query_weight, "zl", axis=0)
    picked = jnp.take(grad_query, positions, axis=0, mode="clip")
    picked = lax.all_gather(picked, "zh", axis=0)
    merge_weight, embeds, grad_resid, picked = lax.optimization_barrier(
        (merge_weight, embeds, grad_resid, picked)
    )
    merge_full = lax.all_gather(merge_weight, DP, axis=0)
    inputs = jnp.take(embeds, positions, axis=0, mode="clip").T
    residual = jnp.take(grad_resid, positions, axis=0, mode="clip").T
    gain = norm_gain[:, None]
    wide = inputs.astype(jnp.float32)
    squares = jnp.sum(wide * wide, axis=0)[None]
    scaled_input = lax.ppermute((gain * wide).astype(jnp.bfloat16), ("zh", "x"), back)
    is_live = jnp.arange(image_count, dtype=jnp.int32) < img_count[0]
    target_dev = img_dest[0]
    dest_hot = (
        (target_dev[:, None] == jnp.arange(groups, dtype=jnp.int32)[None, :]) & is_live[:, None]
    ).astype(jnp.int32)
    earlier = jnp.cumsum(dest_hot, axis=0) - dest_hot
    slot_index = jnp.sum(earlier * dest_hot, axis=1)
    target = jnp.where(is_live, target_dev * SLOT_PITCH + slot_index, -1)
    number = jnp.arange(rows, dtype=jnp.int32)
    spot = number // capacity * SLOT_PITCH + number % capacity
    slope = gelu_slope(merge_pre)

    other = lax.ppermute(own, "core", [(0, 1), (1, 0)])
    partial_value = query_products(place, picked, own, 0)
    partial_value = query_products(place, picked, other, 1, partial_value)
    width, count = inputs.shape
    swapped = lax.all_to_all(partial_value.reshape(shares, width, count), TP, 0, 0, tiled=True)
    normal_grad, stats = pl.pallas_call(
        reduce_kernel,
        in_specs=[pl.BlockSpec(memory_space=pltpu.SMEM)]
        + [pl.BlockSpec(memory_space=pltpu.VMEM)] * 3,
        out_shape=[
            jax.ShapeDtypeStruct((width, count), jnp.bfloat16),
            jax.ShapeDtypeStruct((side * side, 2, count), jnp.float32),
        ],
        compiler_params=pltpu.CompilerParams(vmem_limit_bytes=16 * MIB),
    )(place, swapped, scaled_input, squares)
    normal_grad = lax.ppermute(normal_grad, ("zh", "x"), forth)
    stats = jnp.sum(lax.all_to_all(stats, ("zh", "x"), 0, 0, tiled=True), axis=0)
    stats = lax.all_to_all(
        jnp.broadcast_to(stats[None], (side,) + stats.shape), "y", 0, 0, tiled=True
    )
    partial_hidden = merge_products(normal_grad, inputs, residual, gain, stats, merge_full, shares)
    hidden = lax.all_to_all(partial_hidden, TP, 0, 0, tiled=True)
    lanes = -(-columns // LANES) * LANES
    outbox = pl.pallas_call(
        send_kernel,
        out_shape=jax.ShapeDtypeStruct((groups * SLOT_PITCH, lanes), jnp.bfloat16),
        compiler_params=pltpu.CompilerParams(vmem_limit_bytes=16 * MIB),
    )(hidden, target[None])
    received = lax.all_to_all(outbox.reshape(groups, SLOT_PITCH, lanes), DP, 0, 0, tiled=True)
    return pl.pallas_call(
        finish_kernel,
        out_shape=jax.ShapeDtypeStruct((rows, columns), jnp.float32),
        compiler_params=pltpu.CompilerParams(vmem_limit_bytes=16 * MIB),
    )(received.reshape(groups * SLOT_PITCH, lanes), spot[:, None], slope)


def solution(mesh):
    split = Mesh(mesh.devices.reshape(4, 4, 2, 4, 4), DP + TP)
    in_specs = (
        P(DP, TP),
        P(DP, TP),
        P(DP, TP),
        P(DP, TP),
        P(TP),
        P(DP, None),
        P(DP),
        P(DP, None),
        P(DP, TP),
        P(DP, TP),
    )
    out_specs = P(DP, TP)
    return jax.shard_map(local, mesh=split, in_specs=in_specs, out_specs=out_specs, check_vma=False)
```

time: 213 us -> 225 us (1.056)
  waiting for transfers between devices: 61 us -> 88.3 us
  starting transfers between devices: 46.9 us -> 36 us
  blocking collectives: 66.2 us -> 61.3 us
    all_to_all x1 -> x2, waiting for transfers between devices: 3.98 us -> 31 us  [the longest x1 28 us: local(): lax.all_to_all(partial_value.reshape(shares, width, count), TP, 0, 0, til...]
    all_to_all x1 -> x2, starting transfers between devices: 22.2 us -> 10.6 us  [the longest x1 6.89 us: local(): lax.all_to_all(partial_value.reshape(shares, width, count), TP, 0, 0, til...]
    all_to_all x1, blocking collectives: 34 us -> 30.1 us  [local(): lax.all_to_all(stats, ('zh', 'x'), 0, 0, tiled=True)]
    unnamed x20 -> x16, local copies, waits for them, and re-layouts: 1.4 us -> 3.74 us
    pallas_call x1 -> x2, Pallas kernels: 5.7 us -> 6.27 us  [query_products(): pl.pallas_call(query_kernel, grid_spec=pltpu.PrefetchScalarGridSpec(num_s...]
    pallas_call x1 -> x2, Pallas kernels: 7.58 us -> 7.66 us  [the longest x1 6.82 us: merge_products(): pl.pallas_call(merge_kernel, in_specs=[local_spec] * 5 + [pl.BlockSpec(me...]
  transfers between devices with their start and end apart: 7 -> 9, of which waited for: 6 -> 6; matrix products, arithmetic and copies ran while one was open for 3% -> 2% of each run, Pallas kernels for 3% -> 3%
where the time goes in v5:
time: 225 us
  waiting for transfers between devices  88.3 us (39%)
  blocking collectives  61.3 us (27%)
  starting transfers between devices  36 us (16%)
  Pallas kernels  15.9 us (7%)
  between operations  14.3 us (6%)
  local copies, waits for them, and re-layouts  7.27 us (3%)
    all_gather x1, blocking collectives, local(): picked = lax.all_gather(picked, 'zh', axis=0)  31.2 us
    all_to_all x1, blocking collectives, local(): lax.all_to_all(stats, ('zh', 'x'), 0, 0, tiled=True)  30.1 us
    all_to_all x1, waiting for transfers between devices, local(): lax.all_to_all(partial_value.reshape(shares, width, count), TP, 0, 0, til...  28 us
    all_to_all x1, waiting for transfers between devices, local(): lax.all_to_all(outbox.reshape(groups, SLOT_PITCH, lanes), DP, 0, 0, tiled...  18.4 us
    all_gather x1, waiting for transfers between devices, local(): own = lax.all_gather(query_weight, 'zl', axis=0)  18.4 us
    all_to_all x1, waiting for transfers between devices, local(): hidden = lax.all_to_all(partial_hidden, TP, 0, 0, tiled=True)  17.9 us
    all_to_all x1, starting transfers between devices, local(): hidden = lax.all_to_all(partial_hidden, TP, 0, 0, tiled=True)  11.4 us
    all_to_all x1, starting transfers between devices, local(): lax.all_to_all(outbox.reshape(groups, SLOT_PITCH, lanes), DP, 0, 0, tiled...  10.2 us
  transfers between devices with their start and end apart: 9, of which 6 were waited for; matrix products, arithmetic and copies ran while one was open for 2% of the time, Pallas kernels for 3%

profile of v5, /device:TPU:1, one launch (start us, length us, event | category | flops | bytes accessed | tf_op | source)
XLA Modules:
  0.0 224.6 jit_solution(9032361244512103791)
XLA Ops:
  6.5 0.0 copy-start
  6.5 0.0 all-gather.6.cloned.1.call-start
  6.5 0.7 all-gather.6.cloned.1.call-update
  7.3 0.0 all-gather.8.cloned.1.call-start
  7.3 0.7 pad_clamp_fusion
  8.0 0.0 copy-done
  8.0 0.8 gather_fusion
  8.8 31.2 %all-gather = bf16[512,512]{1,0:T(8,128)(2,1)S(1)} all-gather(bf16[128,512]{1,0:T(8,128)(2,1)S(1)} %gather_fusion), channel_id=2, replica_groups=mesh['zh'=4,'zl'=4,'core'=2,'x'=4,'y'=4] {'zh'}, dimensions={0}, use_global_device_ids=true | all-gather | bytes 655360 | tf_op jit(solution)/shard_map/all_gather | solution.py:187
  40.0 0.0 all-gather.8.cloned.1.call-update
  40.0 18.4 %all-gather.6.cloned.1.call-done = bf16[1024,512]{1,0:T(8,128)(2,1)} async-done(((bf16[256,512]{1,0:T(8,128)(2,1)}), bf16[1024,512]{1,0:T(8,128)(2,1)}) %all-gather.6.cloned.1.call-update) | async-done | bytes 1048592 | tf_op jit(solution)/shard_map/all_gather | solution.py:185
  58.4 2.5 %collective-permute-start = (bf16[4,256,512]{2,1,0:T(8,128)(2,1)}, bf16[4,256,512]{2,1,0:T(8,128)(2,1)S(1)}, u32[]{:S(2)}, u32[]{:S(2)}) collective-permute-start(bf16[4,256,512]{2,1,0:T(8,128)(2,1)} %bitcast.28), channel_id=1, source_target_pairs={{0,16},{16,0},{1,17},{17,1},{2,18},{18,2},{3,19},{19,3},{4,20},{20... | collective-permute-start | bytes 3145736 | tf_op jit(solution)/shard_map/ppermute | solution.py:210
  60.9 0.1 pad_add_fusion.place_ref
  61.0 0.0 copy-start.2
  61.0 1.2 copy-done.2
  62.2 3.1 %shard_map.100.refs_0_ = bf16[4,4,2,256,128]{4,3,2,1,0:T(8,128)(2,1)} custom-call(s32[3]{0:T(128)S(1)} %pad_add_fusion.place_ref, bf16[4,128,512]{2,1,0:T(8,128)(2,1)S(1)} %bitcast.25, bf16[4,256,512]{2,1,0:T(8,128)(2,1)S(1)} %bitcast.29), custom_call_target="tpu_custom_call" | custom-call | tf_op jit(solution)/shard_map/pallas_call | solution.py:57
  65.4 0.0 collective-permute-done.weight_ref
  65.4 3.1 %shard_map.101 = bf16[4,4,2,256,128]{4,3,2,1,0:T(8,128)(2,1)} custom-call(s32[3]{0:T(128)S(1)} %pad_add_fusion.place_ref, bf16[4,128,512]{2,1,0:T(8,128)(2,1)S(1)} %bitcast.26, bf16[4,256,512]{2,1,0:T(8,128)(2,1)S(1)} %collective-permute-done.weight_ref, bf16[4,4,2,256,128]{4,3,2,1,0:T(8,128)(2,1)} %shard_map.100.refs_0_), custom_call_target="tpu_custom_call", output_to_operand_aliasing={{}: (3, {})} | custom-call | tf_op jit(solution)/shard_map/pallas_call | solution.py:57
  68.5 0.0 copy-start.3
  68.5 0.0 copy-start.6
  68.5 6.9 %all-to-all-start = ((bf16[16,512,128]{2,1,0:T(8,128)(2,1)}), bf16[16,512,128]{2,1,0:T(8,128)(2,1)S(1)}, u32[]{:S(2)}, u32[]{:S(2)}) async-start(bf16[16,512,128]{2,1,0:T(8,128)(2,1)} %bitcast.6), calls=%async_computation | async-start | bytes 4194304 | tf_op jit(solution)/shard_map/all_to_all | solution.py:214
  75.4 0.0 copy-done.3
  75.4 0.0 copy-start.4
  75.4 0.8 gather_fusion.1
  76.3 0.1 copy.14
  76.4 0.0 copy-done.6
  76.4 0.1 fusion.7
  76.6 0.7 collective-permute-start.1
  77.2 0.0 collective-permute-done.1.scaled_ref
  77.2 28.0 %all-to-all-done.parts_ref = bf16[16,512,128]{2,1,0:T(8,128)(2,1)S(1)} async-done(((bf16[16,512,128]{2,1,0:T(8,128)(2,1)}), bf16[16,512,128]{2,1,0:T(8,128)(2,1)S(1)}, u32[]{:S(2)}, u32[]{:S(2)}) %all-to-all-start) | async-done | bytes 2097184 | tf_op jit(solution)/shard_map/all_to_all | solution.py:214
  105.3 0.8 shard_map.102
  106.1 0.7 collective-permute-start.2
  106.8 30.1 %all_to_all.25 = f32[16,2,128]{2,1,0:T(2,128)S(1)} all-to-all(f32[16,2,128]{2,1,0:T(2,128)S(1)} %get-tuple-element.15), channel_id=1, replica_groups=mesh['zh'=4,'zl'=4,'core'=2,'x'=4,'y'=4] {'zh','x'}, dimensions={0} | all-to-all | bytes 32768 | tf_op jit(solution)/shard_map/all_to_all | solution.py:226
  137.0 0.6 broadcast_in_dim.29
  137.6 3.7 %all-to-all-start.2 = ((f32[4,2,128]{2,1,0:T(2,128)}), f32[4,2,128]{2,1,0:T(2,128)S(1)}, u32[]{:S(2)}, u32[]{:S(2)}) async-start(f32[4,2,128]{2,1,0:T(2,128)} %broadcast_in_dim.29), calls=%async_computation.2 | async-start | bytes 8192 | tf_op jit(solution)/shard_map/all_to_all | solution.py:227
  141.2 0.0 copy-done.4
  141.2 0.8 gather_fusion.2
  142.1 0.1 copy.15
  142.2 0.1 copy.16.gain_ref
  142.4 3.0 %all-to-all-done.2.stat_ref = f32[4,2,128]{2,1,0:T(2,128)S(1)} async-done(((f32[4,2,128]{2,1,0:T(2,128)}), f32[4,2,128]{2,1,0:T(2,128)S(1)}, u32[]{:S(2)}, u32[]{:S(2)}) %all-to-all-start.2) | async-done | bytes 4128 | tf_op jit(solution)/shard_map/all_to_all | solution.py:227
  145.4 0.0 collective-permute-done.2.grad_ref
  145.4 1.8 all-gather.8.cloned.1.call-done
  147.1 0.0 copy-start.1
  147.1 2.5 %copy-done.1 = bf16[5120,512]{1,0:T(8,128)(2,1)S(1)} copy-done((bf16[5120,512]{1,0:T(8,128)(2,1)S(1)}, bf16[5120,512]{1,0:T(8,128)(2,1)}, u32[]{:S(2)}) %copy-start.1) | copy-done | bytes 5242904
  149.6 6.8 %shard_map.103 = bf16[16,160,256]{2,1,0:T(8,128)(2,1)} custom-call(bf16[512,128]{1,0:T(8,128)(2,1)S(1)} %collective-permute-done.2.grad_ref, bf16[512,128]{1,0:T(8,128)(2,1)S(1)} %bitcast.27, bf16[512,128]{1,0:T(8,128)(2,1)S(1)} %bitcast.31, f32[512,1]{1,0:T(8,128)S(1)} %copy.16.gain_ref, f32[4,2,128]{2,1,0:T(2,128)S(1)} %all-to-all-done.2.stat_ref, ...), custom_call_target="tpu_custom_call" | custom-call | tf_op jit(solution)/shard_map/pallas_call | solution.py:123
  156.4 0.0 copy-start.7
  156.5 0.0 copy-start.5
  156.5 11.4 %all-to-all-start.3 = ((bf16[16,160,256]{2,1,0:T(8,128)(2,1)}), bf16[16,160,256]{2,1,0:T(8,128)(2,1)S(1)}, u32[]{:S(2)}, u32[]{:S(2)}) async-start(bf16[16,160,256]{2,1,0:T(8,128)(2,1)} %shard_map.103), calls=%async_computation.3 | async-start | bytes 2621440 | tf_op jit(solution)/shard_map/all_to_all | solution.py:231
  168.6 0.0 copy-done.7
  168.6 0.1 fusion.18
  168.7 0.2 reduce_window_sum.11
  168.8 0.2 select_reduce_fusion
  169.0 17.9 %all-to-all-done.3.hidden_ref = bf16[16,160,256]{2,1,0:T(8,128)(2,1)S(1)} async-done(((bf16[16,160,256]{2,1,0:T(8,128)(2,1)}), bf16[16,160,256]{2,1,0:T(8,128)(2,1)S(1)}, u32[]{:S(2)}, u32[]{:S(2)}) %all-to-all-start.3) | async-done | bytes 1310752 | tf_op jit(solution)/shard_map/all_to_all | solution.py:231
  186.9 1.0 shard_map.104
  188.0 10.2 %all-to-all-start.4 = ((bf16[32,8,384]{2,1,0:T(8,128)(2,1)}), bf16[32,8,384]{2,1,0:T(8,128)(2,1)S(1)}, u32[]{:S(2)}, u32[]{:S(2)}) async-start(bf16[32,8,384]{2,1,0:T(8,128)(2,1)} %bitcast.15), calls=%async_computation.4 | async-start | bytes 393216 | tf_op jit(solution)/shard_map/all_to_all | solution.py:238
  198.2 0.0 copy-done.5
  198.2 0.1 fusion.3.slope_ref
  198.3 18.4 %all-to-all-done.4 = bf16[32,8,384]{2,1,0:T(8,128)(2,1)S(1)} async-done(((bf16[32,8,384]{2,1,0:T(8,128)(2,1)}), bf16[32,8,384]{2,1,0:T(8,128)(2,1)S(1)}, u32[]{:S(2)}, u32[]{:S(2)}) %all-to-all-start.4) | async-done | bytes 196640 | tf_op jit(solution)/shard_map/all_to_all | solution.py:238
  216.8 1.0 shard_map.105
  (4 shorter events, 0.1 us)
Async XLA Ops:
  6.5 1.4 copy-start
  6.5 51.9 %all-gather.6.cloned.1.call-start = ((), (), s32[]{:S(2)}) async-start(), calls=%async_computation.5 | async-start | bytes 1310720 | tf_op jit(solution)/shard_map/all_gather | solution.py:185
  7.3 139.9 %all-gather.8.cloned.1.call-start = ((), (), s32[]{:S(2)}) async-start(), calls=%async_computation.6 | async-start | bytes 5406720 | tf_op jit(solution)/shard_map/all_gather | solution.py:191
  58.4 6.9 %collective-permute-start = (bf16[4,256,512]{2,1,0:T(8,128)(2,1)}, bf16[4,256,512]{2,1,0:T(8,128)(2,1)S(1)}, u32[]{:S(2)}, u32[]{:S(2)}) collective-permute-start(bf16[4,256,512]{2,1,0:T(8,128)(2,1)} %bitcast.28), channel_id=1, source_target_pairs={{0,16},{16,0},{1,17},{17,1},{2,18},{18,2},{3,19},{19,3},{4,20},{20... | collective-permute-start | bytes 3145736 | tf_op jit(solution)/shard_map/ppermute | solution.py:210
  61.0 1.2 copy-start.2
  68.5 6.9 %copy-start.3 = (bf16[256,512]{1,0:T(8,128)(2,1)S(1)}, bf16[256,512]{1,0:T(8,128)(2,1)}, u32[]{:S(2)}) copy-start(bf16[256,512]{1,0:T(8,128)(2,1)} %param.13) | copy-start | bytes 786436
  68.5 7.9 %copy-start.6 = (f32[512]{0:T(512)S(1)}, f32[512]{0:T(512)}, u32[]{:S(2)}) copy-start(f32[512]{0:T(512)} %param.14) | copy-start | bytes 6148
  68.5 36.8 %all-to-all-start = ((bf16[16,512,128]{2,1,0:T(8,128)(2,1)}), bf16[16,512,128]{2,1,0:T(8,128)(2,1)S(1)}, u32[]{:S(2)}, u32[]{:S(2)}) async-start(bf16[16,512,128]{2,1,0:T(8,128)(2,1)} %bitcast.6), calls=%async_computation | async-start | bytes 4194304 | tf_op jit(solution)/shard_map/all_to_all | solution.py:214
  75.4 65.8 %copy-start.4 = (bf16[256,512]{1,0:T(8,128)(2,1)S(1)}, bf16[256,512]{1,0:T(8,128)(2,1)}, u32[]{:S(2)}) copy-start(bf16[256,512]{1,0:T(8,128)(2,1)} %param.12) | copy-start | bytes 786436
  76.6 0.7 collective-permute-start.1
  106.1 39.3 %collective-permute-start.2 = (bf16[512,128]{1,0:T(8,128)(2,1)S(1)}, bf16[512,128]{1,0:T(8,128)(2,1)S(1)}, u32[]{:S(2)}, u32[]{:S(2)}) collective-permute-start(bf16[512,128]{1,0:T(8,128)(2,1)S(1)} %get-tuple-element.13), channel_id=1, source_target_pairs={{0,0},{132,4},{264,8},{396,12},{4,128},{136,132},{268,136},{384,14... | collective-permute-start | bytes 393224 | tf_op jit(solution)/shard_map/ppermute | solution.py:225
  137.6 7.8 %all-to-all-start.2 = ((f32[4,2,128]{2,1,0:T(2,128)}), f32[4,2,128]{2,1,0:T(2,128)S(1)}, u32[]{:S(2)}, u32[]{:S(2)}) async-start(f32[4,2,128]{2,1,0:T(2,128)} %broadcast_in_dim.29), calls=%async_computation.2 | async-start | bytes 8192 | tf_op jit(solution)/shard_map/all_to_all | solution.py:227
  147.1 2.5 %copy-start.1 = (bf16[5120,512]{1,0:T(8,128)(2,1)S(1)}, bf16[5120,512]{1,0:T(8,128)(2,1)}, u32[]{:S(2)}) copy-start(bf16[5120,512]{1,0:T(8,128)(2,1)} %all-gather.8.cloned.1.call-done) | copy-start | bytes 15728644
  156.4 12.1 %copy-start.7 = (s32[1,128]{1,0:T(1,128)S(1)}, s32[1,128]{1,0:T(1,128)}, u32[]{:S(2)}) copy-start(s32[1,128]{1,0:T(1,128)} %param.17) | copy-start | bytes 1540
  156.5 41.8 %copy-start.5 = (bf16[192,320]{1,0:T(8,128)(2,1)S(1)}, bf16[192,320]{1,0:T(8,128)(2,1)}, u32[]{:S(2)}) copy-start(bf16[192,320]{1,0:T(8,128)(2,1)} %param.19) | copy-start | bytes 368644
  156.5 30.4 %all-to-all-start.3 = ((bf16[16,160,256]{2,1,0:T(8,128)(2,1)}), bf16[16,160,256]{2,1,0:T(8,128)(2,1)S(1)}, u32[]{:S(2)}, u32[]{:S(2)}) async-start(bf16[16,160,256]{2,1,0:T(8,128)(2,1)} %shard_map.103), calls=%async_computation.3 | async-start | bytes 2621440 | tf_op jit(solution)/shard_map/all_to_all | solution.py:231
  188.0 28.8 %all-to-all-start.4 = ((bf16[32,8,384]{2,1,0:T(8,128)(2,1)}), bf16[32,8,384]{2,1,0:T(8,128)(2,1)S(1)}, u32[]{:S(2)}, u32[]{:S(2)}) async-start(bf16[32,8,384]{2,1,0:T(8,128)(2,1)} %bitcast.15), calls=%async_computation.4 | async-start | bytes 393216 | tf_op jit(solution)/shard_map/all_to_all | solution.py:238
Sparse Core Ops, SparseCore 0:
  9.5 48.9 all-gather.5
  60.6 86.5 all-gather.7

commit v6 on v2

--- a/solution.py
+++ b/solution.py
@@ -8,7 +8,7 @@
 
 D = 8192
 NORM_EPS = 1e-06
-VMEM_BYTES = 24 * 1024 * 1024
+MIB = 1024 * 1024
 LANES = 128
 DP = ("zh", "zl", "core")
 TP = ("x", "y")
@@ -21,36 +21,43 @@
     return cdf_part + value * pdf_part
 
 
-def query_kernel(rows_ref, weight_ref, out_ref, turned):
+def query_kernel(core_ref, rows_ref, own_ref, other_ref, out_ref, turned):
     parts, count, depth = rows_ref.shape
+    height = own_ref.shape[1]
+    core = core_ref[0]
 
     @pl.when(pl.program_id(0) == 0)
     def _():
         turned[...] = rows_ref[...].reshape(parts * count, depth).T
 
-    weight = weight_ref[...].reshape(-1, depth)
-    product = jnp.dot(weight, turned[...], preferred_element_type=jnp.float32)
-    product = product.astype(out_ref.dtype)
-    for part in range(parts):
-        out_ref[part] = product[:, part * count : (part + 1) * count]
-
-
-def query_products(rows, weights):
+    for weight_ref, place in ((own_ref, core), (other_ref, 1 - core)):
+        product = jnp.dot(weight_ref[0], turned[...], preferred_element_type=jnp.float32)
+        product = product.astype(out_ref.dtype)
+        spot = pl.ds(pl.multiple_of(place * height, height), height)
+        for part in range(parts):
+            out_ref[part, spot] = product[:, part * count : (part + 1) * count]
+
+
+def query_products(core, rows, own, other):
     parts, count, depth = rows.shape
-    blocks, height, _ = weights.shape
-    steps = blocks // 2
+    steps, height, _ = own.shape
+    weight_spec = pl.BlockSpec((1, height, depth), lambda i, _: (i, 0, 0))
     return pl.pallas_call(
         query_kernel,
-        grid=(steps,),
-        in_specs=[
-            pl.BlockSpec((parts, count, depth), lambda i: (0, 0, 0)),
-            pl.BlockSpec((2, height, depth), lambda i: (i, 0, 0)),
-        ],
-        out_specs=pl.BlockSpec((parts, 2 * height, count), lambda i: (i, 0, 0)),
+        grid_spec=pltpu.PrefetchScalarGridSpec(
+            num_scalar_prefetch=1,
+            grid=(steps,),
+            in_specs=[
+                pl.BlockSpec((parts, count, depth), lambda i, _: (0, 0, 0)),
+                weight_spec,
+                weight_spec,
+            ],
+            out_specs=pl.BlockSpec((parts, 2 * height, count), lambda i, _: (i, 0, 0)),
+            scratch_shapes=[pltpu.VMEM((depth, parts * count), jnp.bfloat16)],
+        ),
         out_shape=jax.ShapeDtypeStruct((steps * parts, 2 * height, count), jnp.bfloat16),
-        scratch_shapes=[pltpu.VMEM((depth, parts * count), jnp.bfloat16)],
-        compiler_params=pltpu.CompilerParams(vmem_limit_bytes=VMEM_BYTES),
-    )(rows, weights)
+        compiler_params=pltpu.CompilerParams(vmem_limit_bytes=24 * MIB),
+    )(core, rows, own, other)
 
 
 def handoff_kernel(capacity, grad_ref, input_ref, resid_ref, gain_ref, stat_ref, target_ref, out_ref):
@@ -116,7 +123,7 @@
         out_specs=pl.BlockSpec((per_step, height, 2 * rows), lambda i: (i, 0, 0)),
         out_shape=jax.ShapeDtypeStruct((shares, height, 2 * rows), jnp.bfloat16),
         scratch_shapes=[pltpu.VMEM((width, rows), jnp.bfloat16)],
-        compiler_params=pltpu.CompilerParams(vmem_limit_bytes=VMEM_BYTES),
+        compiler_params=pltpu.CompilerParams(vmem_limit_bytes=24 * MIB),
     )(box, weights)
 
 
@@ -140,12 +147,15 @@
     image_count = positions.shape[0]
     width = embeds.shape[1]
 
-    query_full = lax.all_gather(query_weight, ("zh", "core"), axis=0)
-    merge_weight, query_full = lax.optimization_barrier((merge_weight, query_full))
+    own = lax.all_gather(query_weight, "zh", axis=0)
+    picked = jnp.take(grad_query, positions, axis=0, mode="clip")
+    picked = lax.all_gather(picked, "zl", axis=0)
+    merge_weight, slope, picked = lax.optimization_barrier(
+        (merge_weight, gelu_slope(merge_pre), picked)
+    )
     merge_full = lax.all_gather(merge_weight, DP, axis=0)
-    picked = lax.all_gather(jnp.take(grad_query, positions, axis=0), "zl", axis=0)
-    inputs = jnp.take(embeds, positions, axis=0).T
-    residual = jnp.take(grad_resid, positions, axis=0).T
+    inputs = jnp.take(embeds, positions, axis=0, mode="clip").T
+    residual = jnp.take(grad_resid, positions, axis=0, mode="clip").T
     gain = norm_gain[:, None]
     wide = inputs.astype(jnp.float32)
     squares = jnp.sum(wide * wide, axis=0)
@@ -159,7 +169,9 @@
     pitch = capacity * (width // LANES)
     target = jnp.where(is_live, target_dev * pitch + slot_index, -groups * pitch)
 
-    partial_value = query_products(picked, query_full)
+    other = lax.ppermute(own, "core", [(0, 1), (1, 0)])
+    core = lax.axis_index("core").astype(jnp.int32)[None]
+    partial_value = query_products(core, picked, own, other)
     swapped = lax.all_to_all(partial_value, TP, 0, 0, tiled=True)
     normal_grad = jnp.sum(swapped.astype(jnp.float32), axis=0).astype(jnp.bfloat16)
     exchange = [(b * side + a, a * side + b) for a in range(side) for b in range(side)]
@@ -172,7 +184,7 @@
     outbox = pl.pallas_call(
         lambda *refs: handoff_kernel(capacity, *refs),
         out_shape=jax.ShapeDtypeStruct((groups * pitch, LANES), jnp.bfloat16),
-        compiler_params=pltpu.CompilerParams(vmem_limit_bytes=VMEM_BYTES),
+        compiler_params=pltpu.CompilerParams(vmem_limit_bytes=24 * MIB),
     )(normal_grad, inputs, residual, gain, stats, target[None])
     received = lax.all_to_all(outbox.reshape(groups, pitch, LANES), DP, 0, 0, tiled=True)
     partial_hidden = merge_products(
@@ -182,7 +194,7 @@
     hidden = jnp.sum(hidden.astype(jnp.float32), axis=0)
     rows = merge_pre.shape[0]
     hidden = jnp.concatenate([hidden[:, :rows].T, hidden[:, rows:].T], axis=1)
-    return hidden * gelu_slope(merge_pre)
+    return hidden * slope
 
 
 def solution(mesh):

time: 229 us -> 219 us (0.956)
  waiting for transfers between devices: 102 us -> 86.4 us
  blocking collectives: 68.2 us -> 71.7 us
  local copies, waits for them, and re-layouts: 6.65 us -> 9.27 us
    all_gather x1, waiting for transfers between devices: 71.2 us -> 49.5 us  [local(): own = lax.all_gather(query_weight, 'zh', axis=0)]
    all_to_all x1, waiting for transfers between devices: 23.7 us -> 28.5 us  [local(): swapped = lax.all_to_all(partial_value, TP, 0, 0, tiled=True)]
    ppermute x0 -> x1, starting transfers between devices: none -> 3.69 us  [local(): other = lax.ppermute(own, 'core', [(0, 1), (1, 0)])]
    all_gather x1, blocking collectives: 13.3 us -> 16.3 us  [local(): picked = lax.all_gather(picked, 'zl', axis=0)]
    ppermute x0 -> x1, waiting for transfers between devices: none -> 2.47 us  [local(): other = lax.ppermute(own, 'core', [(0, 1), (1, 0)])]
    unnamed x18 -> x15, local copies, waits for them, and re-layouts: 3.02 us -> 4.77 us
  transfers between devices with their start and end apart: 5 -> 6, of which waited for: 3 -> 4; matrix products, arithmetic and copies ran while one was open for 3% -> 3% of each run, Pallas kernels for 2% -> 2%
where the time goes in v6:
time: 219 us; the launch traced here: 218 us
  waiting for transfers between devices  86.4 us (39%)
  blocking collectives  71.7 us (33%)
  starting transfers between devices  27.3 us (12%)
  between operations  14.3 us (7%)
  local copies, waits for them, and re-layouts  9.27 us (4%)
  Pallas kernels  6.56 us (3%)
    all_gather x1, waiting for transfers between devices, local(): own = lax.all_gather(query_weight, 'zh', axis=0)  49.5 us
    all_to_all x1, blocking collectives, local(): lax.all_to_all(outbox.reshape(groups, pitch, LANES), DP, 0, 0, tiled=True)  28.7 us
    all_to_all x1, waiting for transfers between devices, local(): swapped = lax.all_to_all(partial_value, TP, 0, 0, tiled=True)  28.5 us
    all_to_all x1, blocking collectives, local(): hidden = lax.all_to_all(partial_hidden, TP, 0, 0, tiled=True)  26.7 us
    all_to_all x1, starting transfers between devices, local(): lax.all_to_all(jnp.broadcast_to(stats[None], (shares,) + stats.shape), TP...  17.5 us
    all_gather x1, blocking collectives, local(): picked = lax.all_gather(picked, 'zl', axis=0)  16.3 us
    all_to_all x1, starting transfers between devices, local(): swapped = lax.all_to_all(partial_value, TP, 0, 0, tiled=True)  5.4 us
    all_to_all x1, waiting for transfers between devices, local(): lax.all_to_all(jnp.broadcast_to(stats[None], (shares,) + stats.shape), TP...  5.29 us
  transfers between devices with their start and end apart: 6, of which 4 were waited for; matrix products, arithmetic and copies ran while one was open for 3% of the time, Pallas kernels for 2%

profile of v6, /device:TPU:1, one launch (start us, length us, event | category | flops | bytes accessed | tf_op | source)
XLA Modules:
  0.0 217.6 jit_solution(1523648639357612845)
XLA Ops:
  6.5 0.0 copy-start
  6.5 0.0 all-gather.6.cloned.1.call-start
  6.5 0.7 all-gather.6.cloned.1.call-update
  7.3 0.0 all-gather.8.cloned.1.call-start
  7.3 1.0 copy.16
  8.3 0.7 pad_clamp_fusion
  9.0 0.0 copy-done
  9.0 0.8 gather_fusion
  9.9 16.3 %all-gather = bf16[512,512]{1,0:T(8,128)(2,1)S(1)} all-gather(bf16[128,512]{1,0:T(8,128)(2,1)S(1)} %gather_fusion), channel_id=2, replica_groups=mesh['zh'=4,'zl'=4,'core'=2,'x'=4,'y'=4] {'zl'}, dimensions={0}, use_global_device_ids=true | all-gather | bytes 655360 | tf_op jit(solution)/shard_map/all_gather | solution.py:152
  26.1 0.1 fusion.3
  26.3 0.0 all-gather.8.cloned.1.call-update
  26.3 49.5 %all-gather.6.cloned.1.call-done = bf16[1024,512]{1,0:T(8,128)(2,1)} async-done(((bf16[256,512]{1,0:T(8,128)(2,1)}), bf16[1024,512]{1,0:T(8,128)(2,1)}) %all-gather.6.cloned.1.call-update) | async-done | bytes 1048592 | tf_op jit(solution)/shard_map/all_gather | solution.py:150
  75.8 3.7 %collective-permute-start = (bf16[4,256,512]{2,1,0:T(8,128)(2,1)}, bf16[4,256,512]{2,1,0:T(8,128)(2,1)S(1)}, u32[]{:S(2)}, u32[]{:S(2)}) collective-permute-start(bf16[4,256,512]{2,1,0:T(8,128)(2,1)} %bitcast.29), channel_id=1, source_target_pairs={{0,16},{16,0},{1,17},{17,1},{2,18},{18,2},{3,19},{19,3},{4,20},{20... | collective-permute-start | bytes 3145736 | tf_op jit(solution)/shard_map/ppermute | solution.py:172
  79.5 2.5 %collective-permute-done.other_ref = bf16[4,256,512]{2,1,0:T(8,128)(2,1)S(1)} collective-permute-done((bf16[4,256,512]{2,1,0:T(8,128)(2,1)}, bf16[4,256,512]{2,1,0:T(8,128)(2,1)S(1)}, u32[]{:S(2)}, u32[]{:S(2)}) %collective-permute-start) | collective-permute-done | bytes 1048608 | tf_op jit(solution)/shard_map/ppermute | solution.py:172
  81.9 0.0 copy-start.2
  82.0 1.2 copy-done.2
  83.2 3.2 %shard_map.100 = bf16[16,512,128]{2,1,0:T(8,128)(2,1)} custom-call(s32[1]{0:T(128)} %bitcast.core_ref, bf16[4,128,512]{2,1,0:T(8,128)(2,1)S(1)} %bitcast.27, bf16[4,256,512]{2,1,0:T(8,128)(2,1)S(1)} %bitcast.30, bf16[4,256,512]{2,1,0:T(8,128)(2,1)S(1)} %collective-permute-done.other_ref), custom_call_target="tpu_custom_call" | custom-call | tf_op jit(solution)/shard_map/pallas_call | solution.py:45
  86.3 5.4 %all-to-all-start = ((bf16[16,512,128]{2,1,0:T(8,128)(2,1)}), bf16[16,512,128]{2,1,0:T(8,128)(2,1)S(1)}, u32[]{:S(2)}, u32[]{:S(2)}) async-start(bf16[16,512,128]{2,1,0:T(8,128)(2,1)} %shard_map.100), calls=%async_computation | async-start | bytes 4194304 | tf_op jit(solution)/shard_map/all_to_all | solution.py:175
  91.7 0.0 copy-start.6
  91.8 0.0 copy-start.3
  91.8 0.0 copy-start.5
  92.5 0.0 copy-start.4
  92.5 28.5 %all-to-all-done = bf16[16,512,128]{2,1,0:T(8,128)(2,1)S(1)} async-done(((bf16[16,512,128]{2,1,0:T(8,128)(2,1)}), bf16[16,512,128]{2,1,0:T(8,128)(2,1)S(1)}, u32[]{:S(2)}, u32[]{:S(2)}) %all-to-all-start) | async-done | bytes 2097184 | tf_op jit(solution)/shard_map/all_to_all | solution.py:175
  121.0 0.3 reduce_sum.50
  121.3 0.7 collective-permute-start.1
  121.9 0.0 copy-done.6
  121.9 0.1 fusion.9
  122.0 0.0 copy-done.3
  122.1 0.8 gather_fusion.1
  122.9 0.1 copy.17
  123.0 0.2 reduce_window_sum.11
  123.2 0.2 select_reduce_fusion
  123.4 0.0 collective-permute-done.1.refs_0_
  123.4 0.0 copy-done.5
  123.4 0.2 fusion.6
  123.6 0.6 broadcast_in_dim.28
  124.2 17.5 %all-to-all-start.1 = ((f32[16,2,128]{2,1,0:T(2,128)}), f32[16,2,128]{2,1,0:T(2,128)S(1)}, u32[]{:S(2)}, u32[]{:S(2)}) async-start(f32[16,2,128]{2,1,0:T(2,128)} %broadcast_in_dim.28), calls=%async_computation.1 | async-start | bytes 32768 | tf_op jit(solution)/shard_map/all_to_all | solution.py:181
  141.7 0.0 copy-done.4
  141.7 0.8 gather_fusion.2
  142.6 0.1 copy.18
  142.7 0.1 copy.19.refs_3_
  142.9 5.3 %all-to-all-done.1.refs_4_ = f32[16,2,128]{2,1,0:T(2,128)S(1)} async-done(((f32[16,2,128]{2,1,0:T(2,128)}), f32[16,2,128]{2,1,0:T(2,128)S(1)}, u32[]{:S(2)}, u32[]{:S(2)}) %all-to-all-start.1) | async-done | bytes 16416 | tf_op jit(solution)/shard_map/all_to_all | solution.py:181
  148.1 0.5 shard_map.101
  148.6 28.7 %all_to_all.20 = bf16[32,24,128]{2,1,0:T(8,128)(2,1)S(1)} all-to-all(bf16[32,24,128]{2,1,0:T(8,128)(2,1)S(1)} %bitcast.31), channel_id=1, replica_groups=mesh['zh'=4,'zl'=4,'core'=2,'x'=4,'y'=4] {'zh','zl','core'}, dimensions={0} | all-to-all | bytes 393216 | tf_op jit(solution)/shard_map/all_to_all | solution.py:189
  177.3 0.0 all-gather.8.cloned.1.call-done
  177.3 0.0 copy-start.1
  177.3 2.5 %copy-done.1 = bf16[5120,512]{1,0:T(8,128)(2,1)S(1)} copy-done((bf16[5120,512]{1,0:T(8,128)(2,1)S(1)}, bf16[5120,512]{1,0:T(8,128)(2,1)}, u32[]{:S(2)}) %copy-start.1) | copy-done | bytes 5242904
  179.8 2.9 %shard_map.102 = bf16[16,160,384]{2,1,0:T(8,128)(2,1)S(1)} custom-call(bf16[768,128]{1,0:T(8,128)(2,1)S(1)} %bitcast.32, bf16[32,160,512]{2,1,0:T(8,128)(2,1)S(1)} %bitcast.26), custom_call_target="tpu_custom_call" | custom-call | tf_op jit(solution)/shard_map/pallas_call | solution.py:116
  182.7 26.7 %all_to_all.21 = bf16[16,160,384]{2,1,0:T(8,128)(2,1)S(1)} all-to-all(bf16[16,160,384]{2,1,0:T(8,128)(2,1)S(1)} %shard_map.102), channel_id=1, replica_groups=mesh['zh'=4,'zl'=4,'core'=2,'x'=4,'y'=4] {'x','y'}, dimensions={0} | all-to-all | bytes 3932160 | tf_op jit(solution)/shard_map/all_to_all | solution.py:193
  209.5 0.3 convert_reduce_fusion
  209.7 0.1 slice_bitcast_fusion.1
  209.9 0.9 copy.20
  (4 shorter events, 0.1 us)
Async XLA Ops:
  6.5 2.5 %copy-start = (bf16[256,512]{1,0:T(8,128)(2,1)S(1)}, bf16[256,512]{1,0:T(8,128)(2,1)}, u32[]{:S(2)}) copy-start(bf16[256,512]{1,0:T(8,128)(2,1)} %param.10) | copy-start | bytes 786436
  6.5 69.2 %all-gather.6.cloned.1.call-start = ((), (), s32[]{:S(2)}) async-start(), calls=%async_computation.4 | async-start | bytes 1310720 | tf_op jit(solution)/shard_map/all_gather | solution.py:150
  7.3 170.0 %all-gather.8.cloned.1.call-start = ((), (), s32[]{:S(2)}) async-start(), calls=%async_computation.5 | async-start | bytes 5406720 | tf_op jit(solution)/shard_map/all_gather | solution.py:156
  75.8 6.2 %collective-permute-start = (bf16[4,256,512]{2,1,0:T(8,128)(2,1)}, bf16[4,256,512]{2,1,0:T(8,128)(2,1)S(1)}, u32[]{:S(2)}, u32[]{:S(2)}) collective-permute-start(bf16[4,256,512]{2,1,0:T(8,128)(2,1)} %bitcast.29), channel_id=1, source_target_pairs={{0,16},{16,0},{1,17},{17,1},{2,18},{18,2},{3,19},{19,3},{4,20},{20... | collective-permute-start | bytes 3145736 | tf_op jit(solution)/shard_map/ppermute | solution.py:172
  81.9 1.2 copy-start.2
  86.3 34.6 %all-to-all-start = ((bf16[16,512,128]{2,1,0:T(8,128)(2,1)}), bf16[16,512,128]{2,1,0:T(8,128)(2,1)S(1)}, u32[]{:S(2)}, u32[]{:S(2)}) async-start(bf16[16,512,128]{2,1,0:T(8,128)(2,1)} %shard_map.100), calls=%async_computation | async-start | bytes 4194304 | tf_op jit(solution)/shard_map/all_to_all | solution.py:175
  91.7 30.2 %copy-start.6 = (s32[1,128]{1,0:T(1,128)S(1)}, s32[1,128]{1,0:T(1,128)}, u32[]{:S(2)}) copy-start(s32[1,128]{1,0:T(1,128)} %param.17) | copy-start | bytes 1540
  91.8 30.3 %copy-start.3 = (bf16[256,512]{1,0:T(8,128)(2,1)S(1)}, bf16[256,512]{1,0:T(8,128)(2,1)}, u32[]{:S(2)}) copy-start(bf16[256,512]{1,0:T(8,128)(2,1)} %param.13) | copy-start | bytes 786436
  91.8 31.6 %copy-start.5 = (f32[512]{0:T(512)S(1)}, f32[512]{0:T(512)}, u32[]{:S(2)}) copy-start(f32[512]{0:T(512)} %param.14) | copy-start | bytes 6148
  92.5 49.2 %copy-start.4 = (bf16[256,512]{1,0:T(8,128)(2,1)S(1)}, bf16[256,512]{1,0:T(8,128)(2,1)}, u32[]{:S(2)}) copy-start(bf16[256,512]{1,0:T(8,128)(2,1)} %param.12) | copy-start | bytes 786436
  121.3 2.1 collective-permute-start.1
  124.2 24.0 %all-to-all-start.1 = ((f32[16,2,128]{2,1,0:T(2,128)}), f32[16,2,128]{2,1,0:T(2,128)S(1)}, u32[]{:S(2)}, u32[]{:S(2)}) async-start(f32[16,2,128]{2,1,0:T(2,128)} %broadcast_in_dim.28), calls=%async_computation.1 | async-start | bytes 32768 | tf_op jit(solution)/shard_map/all_to_all | solution.py:181
  177.3 2.5 %copy-start.1 = (bf16[5120,512]{1,0:T(8,128)(2,1)S(1)}, bf16[5120,512]{1,0:T(8,128)(2,1)}, u32[]{:S(2)}) copy-start(bf16[5120,512]{1,0:T(8,128)(2,1)} %all-gather.8.cloned.1.call-done) | copy-start | bytes 15728644
Sparse Core Ops, SparseCore 0:
  9.5 66.2 all-gather.5
  77.9 76.4 all-gather.7

commit v7 on v6

--- a/solution.py
+++ b/solution.py
@@ -21,51 +21,61 @@
     return cdf_part + value * pdf_part
 
 
-def query_kernel(core_ref, rows_ref, own_ref, other_ref, out_ref, turned):
+def query_kernel(plane_ref, rows_ref, weight_ref, out_ref, turned):
     parts, count, depth = rows_ref.shape
-    height = own_ref.shape[1]
-    core = core_ref[0]
+    plane = plane_ref[0]
 
     @pl.when(pl.program_id(0) == 0)
     def _():
         turned[...] = rows_ref[...].reshape(parts * count, depth).T
 
-    for weight_ref, place in ((own_ref, core), (other_ref, 1 - core)):
-        product = jnp.dot(weight_ref[0], turned[...], preferred_element_type=jnp.float32)
-        product = product.astype(out_ref.dtype)
-        spot = pl.ds(pl.multiple_of(place * height, height), height)
-        for part in range(parts):
-            out_ref[part, spot] = product[:, part * count : (part + 1) * count]
-
-
-def query_products(core, rows, own, other):
+    weight = weight_ref[...].reshape(-1, depth)
+    product = jnp.dot(weight, turned[...], preferred_element_type=jnp.float32)
+    product = product.astype(out_ref.dtype)
+    for part in range(parts):
+        out_ref[lax.rem(part + plane, parts), 0] = product[:, part * count : (part + 1) * count]
+
+
+def query_products(plane, rows, weights):
     parts, count, depth = rows.shape
-    steps, height, _ = own.shape
-    weight_spec = pl.BlockSpec((1, height, depth), lambda i, _: (i, 0, 0))
-    return pl.pallas_call(
+    blocks, height, _ = weights.shape
+    steps = blocks // 2
+    result = pl.pallas_call(
         query_kernel,
         grid_spec=pltpu.PrefetchScalarGridSpec(
             num_scalar_prefetch=1,
             grid=(steps,),
             in_specs=[
                 pl.BlockSpec((parts, count, depth), lambda i, _: (0, 0, 0)),
-                weight_spec,
-                weight_spec,
+                pl.BlockSpec((2, height, depth), lambda i, _: (i, 0, 0)),
             ],
-            out_specs=pl.BlockSpec((parts, 2 * height, count), lambda i, _: (i, 0, 0)),
+            out_specs=pl.BlockSpec((parts, 1, 2 * height, count), lambda i, _: (0, i, 0, 0)),
             scratch_shapes=[pltpu.VMEM((depth, parts * count), jnp.bfloat16)],
         ),
-        out_shape=jax.ShapeDtypeStruct((steps * parts, 2 * height, count), jnp.bfloat16),
-        compiler_params=pltpu.CompilerParams(vmem_limit_bytes=24 * MIB),
-    )(core, rows, own, other)
-
-
-def handoff_kernel(capacity, grad_ref, input_ref, resid_ref, gain_ref, stat_ref, target_ref, out_ref):
-    width, count = grad_ref.shape
+        out_shape=jax.ShapeDtypeStruct((parts, steps, 2 * height, count), jnp.bfloat16),
+        compiler_params=pltpu.CompilerParams(vmem_limit_bytes=16 * MIB),
+    )(plane, rows, weights)
+    return result.reshape(parts * steps, 2 * height, count)
+
+
+def handoff_kernel(
+    capacity, early_ref, late_ref, input_ref, resid_ref, gain_ref, stat_ref, target_ref, out_ref
+):
+    width, count = input_ref.shape
+    fourth = width // 4
+    grad = jnp.concatenate(
+        [
+            early_ref[:fourth].astype(jnp.float32),
+            late_ref[:fourth].astype(jnp.float32),
+            early_ref[fourth:].astype(jnp.float32),
+            late_ref[fourth:].astype(jnp.float32),
+        ],
+        axis=0,
+    )
     stats = jnp.sum(stat_ref[...], axis=0)
     inverse = lax.rsqrt(stats[0:1] / D + NORM_EPS)
     factor = inverse * inverse * inverse * stats[1:2] / D
-    scaled = gain_ref[...] * grad_ref[...].astype(jnp.float32)
+    scaled = gain_ref[...] * grad
     handoff = (
         resid_ref[...].astype(jnp.float32)
         + inverse * scaled
@@ -141,17 +151,21 @@
 ):
     groups = lax.axis_size(DP)
     shares = lax.axis_size(TP)
-    side = lax.axis_size("zl")
+    side = lax.axis_size("zh")
     capacity = merge_pre.shape[0] // groups
     positions = img_pos[0]
     image_count = positions.shape[0]
     width = embeds.shape[1]
 
-    own = lax.all_gather(query_weight, "zh", axis=0)
+    half = query_weight.shape[0] // 2
+    weights = [
+        lax.all_gather(query_weight[:half], ("zl", "core"), axis=0),
+        lax.all_gather(query_weight[half:], ("zl", "core"), axis=0),
+    ]
     picked = jnp.take(grad_query, positions, axis=0, mode="clip")
-    picked = lax.all_gather(picked, "zl", axis=0)
-    merge_weight, slope, picked = lax.optimization_barrier(
-        (merge_weight, gelu_slope(merge_pre), picked)
+    picked = lax.all_gather(picked, "zh", axis=0)
+    merge_weight, slope, picked, weights[0] = lax.optimization_barrier(
+        (merge_weight, gelu_slope(merge_pre), picked, weights[0])
     )
     merge_full = lax.all_gather(merge_weight, DP, axis=0)
     inputs = jnp.take(embeds, positions, axis=0, mode="clip").T
@@ -169,14 +183,17 @@
     pitch = capacity * (width // LANES)
     target = jnp.where(is_live, target_dev * pitch + slot_index, -groups * pitch)
 
-    other = lax.ppermute(own, "core", [(0, 1), (1, 0)])
-    core = lax.axis_index("core").astype(jnp.int32)[None]
-    partial_value = query_products(core, picked, own, other)
-    swapped = lax.all_to_all(partial_value, TP, 0, 0, tiled=True)
-    normal_grad = jnp.sum(swapped.astype(jnp.float32), axis=0).astype(jnp.bfloat16)
-    exchange = [(b * side + a, a * side + b) for a in range(side) for b in range(side)]
-    normal_grad = lax.ppermute(normal_grad, ("zl", "y"), exchange)
-    inner = jnp.sum(gain * normal_grad.astype(jnp.float32) * wide, axis=0)
+    plane = lax.axis_index("zh").astype(jnp.int32)[None]
+    forth = [(h * side + (a + h) % side, a * side + h) for a in range(side) for h in range(side)]
+    scaled_input = (gain * wide).reshape(2, 2, half, image_count)
+    grads, inner = [], 0.0
+    for part in range(2):
+        sums = lax.all_to_all(query_products(plane, picked, weights[part]), TP, 0, 0, tiled=True)
+        grad = jnp.sum(sums.astype(jnp.float32), axis=0).astype(jnp.bfloat16)
+        grad = lax.ppermute(grad, ("zh", "x"), forth)
+        piece = grad.astype(jnp.float32).reshape(2, half, image_count)
+        inner += jnp.sum(piece * scaled_input[:, part], axis=(0, 1))
+        grads.append(grad)
     stats = jnp.stack([squares, inner])
     stats = lax.all_to_all(
         jnp.broadcast_to(stats[None], (shares,) + stats.shape), TP, 0, 0, tiled=True
@@ -185,7 +202,7 @@
         lambda *refs: handoff_kernel(capacity, *refs),
         out_shape=jax.ShapeDtypeStruct((groups * pitch, LANES), jnp.bfloat16),
         compiler_params=pltpu.CompilerParams(vmem_limit_bytes=24 * MIB),
-    )(normal_grad, inputs, residual, gain, stats, target[None])
+    )(*grads, inputs, residual, gain, stats, target[None])
     received = lax.all_to_all(outbox.reshape(groups, pitch, LANES), DP, 0, 0, tiled=True)
     partial_hidden = merge_products(
         received.reshape(groups * pitch, LANES), merge_full, capacity, shares, 4

time: 219 us -> 236 us (1.078)
  blocking collectives: 71.7 us -> 96.9 us
  waiting for transfers between devices: 86.4 us -> 61.7 us
  starting transfers between devices: 27.3 us -> 37.4 us
  local copies, waits for them, and re-layouts: 9.27 us -> 12.9 us
    all_to_all x1 -> x2, waiting for transfers between devices: 28.5 us -> 7.91 us  [local(): lax.all_to_all(query_products(plane, picked, weights[part]), TP, 0, 0, ti...]
    all_gather x1, blocking collectives: 16.3 us -> 31.3 us  [local(): picked = lax.all_gather(picked, 'zh', axis=0)]
    all_to_all x1, blocking collectives: 28.7 us -> 35.8 us  [local(): lax.all_to_all(outbox.reshape(groups, pitch, LANES), DP, 0, 0, tiled=True)]
    all_to_all x1 -> x2, starting transfers between devices: 5.4 us -> 12.3 us  [local(): lax.all_to_all(query_products(plane, picked, weights[part]), TP, 0, 0, ti...]
    all_to_all x1, starting transfers between devices: 17.5 us -> 23.7 us  [local(): lax.all_to_all(jnp.broadcast_to(stats[None], (shares,) + stats.shape), TP...]
    all_to_all x1, blocking collectives: 26.7 us -> 29.8 us  [local(): hidden = lax.all_to_all(partial_hidden, TP, 0, 0, tiled=True)]
    ppermute x2, starting transfers between devices: 4.36 us -> 1.33 us  [local(): grad = lax.ppermute(grad, ('zh', 'x'), forth)]
    ppermute x2, waiting for transfers between devices: 2.47 us -> 0.01 us  [local(): grad = lax.ppermute(grad, ('zh', 'x'), forth)]
  transfers between devices with their start and end apart: 6 -> 8, of which waited for: 4 -> 4; matrix products, arithmetic and copies ran while one was open for 3% -> 3% of each run, Pallas kernels for 2% -> 2%
where the time goes in v7:
time: 236 us; the launch traced here: 235 us
  blocking collectives  96.9 us (41%)
  waiting for transfers between devices  61.7 us (26%)
  starting transfers between devices  37.4 us (16%)
  between operations  14 us (6%)
  local copies, waits for them, and re-layouts  12.9 us (5%)
  Pallas kernels  8.6 us (4%)
  other arithmetic  3.14 us (1%)
    all_to_all x1, blocking collectives, local(): lax.all_to_all(outbox.reshape(groups, pitch, LANES), DP, 0, 0, tiled=True)  35.8 us
    all_gather x1, blocking collectives, local(): picked = lax.all_gather(picked, 'zh', axis=0)  31.3 us
    all_to_all x1, blocking collectives, local(): hidden = lax.all_to_all(partial_hidden, TP, 0, 0, tiled=True)  29.8 us
    all_gather x1, waiting for transfers between devices, local(): lax.all_gather(query_weight[half:], ('zl', 'core'), axis=0)  28.7 us
    all_to_all x1, starting transfers between devices, local(): lax.all_to_all(jnp.broadcast_to(stats[None], (shares,) + stats.shape), TP...  23.7 us
    all_gather x1, waiting for transfers between devices, local(): lax.all_gather(query_weight[:half], ('zl', 'core'), axis=0)  19 us
    all_to_all x2, starting transfers between devices, local(): lax.all_to_all(query_products(plane, picked, weights[part]), TP, 0, 0, ti...  12.3 us
    all_to_all x2, waiting for transfers between devices, local(): lax.all_to_all(query_products(plane, picked, weights[part]), TP, 0, 0, ti...  7.91 us
  transfers between devices with their start and end apart: 8, of which 4 were waited for; matrix products, arithmetic and copies ran while one was open for 3% of the time, Pallas kernels for 2%

profile of v7, /device:TPU:1, one launch (start us, length us, event | category | flops | bytes accessed | tf_op | source)
XLA Modules:
  0.0 234.6 jit_solution(2525749023526533812)
XLA Ops:
  6.5 0.0 copy-start
  6.5 0.0 all-gather.8.cloned.1.call-start
  6.5 1.7 fusion.12
  8.3 0.0 all-gather.8.cloned.1.call-update
  8.3 0.0 all-gather.10.cloned.1.call-start
  8.3 0.7 all-gather.10.cloned.1.call-update
  9.0 0.0 all-gather.12.cloned.1.call-start
  9.1 1.0 copy.16
  10.1 0.7 pad_clamp_fusion
  10.8 0.0 copy-done
  10.8 0.8 gather_fusion
  11.6 31.3 %all-gather = bf16[512,512]{1,0:T(8,128)(2,1)S(1)} all-gather(bf16[128,512]{1,0:T(8,128)(2,1)S(1)} %gather_fusion), channel_id=2, replica_groups=mesh['zh'=4,'zl'=4,'core'=2,'x'=4,'y'=4] {'zh'}, dimensions={0}, use_global_device_ids=true | all-gather | bytes 655360 | tf_op jit(solution)/shard_map/all_gather | solution.py:166
  43.0 0.1 fusion.3
  43.1 19.0 %all-gather.8.cloned.1.call-done = bf16[1024,512]{1,0:T(8,128)(2,1)} async-done(((bf16[128,512]{1,0:T(8,128)(2,1)}), bf16[1024,512]{1,0:T(8,128)(2,1)}) %all-gather.8.cloned.1.call-update) | async-done | bytes 1048592 | tf_op jit(solution)/shard_map/all_gather | solution.py:162
  62.1 0.0 all-gather.12.cloned.1.call-update
  62.1 0.0 copy-start.2
  62.2 1.2 copy-done.2
  63.4 2.6 %shard_map.100 = bf16[4,4,256,128]{3,2,1,0:T(8,128)(2,1)} custom-call(s32[1]{0:T(128)} %bitcast.plane_ref, bf16[4,128,512]{2,1,0:T(8,128)(2,1)S(1)} %bitcast.40, bf16[8,128,512]{2,1,0:T(8,128)(2,1)S(1)} %bitcast.43), custom_call_target="tpu_custom_call" | custom-call | tf_op jit(solution)/shard_map/pallas_call | solution.py:43
  66.0 6.6 %all-to-all-start = ((bf16[16,256,128]{2,1,0:T(8,128)(2,1)}), bf16[16,256,128]{2,1,0:T(8,128)(2,1)S(1)}, u32[]{:S(2)}, u32[]{:S(2)}) async-start(bf16[16,256,128]{2,1,0:T(8,128)(2,1)} %bitcast.4), calls=%async_computation | async-start | bytes 2097152 | tf_op jit(solution)/shard_map/all_to_all | solution.py:191
  72.6 28.7 %all-gather.10.cloned.1.call-done = bf16[1024,512]{1,0:T(8,128)(2,1)} async-done(((bf16[128,512]{1,0:T(8,128)(2,1)}), bf16[1024,512]{1,0:T(8,128)(2,1)}) %all-gather.10.cloned.1.call-update) | async-done | bytes 1048592 | tf_op jit(solution)/shard_map/all_gather | solution.py:163
  101.3 0.0 copy-start.3
  101.3 1.2 copy-done.3
  102.6 2.6 %shard_map.101 = bf16[4,4,256,128]{3,2,1,0:T(8,128)(2,1)} custom-call(s32[1]{0:T(128)} %bitcast.plane_ref, bf16[4,128,512]{2,1,0:T(8,128)(2,1)S(1)} %bitcast.41, bf16[8,128,512]{2,1,0:T(8,128)(2,1)S(1)} %bitcast.44), custom_call_target="tpu_custom_call" | custom-call | tf_op jit(solution)/shard_map/pallas_call | solution.py:43
  105.2 0.0 copy-start.8
  105.2 0.0 copy-start.7
  105.2 0.0 all-to-all-done
  105.2 5.7 %all-to-all-start.1 = ((bf16[16,256,128]{2,1,0:T(8,128)(2,1)}), bf16[16,256,128]{2,1,0:T(8,128)(2,1)S(1)}, u32[]{:S(2)}, u32[]{:S(2)}) async-start(bf16[16,256,128]{2,1,0:T(8,128)(2,1)} %bitcast.6), calls=%async_computation.1 | async-start | bytes 2097152 | tf_op jit(solution)/shard_map/all_to_all | solution.py:191
  110.8 0.0 copy-done.4
  110.8 0.8 gather_fusion.1
  111.7 0.1 copy.17
  111.8 0.0 copy-start.5
  112.5 0.0 copy-done.8
  112.5 0.1 fusion.10
  112.6 0.2 reduce_window_sum.11
  112.8 0.0 copy-done.7
  112.8 0.6 fusion.6
  113.4 0.7 fusion.11
  114.1 0.1 reduce_sum.71
  114.2 0.7 collective-permute-start
  114.9 0.2 select_reduce_fusion
  115.1 7.9 %all-to-all-done.1 = bf16[16,256,128]{2,1,0:T(8,128)(2,1)S(1)} async-done(((bf16[16,256,128]{2,1,0:T(8,128)(2,1)}), bf16[16,256,128]{2,1,0:T(8,128)(2,1)S(1)}, u32[]{:S(2)}, u32[]{:S(2)}) %all-to-all-start.1) | async-done | bytes 1048608 | tf_op jit(solution)/shard_map/all_to_all | solution.py:191
  123.0 0.1 reduce_sum.72
  123.1 0.7 collective-permute-start.1
  123.8 0.0 collective-permute-done.refs_0_
  123.8 0.0 copy-done.6
  123.8 0.1 fusion.8
  123.9 0.0 collective-permute-done.1.refs_1_
  123.9 0.1 fusion.7
  123.9 0.6 pad_maximum_fusion
  124.5 0.6 broadcast_in_dim.28
  125.1 23.7 %all-to-all-start.2 = ((f32[16,2,128]{2,1,0:T(2,128)}), f32[16,2,128]{2,1,0:T(2,128)S(1)}, u32[]{:S(2)}, u32[]{:S(2)}) async-start(f32[16,2,128]{2,1,0:T(2,128)} %broadcast_in_dim.28), calls=%async_computation.2 | async-start | bytes 32768 | tf_op jit(solution)/shard_map/all_to_all | solution.py:198
  148.9 0.0 copy-done.5
  148.9 0.8 gather_fusion.2
  149.7 0.1 copy.18
  149.9 0.1 copy.19.refs_4_
  150.0 5.3 %all-to-all-done.2.refs_5_ = f32[16,2,128]{2,1,0:T(2,128)S(1)} async-done(((f32[16,2,128]{2,1,0:T(2,128)}), f32[16,2,128]{2,1,0:T(2,128)S(1)}, u32[]{:S(2)}, u32[]{:S(2)}) %all-to-all-start.2) | async-done | bytes 16416 | tf_op jit(solution)/shard_map/all_to_all | solution.py:198
  155.3 0.5 shard_map.102
  155.8 35.8 %all_to_all.25 = bf16[32,24,128]{2,1,0:T(8,128)(2,1)S(1)} all-to-all(bf16[32,24,128]{2,1,0:T(8,128)(2,1)S(1)} %bitcast.45), channel_id=1, replica_groups=mesh['zh'=4,'zl'=4,'core'=2,'x'=4,'y'=4] {'zh','zl','core'}, dimensions={0} | all-to-all | bytes 393216 | tf_op jit(solution)/shard_map/all_to_all | solution.py:206
  191.6 2.5 %copy-done.1 = bf16[5120,512]{1,0:T(8,128)(2,1)S(1)} copy-done((bf16[5120,512]{1,0:T(8,128)(2,1)S(1)}, bf16[5120,512]{1,0:T(8,128)(2,1)}, u32[]{:S(2)}) %copy-start.1) | copy-done | bytes 5242904
  194.1 2.9 %shard_map.103 = bf16[16,160,384]{2,1,0:T(8,128)(2,1)S(1)} custom-call(bf16[768,128]{1,0:T(8,128)(2,1)S(1)} %bitcast.46, bf16[32,160,512]{2,1,0:T(8,128)(2,1)S(1)} %bitcast.39), custom_call_target="tpu_custom_call" | custom-call | tf_op jit(solution)/shard_map/pallas_call | solution.py:126
  197.0 29.8 %all_to_all.26 = bf16[16,160,384]{2,1,0:T(8,128)(2,1)S(1)} all-to-all(bf16[16,160,384]{2,1,0:T(8,128)(2,1)S(1)} %shard_map.103), channel_id=1, replica_groups=mesh['zh'=4,'zl'=4,'core'=2,'x'=4,'y'=4] {'x','y'}, dimensions={0} | all-to-all | bytes 3932160 | tf_op jit(solution)/shard_map/all_to_all | solution.py:210
  226.8 0.3 convert_reduce_fusion
  227.1 0.1 slice_bitcast_fusion.1
  227.2 0.9 copy.20
  (8 shorter events, 0.1 us)
Async XLA Ops:
  6.5 4.2 %copy-start = (bf16[256,512]{1,0:T(8,128)(2,1)S(1)}, bf16[256,512]{1,0:T(8,128)(2,1)}, u32[]{:S(2)}) copy-start(bf16[256,512]{1,0:T(8,128)(2,1)} %param.10) | copy-start | bytes 786436
  6.5 55.6 %all-gather.8.cloned.1.call-start = ((), (), s32[]{:S(2)}) async-start(), calls=%async_computation.5 | async-start | bytes 1179648 | tf_op jit(solution)/shard_map/all_gather | solution.py:162
  8.3 93.1 %all-gather.10.cloned.1.call-start = ((), (), s32[]{:S(2)}) async-start(), calls=%async_computation.6 | async-start | bytes 1179648 | tf_op jit(solution)/shard_map/all_gather | solution.py:163
  9.0 182.6 %all-gather.12.cloned.1.call-start = ((), (), s32[]{:S(2)}) async-start(), calls=%async_computation.7 | async-start | bytes 5406720 | tf_op jit(solution)/shard_map/all_gather | solution.py:170
  62.1 1.2 copy-start.2
  66.0 39.2 %all-to-all-start = ((bf16[16,256,128]{2,1,0:T(8,128)(2,1)}), bf16[16,256,128]{2,1,0:T(8,128)(2,1)S(1)}, u32[]{:S(2)}, u32[]{:S(2)}) async-start(bf16[16,256,128]{2,1,0:T(8,128)(2,1)} %bitcast.4), calls=%async_computation | async-start | bytes 2097152 | tf_op jit(solution)/shard_map/all_to_all | solution.py:191
  101.3 1.2 copy-start.3
  102.6 8.3 %copy-start.4 = (bf16[256,512]{1,0:T(8,128)(2,1)S(1)}, bf16[256,512]{1,0:T(8,128)(2,1)}, u32[]{:S(2)}) copy-start(bf16[256,512]{1,0:T(8,128)(2,1)} %param.13) | copy-start | bytes 786436
  105.2 7.4 %copy-start.8 = (s32[1,128]{1,0:T(1,128)S(1)}, s32[1,128]{1,0:T(1,128)}, u32[]{:S(2)}) copy-start(s32[1,128]{1,0:T(1,128)} %param.17) | copy-start | bytes 1540
  105.2 7.7 %copy-start.7 = (f32[512]{0:T(512)S(1)}, f32[512]{0:T(512)}, u32[]{:S(2)}) copy-start(f32[512]{0:T(512)} %param.14) | copy-start | bytes 6148
  105.2 17.8 %all-to-all-start.1 = ((bf16[16,256,128]{2,1,0:T(8,128)(2,1)}), bf16[16,256,128]{2,1,0:T(8,128)(2,1)S(1)}, u32[]{:S(2)}, u32[]{:S(2)}) async-start(bf16[16,256,128]{2,1,0:T(8,128)(2,1)} %bitcast.6), calls=%async_computation.1 | async-start | bytes 2097152 | tf_op jit(solution)/shard_map/all_to_all | solution.py:191
  111.8 37.1 %copy-start.5 = (bf16[256,512]{1,0:T(8,128)(2,1)S(1)}, bf16[256,512]{1,0:T(8,128)(2,1)}, u32[]{:S(2)}) copy-start(bf16[256,512]{1,0:T(8,128)(2,1)} %param.12) | copy-start | bytes 786436
  114.1 9.7 %copy-start.6 = (f32[2,1,128,128]{3,2,1,0:T(8,128)S(1)}, f32[2,1,128,128]{3,2,1,0:T(8,128)}, u32[]{:S(2)}) copy-start(f32[2,1,128,128]{3,2,1,0:T(8,128)} %get-tuple-element.14) | copy-start | bytes 393220
  114.2 9.6 %collective-permute-start = (bf16[256,128]{1,0:T(8,128)(2,1)S(1)}, bf16[256,128]{1,0:T(8,128)(2,1)S(1)}, u32[]{:S(2)}, u32[]{:S(2)}) collective-permute-start(bf16[256,128]{1,0:T(8,128)(2,1)S(1)} %reduce_sum.71), channel_id=1, source_target_pairs={{0,0},{132,4},{264,8},{396,12},{4,128},{136,132},{268,136},{384,14... | collective-permute-start | bytes 196616 | tf_op jit(solution)/shard_map/ppermute | solution.py:193
  123.1 0.7 collective-permute-start.1
  125.1 30.2 %all-to-all-start.2 = ((f32[16,2,128]{2,1,0:T(2,128)}), f32[16,2,128]{2,1,0:T(2,128)S(1)}, u32[]{:S(2)}, u32[]{:S(2)}) async-start(f32[16,2,128]{2,1,0:T(2,128)} %broadcast_in_dim.28), calls=%async_computation.2 | async-start | bytes 32768 | tf_op jit(solution)/shard_map/all_to_all | solution.py:198
  191.6 2.5 %copy-start.1 = (bf16[5120,512]{1,0:T(8,128)(2,1)S(1)}, bf16[5120,512]{1,0:T(8,128)(2,1)}, u32[]{:S(2)}) copy-start(bf16[5120,512]{1,0:T(8,128)(2,1)} %all-gather.12.cloned.1.call-done) | copy-start | bytes 15728644
Sparse Core Ops, SparseCore 0:
  9.4 52.6 all-gather.7
  64.2 37.0 all-gather.9
  103.5 82.8 all-gather.11

commit v8 on v4

--- a/solution.py
+++ b/solution.py
@@ -57,7 +57,7 @@
             scratch_shapes=[pltpu.VMEM((depth, parts * count), jnp.bfloat16)],
         ),
         out_shape=jax.ShapeDtypeStruct((parts, steps, 2 * height, count), jnp.bfloat16),
-        compiler_params=pltpu.CompilerParams(vmem_limit_bytes=56 * MIB),
+        compiler_params=pltpu.CompilerParams(vmem_limit_bytes=24 * MIB),
     )(place, rows, own, other)
 
 
@@ -98,7 +98,7 @@
         out_specs=pl.BlockSpec((shares // steps, height, 2 * count), lambda i: (i, 0, 0)),
         out_shape=jax.ShapeDtypeStruct((shares, height, 2 * count), jnp.bfloat16),
         scratch_shapes=[pltpu.VMEM((width, count), jnp.bfloat16)],
-        compiler_params=pltpu.CompilerParams(vmem_limit_bytes=56 * MIB),
+        compiler_params=pltpu.CompilerParams(vmem_limit_bytes=24 * MIB),
     )(*whole, weights)
 
 
@@ -181,7 +181,7 @@
         jnp.broadcast_to(stats[None], (shares,) + stats.shape), TP, 0, 0, tiled=True
     )
     partial_hidden = merge_products(
-        normal_grad, inputs, residual, gain, stats, merge_full, shares, 8
+        normal_grad, inputs, residual, gain, stats, merge_full, shares, 4
     )
     hidden = lax.all_to_all(partial_hidden, TP, 0, 0, tiled=True)
     lanes = -(-columns // LANES) * LANES

time: 213 us -> 210 us (0.986)
  Pallas kernels: 15.3 us -> 7.88 us
  waiting for transfers between devices: 61 us -> 66.3 us
    pallas_call x1, Pallas kernels: 7.58 us -> 3.09 us  [merge_products(): pl.pallas_call(merge_kernel, grid=(steps,), in_specs=[pl.BlockSpec(a.shap...]
    pallas_call x1, Pallas kernels: 5.7 us -> 2.79 us  [query_products(): pl.pallas_call(query_kernel, grid_spec=pltpu.PrefetchScalarGridSpec(num_s...]
    all_gather x1, waiting for transfers between devices: 0.29 us -> 3.12 us  [local(): merge_full = lax.all_gather(merge_weight, DP, axis=0)]
    unnamed x20 -> x16, local copies, waits for them, and re-layouts: 1.4 us -> 3.73 us
  transfers between devices with their start and end apart: 7 -> 7, of which waited for: 6 -> 6; matrix products, arithmetic and copies ran while one was open for 3% -> 3% of each run, Pallas kernels for 3% -> 1%
where the time goes in v8:
time: 210 us; the launch traced here: 209 us
  waiting for transfers between devices  66.3 us (32%)
  blocking collectives  65 us (31%)
  starting transfers between devices  46.9 us (22%)
  between operations  14.2 us (7%)
  Pallas kernels  7.88 us (4%)
  local copies, waits for them, and re-layouts  7.28 us (3%)
    all_to_all x1, blocking collectives, local(): swapped = lax.all_to_all(partial_value, TP, 0, 0, tiled=True)  33.8 us
    all_gather x1, blocking collectives, local(): lax.all_gather(jnp.take(grad_query, positions, axis=0, mode='clip'), 'zh'...  31.2 us
    all_to_all x1, starting transfers between devices, local(): lax.all_to_all(jnp.broadcast_to(stats[None], (shares,) + stats.shape), TP...  22.9 us
    all_to_all x1, waiting for transfers between devices, local(): lax.all_to_all(outbox.reshape(groups, SLOT_PITCH, lanes), DP, 0, 0, tiled...  18.4 us
    all_gather x1, waiting for transfers between devices, local(): own = lax.all_gather(query_weight, 'zl', axis=0)  18.4 us
    all_to_all x1, waiting for transfers between devices, local(): hidden = lax.all_to_all(partial_hidden, TP, 0, 0, tiled=True)  17.9 us
    all_to_all x1, starting transfers between devices, local(): hidden = lax.all_to_all(partial_hidden, TP, 0, 0, tiled=True)  10.8 us
    all_to_all x1, starting transfers between devices, local(): lax.all_to_all(outbox.reshape(groups, SLOT_PITCH, lanes), DP, 0, 0, tiled...  10 us
  transfers between devices with their start and end apart: 7, of which 6 were waited for; matrix products, arithmetic and copies ran while one was open for 3% of the time, Pallas kernels for 1%

profile of v8, /device:TPU:1, one launch (start us, length us, event | category | flops | bytes accessed | tf_op | source)
XLA Modules:
  0.0 209.3 jit_solution(3111827034893118267)
XLA Ops:
  6.5 0.0 copy-start
  6.5 0.0 all-gather.6.cloned.1.call-start
  6.5 0.7 all-gather.6.cloned.1.call-update
  7.3 0.0 all-gather.8.cloned.1.call-start
  7.3 0.7 pad_clamp_fusion
  8.0 0.0 copy-done
  8.0 0.8 gather_fusion
  8.8 31.2 %all-gather = bf16[512,512]{1,0:T(8,128)(2,1)S(1)} all-gather(bf16[128,512]{1,0:T(8,128)(2,1)S(1)} %gather_fusion), channel_id=2, replica_groups=mesh['zh'=4,'zl'=4,'core'=2,'x'=4,'y'=4] {'zh'}, dimensions={0}, use_global_device_ids=true | all-gather | bytes 655360 | tf_op jit(solution)/shard_map/all_gather | solution.py:148
  40.0 0.0 all-gather.8.cloned.1.call-update
  40.0 18.4 %all-gather.6.cloned.1.call-done = bf16[1024,512]{1,0:T(8,128)(2,1)} async-done(((bf16[256,512]{1,0:T(8,128)(2,1)}), bf16[1024,512]{1,0:T(8,128)(2,1)}) %all-gather.6.cloned.1.call-update) | async-done | bytes 1048592 | tf_op jit(solution)/shard_map/all_gather | solution.py:147
  58.4 2.5 %collective-permute-start = (bf16[4,256,512]{2,1,0:T(8,128)(2,1)}, bf16[4,256,512]{2,1,0:T(8,128)(2,1)S(1)}, u32[]{:S(2)}, u32[]{:S(2)}) collective-permute-start(bf16[4,256,512]{2,1,0:T(8,128)(2,1)} %bitcast.28), channel_id=1, source_target_pairs={{0,16},{16,0},{1,17},{17,1},{2,18},{18,2},{3,19},{19,3},{4,20},{20... | collective-permute-start | bytes 3145736 | tf_op jit(solution)/shard_map/ppermute | solution.py:168
  60.9 0.1 pad_add_fusion.place_ref
  61.0 2.4 %collective-permute-done.other_ref = bf16[4,256,512]{2,1,0:T(8,128)(2,1)S(1)} collective-permute-done((bf16[4,256,512]{2,1,0:T(8,128)(2,1)}, bf16[4,256,512]{2,1,0:T(8,128)(2,1)S(1)}, u32[]{:S(2)}, u32[]{:S(2)}) %collective-permute-start) | collective-permute-done | bytes 1048608 | tf_op jit(solution)/shard_map/ppermute | solution.py:168
  63.4 0.0 copy-start.2
  63.4 1.2 copy-done.2
  64.6 2.8 %shard_map.100 = bf16[4,4,512,128]{3,2,1,0:T(8,128)(2,1)S(1)} custom-call(s32[2]{0:T(128)S(1)} %pad_add_fusion.place_ref, bf16[4,128,512]{2,1,0:T(8,128)(2,1)S(1)} %bitcast.26, bf16[4,256,512]{2,1,0:T(8,128)(2,1)S(1)} %bitcast.29, bf16[4,256,512]{2,1,0:T(8,128)(2,1)S(1)} %collective-permute-done.other_ref), custom_call_target="tpu_custom_call" | custom-call | tf_op jit(solution)/shard_map/pallas_call | solution.py:46
  67.4 33.8 %all_to_all.20 = bf16[16,512,128]{2,1,0:T(8,128)(2,1)S(1)} all-to-all(bf16[16,512,128]{2,1,0:T(8,128)(2,1)S(1)} %bitcast.24), channel_id=1, replica_groups=mesh['zh'=4,'zl'=4,'core'=2,'x'=4,'y'=4] {'x','y'}, dimensions={0} | all-to-all | bytes 4194304 | tf_op jit(solution)/shard_map/all_to_all | solution.py:172
  101.2 0.0 copy-start.3
  101.2 0.0 copy-start.6
  101.2 0.0 copy-start.4
  101.2 0.3 reduce_sum.41
  101.5 0.7 collective-permute-start.1
  102.1 0.0 copy-done.3
  102.2 0.8 gather_fusion.1
  103.0 0.1 copy.13
  103.1 0.0 collective-permute-done.1.grad_ref
  103.1 0.0 copy-done.6
  103.1 0.2 fusion.6
  103.3 0.6 broadcast_in_dim.25
  103.9 22.9 %all-to-all-start.1 = ((f32[16,2,128]{2,1,0:T(2,128)}), f32[16,2,128]{2,1,0:T(2,128)S(1)}, u32[]{:S(2)}, u32[]{:S(2)}) async-start(f32[16,2,128]{2,1,0:T(2,128)} %broadcast_in_dim.25), calls=%async_computation.1 | async-start | bytes 32768 | tf_op jit(solution)/shard_map/all_to_all | solution.py:180
  126.9 0.0 copy-done.4
  126.9 0.8 gather_fusion.2
  127.7 0.1 copy.14
  127.9 0.1 copy.15.gain_ref
  128.0 5.3 %all-to-all-done.1.stat_ref = f32[16,2,128]{2,1,0:T(2,128)S(1)} async-done(((f32[16,2,128]{2,1,0:T(2,128)}), f32[16,2,128]{2,1,0:T(2,128)S(1)}, u32[]{:S(2)}, u32[]{:S(2)}) %all-to-all-start.1) | async-done | bytes 16416 | tf_op jit(solution)/shard_map/all_to_all | solution.py:180
  133.3 3.1 %all-gather.8.cloned.1.call-done = bf16[5120,512]{1,0:T(8,128)(2,1)} async-done(((bf16[160,512]{1,0:T(8,128)(2,1)}), bf16[5120,512]{1,0:T(8,128)(2,1)}) %all-gather.8.cloned.1.call-update) | async-done | bytes 5242896 | tf_op jit(solution)/shard_map/all_gather | solution.py:150
  136.5 0.0 copy-start.1
  136.5 2.5 %copy-done.1 = bf16[5120,512]{1,0:T(8,128)(2,1)S(1)} copy-done((bf16[5120,512]{1,0:T(8,128)(2,1)S(1)}, bf16[5120,512]{1,0:T(8,128)(2,1)}, u32[]{:S(2)}) %copy-start.1) | copy-done | bytes 5242904
  138.9 3.1 %shard_map.101 = bf16[16,160,256]{2,1,0:T(8,128)(2,1)} custom-call(bf16[512,128]{1,0:T(8,128)(2,1)S(1)} %collective-permute-done.1.grad_ref, bf16[512,128]{1,0:T(8,128)(2,1)S(1)} %bitcast.27, bf16[512,128]{1,0:T(8,128)(2,1)S(1)} %bitcast.31, f32[512,1]{1,0:T(8,128)S(1)} %copy.15.gain_ref, f32[16,2,128]{2,1,0:T(2,128)S(1)} %all-to-all-done.1.stat_ref, ...), custom_call_target="tpu_custom_call" | custom-call | tf_op jit(solution)/shard_map/pallas_call | solution.py:91
  142.0 0.0 copy-start.7
  142.0 0.0 copy-start.5
  142.0 10.8 %all-to-all-start.2 = ((bf16[16,160,256]{2,1,0:T(8,128)(2,1)}), bf16[16,160,256]{2,1,0:T(8,128)(2,1)S(1)}, u32[]{:S(2)}, u32[]{:S(2)}) async-start(bf16[16,160,256]{2,1,0:T(8,128)(2,1)} %shard_map.101), calls=%async_computation.2 | async-start | bytes 2621440 | tf_op jit(solution)/shard_map/all_to_all | solution.py:186
  153.5 0.0 copy-done.7
  153.5 0.1 fusion.18
  153.6 0.2 reduce_window_sum.11
  153.7 0.2 select_reduce_fusion
  153.9 17.9 %all-to-all-done.2.hidden_ref = bf16[16,160,256]{2,1,0:T(8,128)(2,1)S(1)} async-done(((bf16[16,160,256]{2,1,0:T(8,128)(2,1)}), bf16[16,160,256]{2,1,0:T(8,128)(2,1)S(1)}, u32[]{:S(2)}, u32[]{:S(2)}) %all-to-all-start.2) | async-done | bytes 1310752 | tf_op jit(solution)/shard_map/all_to_all | solution.py:186
  171.8 1.0 shard_map.102
  172.9 10.0 %all-to-all-start.3 = ((bf16[32,8,384]{2,1,0:T(8,128)(2,1)}), bf16[32,8,384]{2,1,0:T(8,128)(2,1)S(1)}, u32[]{:S(2)}, u32[]{:S(2)}) async-start(bf16[32,8,384]{2,1,0:T(8,128)(2,1)} %bitcast.15), calls=%async_computation.3 | async-start | bytes 393216 | tf_op jit(solution)/shard_map/all_to_all | solution.py:193
  183.0 0.0 copy-done.5
  183.0 0.1 fusion.3.slope_ref
  183.1 18.4 %all-to-all-done.3 = bf16[32,8,384]{2,1,0:T(8,128)(2,1)S(1)} async-done(((bf16[32,8,384]{2,1,0:T(8,128)(2,1)}), bf16[32,8,384]{2,1,0:T(8,128)(2,1)S(1)}, u32[]{:S(2)}, u32[]{:S(2)}) %all-to-all-start.3) | async-done | bytes 196640 | tf_op jit(solution)/shard_map/all_to_all | solution.py:193
  201.5 1.0 shard_map.103
  (4 shorter events, 0.1 us)
Async XLA Ops:
  6.5 1.4 copy-start
  6.5 51.9 %all-gather.6.cloned.1.call-start = ((), (), s32[]{:S(2)}) async-start(), calls=%async_computation.4 | async-start | bytes 1310720 | tf_op jit(solution)/shard_map/all_gather | solution.py:147
  7.3 129.2 %all-gather.8.cloned.1.call-start = ((), (), s32[]{:S(2)}) async-start(), calls=%async_computation.5 | async-start | bytes 5406720 | tf_op jit(solution)/shard_map/all_gather | solution.py:150
  58.4 4.9 %collective-permute-start = (bf16[4,256,512]{2,1,0:T(8,128)(2,1)}, bf16[4,256,512]{2,1,0:T(8,128)(2,1)S(1)}, u32[]{:S(2)}, u32[]{:S(2)}) collective-permute-start(bf16[4,256,512]{2,1,0:T(8,128)(2,1)} %bitcast.28), channel_id=1, source_target_pairs={{0,16},{16,0},{1,17},{17,1},{2,18},{18,2},{3,19},{19,3},{4,20},{20... | collective-permute-start | bytes 3145736 | tf_op jit(solution)/shard_map/ppermute | solution.py:168
  63.4 1.2 copy-start.2
  101.2 1.0 copy-start.3
  101.2 2.0 copy-start.6
  101.2 25.7 %copy-start.4 = (bf16[256,512]{1,0:T(8,128)(2,1)S(1)}, bf16[256,512]{1,0:T(8,128)(2,1)}, u32[]{:S(2)}) copy-start(bf16[256,512]{1,0:T(8,128)(2,1)} %param.12) | copy-start | bytes 786436
  101.5 1.7 collective-permute-start.1
  103.9 29.4 %all-to-all-start.1 = ((f32[16,2,128]{2,1,0:T(2,128)}), f32[16,2,128]{2,1,0:T(2,128)S(1)}, u32[]{:S(2)}, u32[]{:S(2)}) async-start(f32[16,2,128]{2,1,0:T(2,128)} %broadcast_in_dim.25), calls=%async_computation.1 | async-start | bytes 32768 | tf_op jit(solution)/shard_map/all_to_all | solution.py:180
  136.5 2.5 %copy-start.1 = (bf16[5120,512]{1,0:T(8,128)(2,1)S(1)}, bf16[5120,512]{1,0:T(8,128)(2,1)}, u32[]{:S(2)}) copy-start(bf16[5120,512]{1,0:T(8,128)(2,1)} %all-gather.8.cloned.1.call-done) | copy-start | bytes 15728644
  142.0 11.4 %copy-start.7 = (s32[1,128]{1,0:T(1,128)S(1)}, s32[1,128]{1,0:T(1,128)}, u32[]{:S(2)}) copy-start(s32[1,128]{1,0:T(1,128)} %param.17) | copy-start | bytes 1540
  142.0 40.9 %copy-start.5 = (bf16[192,320]{1,0:T(8,128)(2,1)S(1)}, bf16[192,320]{1,0:T(8,128)(2,1)}, u32[]{:S(2)}) copy-start(bf16[192,320]{1,0:T(8,128)(2,1)} %param.19) | copy-start | bytes 368644
  142.0 29.8 %all-to-all-start.2 = ((bf16[16,160,256]{2,1,0:T(8,128)(2,1)}), bf16[16,160,256]{2,1,0:T(8,128)(2,1)S(1)}, u32[]{:S(2)}, u32[]{:S(2)}) async-start(bf16[16,160,256]{2,1,0:T(8,128)(2,1)} %shard_map.101), calls=%async_computation.2 | async-start | bytes 2621440 | tf_op jit(solution)/shard_map/all_to_all | solution.py:186
  172.9 28.7 %all-to-all-start.3 = ((bf16[32,8,384]{2,1,0:T(8,128)(2,1)}), bf16[32,8,384]{2,1,0:T(8,128)(2,1)S(1)}, u32[]{:S(2)}, u32[]{:S(2)}) async-start(bf16[32,8,384]{2,1,0:T(8,128)(2,1)} %bitcast.15), calls=%async_computation.3 | async-start | bytes 393216 | tf_op jit(solution)/shard_map/all_to_all | solution.py:193
Sparse Core Ops, SparseCore 0:
  9.5 48.9 all-gather.5
  60.6 75.8 all-gather.7

commit v9 on v8

--- a/solution.py
+++ b/solution.py
@@ -11,6 +11,7 @@
 MIB = 1024 * 1024
 LANES = 128
 SLOT_PITCH = 8
+COPIES = 8
 DP = ("zh", "zl", "core")
 TP = ("x", "y")
 
@@ -61,45 +62,56 @@
     )(place, rows, own, other)
 
 
-def merge_kernel(grad_ref, input_ref, resid_ref, gain_ref, stat_ref, weight_ref, out_ref, handoff):
+def merge_kernel(
+    grad_ref, input_ref, resid_ref, gain_ref, stat_ref, weight_ref, out_ref, handoff, held, sems
+):
     count = grad_ref.shape[1]
-
-    @pl.when(pl.program_id(0) == 0)
-    def _():
-        stats = jnp.sum(stat_ref[...], axis=0)
-        inverse = lax.rsqrt(stats[0:1] / D + NORM_EPS)
-        factor = inverse * inverse * inverse * stats[1:2] / D
-        scaled = gain_ref[...] * grad_ref[...].astype(jnp.float32)
-        handoff[...] = (
-            resid_ref[...].astype(jnp.float32)
-            + inverse * scaled
-            - input_ref[...].astype(jnp.float32) * factor
-        ).astype(jnp.bfloat16)
-
-    for part in range(out_ref.shape[0]):
-        for half in range(2):
-            product = jnp.dot(
-                weight_ref[2 * part + half], handoff[...], preferred_element_type=jnp.float32
-            )
-            out_ref[part, :, half * count : (half + 1) * count] = product.astype(out_ref.dtype)
-
-
-def merge_products(grad, inputs, residual, gain, stats, weights, shares, steps):
+    blocks, height, width = held.shape
+    step = blocks // COPIES
+
+    def copy(number):
+        spot = pl.ds(number * step, step)
+        return pltpu.make_async_copy(weight_ref.at[spot], held.at[spot], sems.at[number])
+
+    for number in range(COPIES):
+        copy(number).start()
+    stats = jnp.sum(stat_ref[...], axis=0)
+    inverse = lax.rsqrt(stats[0:1] / D + NORM_EPS)
+    factor = inverse * inverse * inverse * stats[1:2] / D
+    scaled = gain_ref[...] * grad_ref[...].astype(jnp.float32)
+    handoff[...] = (
+        resid_ref[...].astype(jnp.float32)
+        + inverse * scaled
+        - input_ref[...].astype(jnp.float32) * factor
+    ).astype(jnp.bfloat16)
+    for number in range(COPIES):
+        copy(number).wait()
+        weight = held[number * step : (number + 1) * step].reshape(step * height, width)
+        product = jnp.dot(weight, handoff[...], preferred_element_type=jnp.float32)
+        product = product.astype(out_ref.dtype)
+        for block in range(step):
+            share, half = divmod(number * step + block, 2)
+            out_ref[share, :, half * count : (half + 1) * count] = product[
+                block * height : (block + 1) * height
+            ]
+
+
+def merge_products(grad, inputs, residual, gain, stats, weights, shares):
     blocks, height, width = weights.shape
     count = grad.shape[1]
-    whole = [grad, inputs, residual, gain, stats]
+    local_spec = pl.BlockSpec(memory_space=pltpu.VMEM)
     return pl.pallas_call(
         merge_kernel,
-        grid=(steps,),
-        in_specs=[
-            pl.BlockSpec(a.shape, lambda i, rank=a.ndim: (0,) * rank) for a in whole
-        ]
-        + [pl.BlockSpec((blocks // steps, height, width), lambda i: (i, 0, 0))],
-        out_specs=pl.BlockSpec((shares // steps, height, 2 * count), lambda i: (i, 0, 0)),
+        in_specs=[local_spec] * 5 + [pl.BlockSpec(memory_space=pl.ANY)],
+        out_specs=local_spec,
         out_shape=jax.ShapeDtypeStruct((shares, height, 2 * count), jnp.bfloat16),
-        scratch_shapes=[pltpu.VMEM((width, count), jnp.bfloat16)],
-        compiler_params=pltpu.CompilerParams(vmem_limit_bytes=24 * MIB),
-    )(*whole, weights)
+        scratch_shapes=[
+            pltpu.VMEM((width, count), jnp.bfloat16),
+            pltpu.VMEM((blocks, height, width), jnp.bfloat16),
+            pltpu.SemaphoreType.DMA((COPIES,)),
+        ],
+        compiler_params=pltpu.CompilerParams(vmem_limit_bytes=56 * MIB),
+    )(grad, inputs, residual, gain, stats, weights)
 
 
 def send_kernel(hidden_ref, target_ref, out_ref):
@@ -145,9 +157,7 @@
     image_count = positions.shape[0]
 
     own = lax.all_gather(query_weight, "zl", axis=0)
-    picked = lax.all_gather(jnp.take(grad_query, positions, axis=0, mode="clip"), "zh", axis=0)
-    merge_weight, picked = lax.optimization_barrier((merge_weight, picked))
-    merge_full = lax.all_gather(merge_weight, DP, axis=0)
+    picked = jnp.take(grad_query, positions, axis=0, mode="clip")
     inputs = jnp.take(embeds, positions, axis=0, mode="clip").T
     residual = jnp.take(grad_resid, positions, axis=0, mode="clip").T
     gain = norm_gain[:, None]
@@ -164,6 +174,13 @@
     number = jnp.arange(rows, dtype=jnp.int32)
     spot = number // capacity * SLOT_PITCH + number % capacity
     slope = gelu_slope(merge_pre)
+    picked, inputs, residual, squares, target, slope = lax.optimization_barrier(
+        (picked, inputs, residual, squares, target, slope)
+    )
+    wide = inputs.astype(jnp.float32)
+    picked = lax.all_gather(picked, "zh", axis=0)
+    merge_weight, picked = lax.optimization_barrier((merge_weight, picked))
+    merge_full = lax.all_gather(merge_weight, DP, axis=0)
 
     other = lax.ppermute(own, "core", [(0, 1), (1, 0)])
     place = jnp.stack([lax.axis_index("core"), lax.axis_index("zh")]).astype(jnp.int32)
@@ -180,9 +197,7 @@
     stats = lax.all_to_all(
         jnp.broadcast_to(stats[None], (shares,) + stats.shape), TP, 0, 0, tiled=True
     )
-    partial_hidden = merge_products(
-        normal_grad, inputs, residual, gain, stats, merge_full, shares, 4
-    )
+    partial_hidden = merge_products(normal_grad, inputs, residual, gain, stats, merge_full, shares)
     hidden = lax.all_to_all(partial_hidden, TP, 0, 0, tiled=True)
     lanes = -(-columns // LANES) * LANES
     outbox = pl.pallas_call(

time: 210 us -> 214 us (1.019)
  blocking collectives: 65 us -> 96.4 us
  waiting for transfers between devices: 66.3 us -> 47.8 us
  starting transfers between devices: 46.9 us -> 35 us
  Pallas kernels: 7.88 us -> 12.1 us
    all_to_all x0 -> x1, blocking collectives: none -> 30.6 us  [local(): hidden = lax.all_to_all(partial_hidden, TP, 0, 0, tiled=True)]
    all_to_all x1 -> x0, waiting for transfers between devices: 17.9 us -> none  [local(): hidden = lax.all_to_all(partial_hidden, TP, 0, 0, tiled=True)]
    all_to_all x1 -> x0, starting transfers between devices: 10.8 us -> none  [local(): hidden = lax.all_to_all(partial_hidden, TP, 0, 0, tiled=True)]
    pallas_call x1, Pallas kernels: 3.09 us -> 7.28 us  [merge_products(): pl.pallas_call(merge_kernel, in_specs=[local_spec] * 5 + [pl.BlockSpec(me...]
    unnamed x16 -> x20, local copies, waits for them, and re-layouts: 3.73 us -> 1.26 us
  transfers between devices with their start and end apart: 7 -> 6, of which waited for: 6 -> 5; matrix products, arithmetic and copies ran while one was open for 3% -> 3% of each run, Pallas kernels for 1% -> 1%
where the time goes in v9:
time: 214 us
  blocking collectives  96.4 us (45%)
  waiting for transfers between devices  47.8 us (22%)
  starting transfers between devices  35 us (16%)
  between operations  14.2 us (7%)
  Pallas kernels  12.1 us (6%)
  local copies, waits for them, and re-layouts  6.14 us (3%)
    all_to_all x1, blocking collectives, local(): swapped = lax.all_to_all(partial_value, TP, 0, 0, tiled=True)  33.8 us
    all_gather x1, blocking collectives, local(): picked = lax.all_gather(picked, 'zh', axis=0)  32 us
    all_to_all x1, blocking collectives, local(): hidden = lax.all_to_all(partial_hidden, TP, 0, 0, tiled=True)  30.6 us
    all_to_all x1, starting transfers between devices, local(): lax.all_to_all(jnp.broadcast_to(stats[None], (shares,) + stats.shape), TP...  23.1 us
    all_to_all x1, waiting for transfers between devices, local(): lax.all_to_all(outbox.reshape(groups, SLOT_PITCH, lanes), DP, 0, 0, tiled...  18.6 us
    all_gather x1, waiting for transfers between devices, local(): own = lax.all_gather(query_weight, 'zl', axis=0)  17.6 us
    all_to_all x1, starting transfers between devices, local(): lax.all_to_all(outbox.reshape(groups, SLOT_PITCH, lanes), DP, 0, 0, tiled...  8.77 us
    pallas_call x1, Pallas kernels, merge_products(): pl.pallas_call(merge_kernel, in_specs=[local_spec] * 5 + [pl.BlockSpec(me...  7.28 us
  transfers between devices with their start and end apart: 6, of which 5 were waited for; matrix products, arithmetic and copies ran while one was open for 3% of the time, Pallas kernels for 1%

profile of v9, /device:TPU:1, one launch (start us, length us, event | category | flops | bytes accessed | tf_op | source)
XLA Modules:
  0.0 213.5 jit_solution(14498392540684012376)
XLA Ops:
  6.5 0.0 copy-start
  6.5 0.0 copy-start.2
  6.5 0.0 copy-start.3
  6.5 0.0 all-gather.6.cloned.1.call-start
  6.5 0.7 all-gather.6.cloned.1.call-update
  7.3 0.0 copy-start.9
  7.3 0.0 all-gather.8.cloned.1.call-start
  8.0 0.7 pad_clamp_fusion
  8.6 0.0 copy-done
  8.6 0.0 copy-start.6
  8.6 0.8 gather_fusion.1
  9.5 0.1 copy.13
  9.6 0.0 copy-done.2
  9.6 0.0 copy-start.4
  9.6 0.8 gather_fusion.2
  10.5 0.7 copy.14
  11.2 0.0 copy-done.3
  11.2 0.8 gather_fusion
  12.1 0.0 copy-done.9
  12.1 0.1 fusion.16
  12.2 0.2 reduce_window_sum.11
  12.4 0.2 select_reduce_fusion
  12.6 0.1 multiply_reduce_fusion.1
  12.7 0.0 copy-done.6
  12.7 0.1 fusion.3.slope_ref
  12.8 32.0 %all-gather = bf16[512,512]{1,0:T(8,128)(2,1)S(1)} all-gather(bf16[128,512]{1,0:T(8,128)(2,1)S(1)} %gather_fusion), channel_id=2, replica_groups=mesh['zh'=4,'zl'=4,'core'=2,'x'=4,'y'=4] {'zh'}, dimensions={0}, use_global_device_ids=true | all-gather | bytes 655360 | tf_op jit(solution)/shard_map/all_gather | solution.py:181
  44.8 0.0 all-gather.8.cloned.1.call-update
  44.8 17.6 %all-gather.6.cloned.1.call-done = bf16[1024,512]{1,0:T(8,128)(2,1)} async-done(((bf16[256,512]{1,0:T(8,128)(2,1)}), bf16[1024,512]{1,0:T(8,128)(2,1)}) %all-gather.6.cloned.1.call-update) | async-done | bytes 1048592 | tf_op jit(solution)/shard_map/all_gather | solution.py:159
  62.5 2.3 %collective-permute-start = (bf16[4,256,512]{2,1,0:T(8,128)(2,1)}, bf16[4,256,512]{2,1,0:T(8,128)(2,1)S(1)}, u32[]{:S(2)}, u32[]{:S(2)}) collective-permute-start(bf16[4,256,512]{2,1,0:T(8,128)(2,1)} %bitcast.23), channel_id=1, source_target_pairs={{0,16},{16,0},{1,17},{17,1},{2,18},{18,2},{3,19},{19,3},{4,20},{20... | collective-permute-start | bytes 3145736 | tf_op jit(solution)/shard_map/ppermute | solution.py:185
  64.8 0.1 pad_add_fusion.place_ref
  64.9 2.4 %collective-permute-done.other_ref = bf16[4,256,512]{2,1,0:T(8,128)(2,1)S(1)} collective-permute-done((bf16[4,256,512]{2,1,0:T(8,128)(2,1)}, bf16[4,256,512]{2,1,0:T(8,128)(2,1)S(1)}, u32[]{:S(2)}, u32[]{:S(2)}) %collective-permute-start) | collective-permute-done | bytes 1048608 | tf_op jit(solution)/shard_map/ppermute | solution.py:185
  67.3 0.0 copy-start.1
  67.3 1.2 copy-done.1
  68.5 2.8 %shard_map.100 = bf16[4,4,512,128]{3,2,1,0:T(8,128)(2,1)S(1)} custom-call(s32[2]{0:T(128)S(1)} %pad_add_fusion.place_ref, bf16[4,128,512]{2,1,0:T(8,128)(2,1)S(1)} %bitcast.22, bf16[4,256,512]{2,1,0:T(8,128)(2,1)S(1)} %bitcast.24, bf16[4,256,512]{2,1,0:T(8,128)(2,1)S(1)} %collective-permute-done.other_ref), custom_call_target="tpu_custom_call" | custom-call | tf_op jit(solution)/shard_map/pallas_call | solution.py:47
  71.3 33.8 %all_to_all.20 = bf16[16,512,128]{2,1,0:T(8,128)(2,1)S(1)} all-to-all(bf16[16,512,128]{2,1,0:T(8,128)(2,1)S(1)} %bitcast.21), channel_id=1, replica_groups=mesh['zh'=4,'zl'=4,'core'=2,'x'=4,'y'=4] {'x','y'}, dimensions={0} | all-to-all | bytes 4194304 | tf_op jit(solution)/shard_map/all_to_all | solution.py:189
  105.1 0.0 copy-start.8
  105.1 0.3 reduce_sum.41
  105.4 0.7 collective-permute-start.1
  106.1 0.0 collective-permute-done.1.grad_ref
  106.1 0.0 copy-done.4
  106.1 0.0 copy-done.8
  106.1 0.0 copy-start.5
  106.1 0.1 multiply_reduce_fusion
  106.3 0.6 broadcast_in_dim.28
  106.9 23.1 %all-to-all-start.1 = ((f32[16,2,128]{2,1,0:T(2,128)}), f32[16,2,128]{2,1,0:T(2,128)S(1)}, u32[]{:S(2)}, u32[]{:S(2)}) async-start(f32[16,2,128]{2,1,0:T(2,128)} %broadcast_in_dim.28), calls=%async_computation.1 | async-start | bytes 32768 | tf_op jit(solution)/shard_map/all_to_all | solution.py:197
  130.0 0.9 copy.15.gain_ref
  130.9 5.6 %all-to-all-done.1.stat_ref = f32[16,2,128]{2,1,0:T(2,128)S(1)} async-done(((f32[16,2,128]{2,1,0:T(2,128)}), f32[16,2,128]{2,1,0:T(2,128)S(1)}, u32[]{:S(2)}, u32[]{:S(2)}) %all-to-all-start.1) | async-done | bytes 16416 | tf_op jit(solution)/shard_map/all_to_all | solution.py:197
  136.5 0.0 copy-start.7
  136.5 2.9 %all-gather.8.cloned.1.call-done = bf16[5120,512]{1,0:T(8,128)(2,1)} async-done(((bf16[160,512]{1,0:T(8,128)(2,1)}), bf16[5120,512]{1,0:T(8,128)(2,1)}) %all-gather.8.cloned.1.call-update) | async-done | bytes 5242896 | tf_op jit(solution)/shard_map/all_gather | solution.py:183
  139.4 0.0 copy-done.5
  139.4 0.0 copy-done.7
  139.4 7.3 %shard_map.101 = bf16[16,160,256]{2,1,0:T(8,128)(2,1)} custom-call(bf16[512,128]{1,0:T(8,128)(2,1)} %copy-done.5, bf16[512,128]{1,0:T(8,128)(2,1)} %bitcast.29, bf16[512,128]{1,0:T(8,128)(2,1)} %bitcast.30, f32[512,1]{1,0:T(8,128)} %copy.15.gain_ref, f32[16,2,128]{2,1,0:T(2,128)} %copy-done.7, bf16[32,160,512]{2,1,0:T(8,128)(2,1)} %bitcast.27), custom_call_target="tpu_custom_call" | custom-call | tf_op jit(solution)/shard_map/pallas_call | solution.py:103
  146.7 30.6 %all_to_all.21.hidden_ref = bf16[16,160,256]{2,1,0:T(8,128)(2,1)S(1)} all-to-all(bf16[16,160,256]{2,1,0:T(8,128)(2,1)} %shard_map.101), channel_id=1, replica_groups=mesh['zh'=4,'zl'=4,'core'=2,'x'=4,'y'=4] {'x','y'}, dimensions={0} | all-to-all | bytes 2621440 | tf_op jit(solution)/shard_map/all_to_all | solution.py:201
  177.3 1.0 shard_map.102
  178.3 8.8 %all-to-all-start.3 = ((bf16[32,8,384]{2,1,0:T(8,128)(2,1)}), bf16[32,8,384]{2,1,0:T(8,128)(2,1)S(1)}, u32[]{:S(2)}, u32[]{:S(2)}) async-start(bf16[32,8,384]{2,1,0:T(8,128)(2,1)} %bitcast.15), calls=%async_computation.3 | async-start | bytes 393216 | tf_op jit(solution)/shard_map/all_to_all | solution.py:208
  187.1 18.6 %all-to-all-done.3 = bf16[32,8,384]{2,1,0:T(8,128)(2,1)S(1)} async-done(((bf16[32,8,384]{2,1,0:T(8,128)(2,1)}), bf16[32,8,384]{2,1,0:T(8,128)(2,1)S(1)}, u32[]{:S(2)}, u32[]{:S(2)}) %all-to-all-start.3) | async-done | bytes 196640 | tf_op jit(solution)/shard_map/all_to_all | solution.py:208
  205.7 1.0 shard_map.103
  (4 shorter events, 0.1 us)
Async XLA Ops:
  6.5 2.1 copy-start
  6.5 3.1 %copy-start.2 = (bf16[256,512]{1,0:T(8,128)(2,1)S(1)}, bf16[256,512]{1,0:T(8,128)(2,1)}, u32[]{:S(2)}) copy-start(bf16[256,512]{1,0:T(8,128)(2,1)} %param.12) | copy-start | bytes 786436
  6.5 4.7 %copy-start.3 = (bf16[256,512]{1,0:T(8,128)(2,1)S(1)}, bf16[256,512]{1,0:T(8,128)(2,1)}, u32[]{:S(2)}) copy-start(bf16[256,512]{1,0:T(8,128)(2,1)} %param.10) | copy-start | bytes 786436
  6.5 55.9 %all-gather.6.cloned.1.call-start = ((), (), s32[]{:S(2)}) async-start(), calls=%async_computation.4 | async-start | bytes 1310720 | tf_op jit(solution)/shard_map/all_gather | solution.py:159
  7.3 4.8 %copy-start.9 = (s32[1,128]{1,0:T(1,128)S(1)}, s32[1,128]{1,0:T(1,128)}, u32[]{:S(2)}) copy-start(s32[1,128]{1,0:T(1,128)} %param.17) | copy-start | bytes 1540
  7.3 132.1 %all-gather.8.cloned.1.call-start = ((), (), s32[]{:S(2)}) async-start(), calls=%async_computation.5 | async-start | bytes 5406720 | tf_op jit(solution)/shard_map/all_gather | solution.py:183
  8.6 4.0 %copy-start.6 = (bf16[192,320]{1,0:T(8,128)(2,1)S(1)}, bf16[192,320]{1,0:T(8,128)(2,1)}, u32[]{:S(2)}) copy-start(bf16[192,320]{1,0:T(8,128)(2,1)} %param.19) | copy-start | bytes 368644
  9.6 96.4 %copy-start.4 = (bf16[128,512]{0,1:T(8,128)(2,1)}, bf16[128,512]{0,1:T(8,128)(2,1)S(1)}, u32[]{:S(2)}) copy-start(bf16[128,512]{0,1:T(8,128)(2,1)S(1)} %copy.13) | copy-start | bytes 393220
  62.5 4.8 %collective-permute-start = (bf16[4,256,512]{2,1,0:T(8,128)(2,1)}, bf16[4,256,512]{2,1,0:T(8,128)(2,1)S(1)}, u32[]{:S(2)}, u32[]{:S(2)}) collective-permute-start(bf16[4,256,512]{2,1,0:T(8,128)(2,1)} %bitcast.23), channel_id=1, source_target_pairs={{0,16},{16,0},{1,17},{17,1},{2,18},{18,2},{3,19},{19,3},{4,20},{20... | collective-permute-start | bytes 3145736 | tf_op jit(solution)/shard_map/ppermute | solution.py:185
  67.3 1.2 copy-start.1
  105.1 1.0 copy-start.8
  105.4 0.7 collective-permute-start.1
  106.1 33.3 %copy-start.5 = (bf16[512,128]{1,0:T(8,128)(2,1)}, bf16[512,128]{1,0:T(8,128)(2,1)S(1)}, u32[]{:S(2)}) copy-start(bf16[512,128]{1,0:T(8,128)(2,1)S(1)} %collective-permute-done.1.grad_ref) | copy-start | bytes 393220
  106.9 29.6 %all-to-all-start.1 = ((f32[16,2,128]{2,1,0:T(2,128)}), f32[16,2,128]{2,1,0:T(2,128)S(1)}, u32[]{:S(2)}, u32[]{:S(2)}) async-start(f32[16,2,128]{2,1,0:T(2,128)} %broadcast_in_dim.28), calls=%async_computation.1 | async-start | bytes 32768 | tf_op jit(solution)/shard_map/all_to_all | solution.py:197
  136.5 2.9 %copy-start.7 = (f32[16,2,128]{2,1,0:T(2,128)}, f32[16,2,128]{2,1,0:T(2,128)S(1)}, u32[]{:S(2)}) copy-start(f32[16,2,128]{2,1,0:T(2,128)S(1)} %all-to-all-done.1.stat_ref) | copy-start | bytes 49156
  178.3 27.4 %all-to-all-start.3 = ((bf16[32,8,384]{2,1,0:T(8,128)(2,1)}), bf16[32,8,384]{2,1,0:T(8,128)(2,1)S(1)}, u32[]{:S(2)}, u32[]{:S(2)}) async-start(bf16[32,8,384]{2,1,0:T(8,128)(2,1)} %bitcast.15), calls=%async_computation.3 | async-start | bytes 393216 | tf_op jit(solution)/shard_map/all_to_all | solution.py:208
Sparse Core Ops, SparseCore 0:
  9.5 52.9 all-gather.5
  64.6 74.7 all-gather.7

commit v10 on v8

--- a/solution.py
+++ b/solution.py
@@ -144,10 +144,14 @@
     positions = img_pos[0]
     image_count = positions.shape[0]
 
-    own = lax.all_gather(query_weight, "zl", axis=0)
-    picked = lax.all_gather(jnp.take(grad_query, positions, axis=0, mode="clip"), "zh", axis=0)
-    merge_weight, picked = lax.optimization_barrier((merge_weight, picked))
     merge_full = lax.all_gather(merge_weight, DP, axis=0)
+    own = lax.all_to_all(
+        jnp.broadcast_to(query_weight[None], (side,) + query_weight.shape), "zl", 0, 0, tiled=True
+    )
+    picked = jnp.take(grad_query, positions, axis=0, mode="clip")
+    own, picked = lax.optimization_barrier((own, picked))
+    other = lax.ppermute(own, "core", [(0, 1), (1, 0)])
+    picked = lax.all_gather(picked, "zh", axis=0)
     inputs = jnp.take(embeds, positions, axis=0, mode="clip").T
     residual = jnp.take(grad_resid, positions, axis=0, mode="clip").T
     gain = norm_gain[:, None]
@@ -165,7 +169,6 @@
     spot = number // capacity * SLOT_PITCH + number % capacity
     slope = gelu_slope(merge_pre)
 
-    other = lax.ppermute(own, "core", [(0, 1), (1, 0)])
     place = jnp.stack([lax.axis_index("core"), lax.axis_index("zh")]).astype(jnp.int32)
     partial_value = query_products(place, picked, own, other)
     partial_value = partial_value.reshape((shares,) + partial_value.shape[2:])
@@ -174,6 +177,7 @@
     exchange = [
         (h * side + (a + h) % side, a * side + h) for a in range(side) for h in range(side)
     ]
+    normal_grad, merge_full = lax.optimization_barrier((normal_grad, merge_full))
     normal_grad = lax.ppermute(normal_grad, ("zh", "x"), exchange)
     inner = jnp.sum(gain * normal_grad.astype(jnp.float32) * wide, axis=0)
     stats = jnp.stack([squares, inner])

time: 210 us -> 214 us (1.019)
  starting transfers between devices: 46.9 us -> 52.2 us
    all_to_all x0 -> x1, waiting for transfers between devices: none -> 26.9 us  [local(): lax.all_to_all(jnp.broadcast_to(query_weight[None], (side,) + query_weigh...]
    all_gather x1 -> x0, waiting for transfers between devices: 18.4 us -> none  [local(): own = lax.all_gather(query_weight, 'zl', axis=0)]
    all_to_all x1, starting transfers between devices: 10 us -> 17.8 us  [local(): lax.all_to_all(outbox.reshape(groups, SLOT_PITCH, lanes), DP, 0, 0, tiled...]
    all_to_all x1, starting transfers between devices: 10.8 us -> 3.83 us  [local(): hidden = lax.all_to_all(partial_hidden, TP, 0, 0, tiled=True)]
    all_to_all x0 -> x1, starting transfers between devices: none -> 6.44 us  [local(): lax.all_to_all(jnp.broadcast_to(query_weight[None], (side,) + query_weigh...]
    all_to_all x1, starting transfers between devices: 22.9 us -> 16.6 us  [local(): lax.all_to_all(jnp.broadcast_to(stats[None], (shares,) + stats.shape), TP...]
    all_to_all x1, waiting for transfers between devices: 17.9 us -> 12.8 us  [local(): hidden = lax.all_to_all(partial_hidden, TP, 0, 0, tiled=True)]
    ppermute x1, starting transfers between devices: 2.46 us -> 6.87 us  [local(): other = lax.ppermute(own, 'core', [(0, 1), (1, 0)])]
  transfers between devices with their start and end apart: 7 -> 7, of which waited for: 6 -> 4; matrix products, arithmetic and copies ran while one was open for 3% -> 3% of each run, Pallas kernels for 1% -> 1%
where the time goes in v10:
time: 214 us
  blocking collectives  66 us (31%)
  waiting for transfers between devices  64.2 us (30%)
  starting transfers between devices  52.2 us (24%)
  between operations  14.2 us (7%)
  local copies, waits for them, and re-layouts  8.1 us (4%)
  Pallas kernels  7.87 us (4%)
    all_gather x1, blocking collectives, local(): picked = lax.all_gather(picked, 'zh', axis=0)  33.6 us
    all_to_all x1, blocking collectives, local(): swapped = lax.all_to_all(partial_value, TP, 0, 0, tiled=True)  32.4 us
    all_to_all x1, waiting for transfers between devices, local(): lax.all_to_all(jnp.broadcast_to(query_weight[None], (side,) + query_weigh...  26.9 us
    all_to_all x1, waiting for transfers between devices, local(): lax.all_to_all(outbox.reshape(groups, SLOT_PITCH, lanes), DP, 0, 0, tiled...  18.4 us
    all_to_all x1, starting transfers between devices, local(): lax.all_to_all(outbox.reshape(groups, SLOT_PITCH, lanes), DP, 0, 0, tiled...  17.8 us
    all_to_all x1, starting transfers between devices, local(): lax.all_to_all(jnp.broadcast_to(stats[None], (shares,) + stats.shape), TP...  16.6 us
    all_to_all x1, waiting for transfers between devices, local(): hidden = lax.all_to_all(partial_hidden, TP, 0, 0, tiled=True)  12.8 us
    ppermute x1, starting transfers between devices, local(): other = lax.ppermute(own, 'core', [(0, 1), (1, 0)])  6.87 us
  transfers between devices with their start and end apart: 7, of which 4 were waited for; matrix products, arithmetic and copies ran while one was open for 3% of the time, Pallas kernels for 1%

profile of v10, /device:TPU:1, one launch (start us, length us, event | category | flops | bytes accessed | tf_op | source)
XLA Modules:
  0.0 213.8 jit_solution(7646527403876910687)
XLA Ops:
  6.5 0.0 copy-start
  6.5 0.0 copy-start.7
  6.5 0.0 all-gather.4.cloned.1.call-start
  6.5 0.7 all-gather.4.cloned.1.call-update
  7.3 2.0 broadcast_in_dim.16
  9.3 6.4 %all-to-all-start = ((bf16[4,256,512]{2,1,0:T(8,128)(2,1)}), bf16[4,256,512]{2,1,0:T(8,128)(2,1)S(1)}, u32[]{:S(2)}, u32[]{:S(2)}) async-start(bf16[4,256,512]{2,1,0:T(8,128)(2,1)} %broadcast_in_dim.16), calls=%async_computation | async-start | bytes 2097152 | tf_op jit(solution)/shard_map/all_to_all | solution.py:148
  15.7 0.0 copy-done.7
  15.8 0.0 copy-done
  15.8 0.8 gather_fusion
  16.6 26.9 %all-to-all-done.own_ref = bf16[4,256,512]{2,1,0:T(8,128)(2,1)S(1)} async-done(((bf16[4,256,512]{2,1,0:T(8,128)(2,1)}), bf16[4,256,512]{2,1,0:T(8,128)(2,1)S(1)}, u32[]{:S(2)}, u32[]{:S(2)}) %all-to-all-start) | async-done | bytes 1048608 | tf_op jit(solution)/shard_map/all_to_all | solution.py:148
  43.5 6.9 %collective-permute-start = (bf16[4,256,512]{2,1,0:T(8,128)(2,1)S(1)}, bf16[4,256,512]{2,1,0:T(8,128)(2,1)S(1)}, u32[]{:S(2)}, u32[]{:S(2)}) collective-permute-start(bf16[4,256,512]{2,1,0:T(8,128)(2,1)S(1)} %all-to-all-done.own_ref), channel_id=1, source_target_pairs={{0,16},{16,0},{1,17},{17,1},{2,18},{18,2},{3,19},{19,3},{4,20},{20... | collective-permute-start | bytes 3145736 | tf_op jit(solution)/shard_map/ppermute | solution.py:153
  50.4 0.1 pad_add_fusion.place_ref
  50.5 33.6 %all-gather = bf16[512,512]{1,0:T(8,128)(2,1)S(1)} all-gather(bf16[128,512]{1,0:T(8,128)(2,1)S(1)} %gather_fusion), channel_id=2, replica_groups=mesh['zh'=4,'zl'=4,'core'=2,'x'=4,'y'=4] {'zh'}, dimensions={0}, use_global_device_ids=true | all-gather | bytes 655360 | tf_op jit(solution)/shard_map/all_gather | solution.py:154
  84.1 0.0 collective-permute-done.other_ref
  84.1 2.8 %shard_map.100 = bf16[4,4,512,128]{3,2,1,0:T(8,128)(2,1)S(1)} custom-call(s32[2]{0:T(128)S(1)} %pad_add_fusion.place_ref, bf16[4,128,512]{2,1,0:T(8,128)(2,1)S(1)} %bitcast.25, bf16[4,256,512]{2,1,0:T(8,128)(2,1)S(1)} %all-to-all-done.own_ref, bf16[4,256,512]{2,1,0:T(8,128)(2,1)S(1)} %collective-permute-done.other_ref), custom_call_target="tpu_custom_call" | custom-call | tf_op jit(solution)/shard_map/pallas_call | solution.py:46
  86.8 32.4 %all_to_all.25 = bf16[16,512,128]{2,1,0:T(8,128)(2,1)S(1)} all-to-all(bf16[16,512,128]{2,1,0:T(8,128)(2,1)S(1)} %bitcast.23), channel_id=1, replica_groups=mesh['zh'=4,'zl'=4,'core'=2,'x'=4,'y'=4] {'x','y'}, dimensions={0} | all-to-all | bytes 4194304 | tf_op jit(solution)/shard_map/all_to_all | solution.py:175
  119.3 0.0 copy-start.2
  119.3 0.0 copy-start.5
  119.3 0.0 copy-start.3
  119.3 0.3 reduce_sum.41
  119.6 0.0 all-gather.4.cloned.1.call-done
  119.6 0.7 collective-permute-start.1
  120.3 0.0 copy-done.2
  120.3 0.8 gather_fusion.1
  121.1 0.1 copy.13
  121.3 0.0 collective-permute-done.1.grad_ref
  121.3 0.0 copy-done.5
  121.3 0.2 fusion.6
  121.4 0.6 broadcast_in_dim.32
  122.1 16.6 %all-to-all-start.2 = ((f32[16,2,128]{2,1,0:T(2,128)}), f32[16,2,128]{2,1,0:T(2,128)S(1)}, u32[]{:S(2)}, u32[]{:S(2)}) async-start(f32[16,2,128]{2,1,0:T(2,128)} %broadcast_in_dim.32), calls=%async_computation.2 | async-start | bytes 32768 | tf_op jit(solution)/shard_map/all_to_all | solution.py:184
  138.7 0.0 copy-done.3
  138.7 0.8 gather_fusion.2
  139.5 0.1 copy.14
  139.7 0.1 copy.15.gain_ref
  139.8 5.3 %all-to-all-done.2.stat_ref = f32[16,2,128]{2,1,0:T(2,128)S(1)} async-done(((f32[16,2,128]{2,1,0:T(2,128)}), f32[16,2,128]{2,1,0:T(2,128)S(1)}, u32[]{:S(2)}, u32[]{:S(2)}) %all-to-all-start.2) | async-done | bytes 16416 | tf_op jit(solution)/shard_map/all_to_all | solution.py:184
  145.1 0.0 copy-start.1
  145.1 2.5 %copy-done.1 = bf16[5120,512]{1,0:T(8,128)(2,1)S(1)} copy-done((bf16[5120,512]{1,0:T(8,128)(2,1)S(1)}, bf16[5120,512]{1,0:T(8,128)(2,1)}, u32[]{:S(2)}) %copy-start.1) | copy-done | bytes 5242904
  147.6 3.1 %shard_map.101 = bf16[16,160,256]{2,1,0:T(8,128)(2,1)} custom-call(bf16[512,128]{1,0:T(8,128)(2,1)S(1)} %collective-permute-done.1.grad_ref, bf16[512,128]{1,0:T(8,128)(2,1)S(1)} %bitcast.26, bf16[512,128]{1,0:T(8,128)(2,1)S(1)} %bitcast.28, f32[512,1]{1,0:T(8,128)S(1)} %copy.15.gain_ref, f32[16,2,128]{2,1,0:T(2,128)S(1)} %all-to-all-done.2.stat_ref, ...), custom_call_target="tpu_custom_call" | custom-call | tf_op jit(solution)/shard_map/pallas_call | solution.py:91
  150.7 0.0 copy-start.6
  150.7 0.0 copy-start.4
  150.7 3.8 %all-to-all-start.3 = ((bf16[16,160,256]{2,1,0:T(8,128)(2,1)}), bf16[16,160,256]{2,1,0:T(8,128)(2,1)S(1)}, u32[]{:S(2)}, u32[]{:S(2)}) async-start(bf16[16,160,256]{2,1,0:T(8,128)(2,1)} %shard_map.101), calls=%async_computation.3 | async-start | bytes 2621440 | tf_op jit(solution)/shard_map/all_to_all | solution.py:190
  155.2 0.0 copy-done.6
  155.2 0.1 fusion.18
  155.3 0.2 reduce_window_sum.11
  155.5 0.2 select_reduce_fusion
  155.7 12.8 %all-to-all-done.3.hidden_ref = bf16[16,160,256]{2,1,0:T(8,128)(2,1)S(1)} async-done(((bf16[16,160,256]{2,1,0:T(8,128)(2,1)}), bf16[16,160,256]{2,1,0:T(8,128)(2,1)S(1)}, u32[]{:S(2)}, u32[]{:S(2)}) %all-to-all-start.3) | async-done | bytes 1310752 | tf_op jit(solution)/shard_map/all_to_all | solution.py:190
  168.5 1.0 shard_map.102
  169.5 17.8 %all-to-all-start.4 = ((bf16[32,8,384]{2,1,0:T(8,128)(2,1)}), bf16[32,8,384]{2,1,0:T(8,128)(2,1)S(1)}, u32[]{:S(2)}, u32[]{:S(2)}) async-start(bf16[32,8,384]{2,1,0:T(8,128)(2,1)} %bitcast.14), calls=%async_computation.4 | async-start | bytes 393216 | tf_op jit(solution)/shard_map/all_to_all | solution.py:197
  187.4 0.0 copy-done.4
  187.4 0.1 fusion.3.slope_ref
  187.6 18.4 %all-to-all-done.4 = bf16[32,8,384]{2,1,0:T(8,128)(2,1)S(1)} async-done(((bf16[32,8,384]{2,1,0:T(8,128)(2,1)}), bf16[32,8,384]{2,1,0:T(8,128)(2,1)S(1)}, u32[]{:S(2)}, u32[]{:S(2)}) %all-to-all-start.4) | async-done | bytes 196640 | tf_op jit(solution)/shard_map/all_to_all | solution.py:197
  206.0 1.0 shard_map.103
  (5 shorter events, 0.1 us)
Async XLA Ops:
  6.5 9.2 %copy-start = (bf16[256,512]{1,0:T(8,128)(2,1)S(1)}, bf16[256,512]{1,0:T(8,128)(2,1)}, u32[]{:S(2)}) copy-start(bf16[256,512]{1,0:T(8,128)(2,1)} %param.10) | copy-start | bytes 786436
  6.5 9.2 %copy-start.7 = (s32[1,128]{1,0:T(1,128)S(1)}, s32[1,128]{1,0:T(1,128)}, u32[]{:S(2)}) copy-start(s32[1,128]{1,0:T(1,128)} %param.15) | copy-start | bytes 1540
  6.5 113.0 %all-gather.4.cloned.1.call-start = ((), (), s32[]{:S(2)}) async-start(), calls=%async_computation.5 | async-start | bytes 5406720 | tf_op jit(solution)/shard_map/all_gather | solution.py:147
  9.3 34.2 %all-to-all-start = ((bf16[4,256,512]{2,1,0:T(8,128)(2,1)}), bf16[4,256,512]{2,1,0:T(8,128)(2,1)S(1)}, u32[]{:S(2)}, u32[]{:S(2)}) async-start(bf16[4,256,512]{2,1,0:T(8,128)(2,1)} %broadcast_in_dim.16), calls=%async_computation | async-start | bytes 2097152 | tf_op jit(solution)/shard_map/all_to_all | solution.py:148
  43.5 40.6 %collective-permute-start = (bf16[4,256,512]{2,1,0:T(8,128)(2,1)S(1)}, bf16[4,256,512]{2,1,0:T(8,128)(2,1)S(1)}, u32[]{:S(2)}, u32[]{:S(2)}) collective-permute-start(bf16[4,256,512]{2,1,0:T(8,128)(2,1)S(1)} %all-to-all-done.own_ref), channel_id=1, source_target_pairs={{0,16},{16,0},{1,17},{17,1},{2,18},{18,2},{3,19},{19,3},{4,20},{20... | collective-permute-start | bytes 3145736 | tf_op jit(solution)/shard_map/ppermute | solution.py:153
  119.3 1.0 copy-start.2
  119.3 2.0 copy-start.5
  119.3 19.4 %copy-start.3 = (bf16[256,512]{1,0:T(8,128)(2,1)S(1)}, bf16[256,512]{1,0:T(8,128)(2,1)}, u32[]{:S(2)}) copy-start(bf16[256,512]{1,0:T(8,128)(2,1)} %param.12) | copy-start | bytes 786436
  119.6 1.7 collective-permute-start.1
  122.1 23.1 %all-to-all-start.2 = ((f32[16,2,128]{2,1,0:T(2,128)}), f32[16,2,128]{2,1,0:T(2,128)S(1)}, u32[]{:S(2)}, u32[]{:S(2)}) async-start(f32[16,2,128]{2,1,0:T(2,128)} %broadcast_in_dim.32), calls=%async_computation.2 | async-start | bytes 32768 | tf_op jit(solution)/shard_map/all_to_all | solution.py:184
  145.1 2.5 %copy-start.1 = (bf16[5120,512]{1,0:T(8,128)(2,1)S(1)}, bf16[5120,512]{1,0:T(8,128)(2,1)}, u32[]{:S(2)}) copy-start(bf16[5120,512]{1,0:T(8,128)(2,1)} %all-gather.4.cloned.1.call-done) | copy-start | bytes 15728644
  150.7 4.5 %copy-start.6 = (s32[1,128]{1,0:T(1,128)S(1)}, s32[1,128]{1,0:T(1,128)}, u32[]{:S(2)}) copy-start(s32[1,128]{1,0:T(1,128)} %param.17) | copy-start | bytes 1540
  150.7 36.7 %copy-start.4 = (bf16[192,320]{1,0:T(8,128)(2,1)S(1)}, bf16[192,320]{1,0:T(8,128)(2,1)}, u32[]{:S(2)}) copy-start(bf16[192,320]{1,0:T(8,128)(2,1)} %param.19) | copy-start | bytes 368644
  150.7 17.8 %all-to-all-start.3 = ((bf16[16,160,256]{2,1,0:T(8,128)(2,1)}), bf16[16,160,256]{2,1,0:T(8,128)(2,1)S(1)}, u32[]{:S(2)}, u32[]{:S(2)}) async-start(bf16[16,160,256]{2,1,0:T(8,128)(2,1)} %shard_map.101), calls=%async_computation.3 | async-start | bytes 2621440 | tf_op jit(solution)/shard_map/all_to_all | solution.py:190
  169.5 36.4 %all-to-all-start.4 = ((bf16[32,8,384]{2,1,0:T(8,128)(2,1)}), bf16[32,8,384]{2,1,0:T(8,128)(2,1)S(1)}, u32[]{:S(2)}, u32[]{:S(2)}) async-start(bf16[32,8,384]{2,1,0:T(8,128)(2,1)} %bitcast.14), calls=%async_computation.4 | async-start | bytes 393216 | tf_op jit(solution)/shard_map/all_to_all | solution.py:197
Sparse Core Ops, SparseCore 0:
  9.5 99.1 all-gather.3

commit v11 on v10

--- a/solution.py
+++ b/solution.py
@@ -22,84 +22,64 @@
     return cdf_part + value * pdf_part
 
 
-def query_kernel(place_ref, rows_ref, own_ref, other_ref, out_ref, turned):
+def query_kernel(place_ref, rows_ref, own_ref, other_ref, out_ref):
     parts, count, depth = rows_ref.shape
-    height = own_ref.shape[1]
+    blocks, height, _ = own_ref.shape
     core, shift = place_ref[0], place_ref[1]
-
-    @pl.when(pl.program_id(0) == 0)
-    def _():
-        turned[...] = rows_ref[...].reshape(parts * count, depth).T
-
-    for weight_ref, place in ((own_ref, core), (other_ref, 1 - core)):
-        product = jnp.dot(weight_ref[0], turned[...], preferred_element_type=jnp.float32)
-        product = product.astype(out_ref.dtype)
-        spot = pl.ds(pl.multiple_of(place * height, height), height)
-        for part in range(parts):
-            out_ref[lax.rem(part + shift, parts), 0, spot] = product[:, part * count : (part + 1) * count]
+    turned = rows_ref[...].reshape(parts * count, depth).T
+    for block in range(blocks):
+        for weight_ref, place in ((own_ref, core), (other_ref, 1 - core)):
+            product = jnp.dot(weight_ref[block], turned, preferred_element_type=jnp.float32)
+            product = product.astype(out_ref.dtype)
+            spot = pl.ds(pl.multiple_of(place * height, height), height)
+            for part in range(parts):
+                out_ref[lax.rem(part + shift, parts), block, spot] = product[
+                    :, part * count : (part + 1) * count
+                ]
 
 
 def query_products(place, rows, own, other):
-    parts, count, depth = rows.shape
-    steps, height, _ = own.shape
-    weight_spec = pl.BlockSpec((1, height, depth), lambda i, _: (i, 0, 0))
+    parts, count, _ = rows.shape
+    blocks, height, _ = own.shape
     return pl.pallas_call(
         query_kernel,
-        grid_spec=pltpu.PrefetchScalarGridSpec(
-            num_scalar_prefetch=1,
-            grid=(steps,),
-            in_specs=[
-                pl.BlockSpec((parts, count, depth), lambda i, _: (0, 0, 0)),
-                weight_spec,
-                weight_spec,
-            ],
-            out_specs=pl.BlockSpec((parts, 1, 2 * height, count), lambda i, _: (0, i, 0, 0)),
-            scratch_shapes=[pltpu.VMEM((depth, parts * count), jnp.bfloat16)],
-        ),
-        out_shape=jax.ShapeDtypeStruct((parts, steps, 2 * height, count), jnp.bfloat16),
+        in_specs=[pl.BlockSpec(memory_space=pltpu.SMEM)]
+        + [pl.BlockSpec(memory_space=pltpu.VMEM)] * 3,
+        out_specs=pl.BlockSpec(memory_space=pltpu.VMEM),
+        out_shape=jax.ShapeDtypeStruct((parts, blocks, 2 * height, count), jnp.bfloat16),
         compiler_params=pltpu.CompilerParams(vmem_limit_bytes=24 * MIB),
     )(place, rows, own, other)
 
 
-def merge_kernel(grad_ref, input_ref, resid_ref, gain_ref, stat_ref, weight_ref, out_ref, handoff):
+def merge_kernel(grad_ref, input_ref, resid_ref, gain_ref, stat_ref, weight_ref, out_ref):
     count = grad_ref.shape[1]
-
-    @pl.when(pl.program_id(0) == 0)
-    def _():
-        stats = jnp.sum(stat_ref[...], axis=0)
-        inverse = lax.rsqrt(stats[0:1] / D + NORM_EPS)
-        factor = inverse * inverse * inverse * stats[1:2] / D
-        scaled = gain_ref[...] * grad_ref[...].astype(jnp.float32)
-        handoff[...] = (
-            resid_ref[...].astype(jnp.float32)
-            + inverse * scaled
-            - input_ref[...].astype(jnp.float32) * factor
-        ).astype(jnp.bfloat16)
-
-    for part in range(out_ref.shape[0]):
+    stats = jnp.sum(stat_ref[...], axis=0)
+    inverse = lax.rsqrt(stats[0:1] / D + NORM_EPS)
+    factor = inverse * inverse * inverse * stats[1:2] / D
+    scaled = gain_ref[...] * grad_ref[...].astype(jnp.float32)
+    handoff = (
+        resid_ref[...].astype(jnp.float32)
+        + inverse * scaled
+        - input_ref[...].astype(jnp.float32) * factor
+    ).astype(jnp.bfloat16)
+    for share in range(out_ref.shape[0]):
         for half in range(2):
             product = jnp.dot(
-                weight_ref[2 * part + half], handoff[...], preferred_element_type=jnp.float32
+                weight_ref[2 * share + half], handoff, preferred_element_type=jnp.float32
             )
-            out_ref[part, :, half * count : (half + 1) * count] = product.astype(out_ref.dtype)
-
-
-def merge_products(grad, inputs, residual, gain, stats, weights, shares, steps):
-    blocks, height, width = weights.shape
+            out_ref[share, :, half * count : (half + 1) * count] = product.astype(out_ref.dtype)
+
+
+def merge_products(grad, inputs, residual, gain, stats, weights, shares):
+    _, height, _ = weights.shape
     count = grad.shape[1]
-    whole = [grad, inputs, residual, gain, stats]
     return pl.pallas_call(
         merge_kernel,
-        grid=(steps,),
-        in_specs=[
-            pl.BlockSpec(a.shape, lambda i, rank=a.ndim: (0,) * rank) for a in whole
-        ]
-        + [pl.BlockSpec((blocks // steps, height, width), lambda i: (i, 0, 0))],
-        out_specs=pl.BlockSpec((shares // steps, height, 2 * count), lambda i: (i, 0, 0)),
+        in_specs=[pl.BlockSpec(memory_space=pltpu.VMEM)] * 6,
+        out_specs=pl.BlockSpec(memory_space=pltpu.VMEM),
         out_shape=jax.ShapeDtypeStruct((shares, height, 2 * count), jnp.bfloat16),
-        scratch_shapes=[pltpu.VMEM((width, count), jnp.bfloat16)],
-        compiler_params=pltpu.CompilerParams(vmem_limit_bytes=24 * MIB),
-    )(*whole, weights)
+        compiler_params=pltpu.CompilerParams(vmem_limit_bytes=24 * MIB),
+    )(grad, inputs, residual, gain, stats, weights)
 
 
 def send_kernel(hidden_ref, target_ref, out_ref):
@@ -144,12 +124,12 @@
     positions = img_pos[0]
     image_count = positions.shape[0]
 
-    merge_full = lax.all_gather(merge_weight, DP, axis=0)
     own = lax.all_to_all(
         jnp.broadcast_to(query_weight[None], (side,) + query_weight.shape), "zl", 0, 0, tiled=True
     )
     picked = jnp.take(grad_query, positions, axis=0, mode="clip")
-    own, picked = lax.optimization_barrier((own, picked))
+    own, picked, merge_weight = lax.optimization_barrier((own, picked, merge_weight))
+    merge_full = lax.all_gather(merge_weight, DP, axis=0)
     other = lax.ppermute(own, "core", [(0, 1), (1, 0)])
     picked = lax.all_gather(picked, "zh", axis=0)
     inputs = jnp.take(embeds, positions, axis=0, mode="clip").T
@@ -185,7 +165,7 @@
         jnp.broadcast_to(stats[None], (shares,) + stats.shape), TP, 0, 0, tiled=True
     )
     partial_hidden = merge_products(
-        normal_grad, inputs, residual, gain, stats, merge_full, shares, 4
+        normal_grad, inputs, residual, gain, stats, merge_full, shares
     )
     hidden = lax.all_to_all(partial_hidden, TP, 0, 0, tiled=True)
     lanes = -(-columns // LANES) * LANES

time: 214 us -> 225 us (1.051)
  waiting for transfers between devices: 64.2 us -> 75.6 us
    all_gather x1, waiting for transfers between devices: 0.02 us -> 11.5 us  [local(): merge_full = lax.all_gather(merge_weight, DP, axis=0)]
    all_to_all x1, starting transfers between devices: 16.6 us -> 22.6 us  [local(): lax.all_to_all(jnp.broadcast_to(stats[None], (shares,) + stats.shape), TP...]
    all_to_all x1, starting transfers between devices: 17.8 us -> 13.7 us  [local(): lax.all_to_all(outbox.reshape(groups, SLOT_PITCH, lanes), DP, 0, 0, tiled...]
    all_to_all x1, waiting for transfers between devices: 12.8 us -> 16.5 us  [local(): hidden = lax.all_to_all(partial_hidden, TP, 0, 0, tiled=True)]
    all_to_all x1, waiting for transfers between devices: 26.9 us -> 23.8 us  [local(): lax.all_to_all(jnp.broadcast_to(query_weight[None], (side,) + query_weigh...]
    ppermute x1, starting transfers between devices: 6.87 us -> 3.94 us  [local(): other = lax.ppermute(own, 'core', [(0, 1), (1, 0)])]
  transfers between devices with their start and end apart: 7 -> 7, of which waited for: 4 -> 5; matrix products, arithmetic and copies ran while one was open for 3% -> 2% of each run, Pallas kernels for 1% -> 1%
where the time goes in v11:
time: 225 us; the launch traced here: 224 us
  waiting for transfers between devices  75.6 us (34%)
  blocking collectives  67.2 us (30%)
  starting transfers between devices  51.2 us (23%)
  between operations  14.2 us (6%)
  local copies, waits for them, and re-layouts  8.11 us (4%)
  Pallas kernels  6.69 us (3%)
    all_gather x1, blocking collectives, local(): picked = lax.all_gather(picked, 'zh', axis=0)  34.8 us
    all_to_all x1, blocking collectives, local(): swapped = lax.all_to_all(partial_value, TP, 0, 0, tiled=True)  32.4 us
    all_to_all x1, waiting for transfers between devices, local(): lax.all_to_all(jnp.broadcast_to(query_weight[None], (side,) + query_weigh...  23.8 us
    all_to_all x1, starting transfers between devices, local(): lax.all_to_all(jnp.broadcast_to(stats[None], (shares,) + stats.shape), TP...  22.6 us
    all_to_all x1, waiting for transfers between devices, local(): lax.all_to_all(outbox.reshape(groups, SLOT_PITCH, lanes), DP, 0, 0, tiled...  18.4 us
    all_to_all x1, waiting for transfers between devices, local(): hidden = lax.all_to_all(partial_hidden, TP, 0, 0, tiled=True)  16.5 us
    all_to_all x1, starting transfers between devices, local(): lax.all_to_all(outbox.reshape(groups, SLOT_PITCH, lanes), DP, 0, 0, tiled...  13.7 us
    all_gather x1, waiting for transfers between devices, local(): merge_full = lax.all_gather(merge_weight, DP, axis=0)  11.5 us
  transfers between devices with their start and end apart: 7, of which 5 were waited for; matrix products, arithmetic and copies ran while one was open for 2% of the time, Pallas kernels for 1%

profile of v11, /device:TPU:1, one launch (start us, length us, event | category | flops | bytes accessed | tf_op | source)
XLA Modules:
  0.0 224.1 jit_solution(15526026407796580829)
XLA Ops:
  6.5 0.0 copy-start
  6.5 0.0 copy-start.7
  6.5 2.1 broadcast_in_dim.16
  8.6 6.4 %all-to-all-start = ((bf16[4,256,512]{2,1,0:T(8,128)(2,1)}), bf16[4,256,512]{2,1,0:T(8,128)(2,1)S(1)}, u32[]{:S(2)}, u32[]{:S(2)}) async-start(bf16[4,256,512]{2,1,0:T(8,128)(2,1)} %broadcast_in_dim.16), calls=%async_computation | async-start | bytes 2097152 | tf_op jit(solution)/shard_map/all_to_all | solution.py:127
  15.0 0.0 all-gather.4.cloned.1.call-start
  15.0 0.0 copy-done.7
  15.1 0.0 copy-done
  15.1 0.8 gather_fusion
  15.9 23.8 %all-to-all-done.own_ref = bf16[4,256,512]{2,1,0:T(8,128)(2,1)S(1)} async-done(((bf16[4,256,512]{2,1,0:T(8,128)(2,1)}), bf16[4,256,512]{2,1,0:T(8,128)(2,1)S(1)}, u32[]{:S(2)}, u32[]{:S(2)}) %all-to-all-start) | async-done | bytes 1048608 | tf_op jit(solution)/shard_map/all_to_all | solution.py:127
  39.7 0.0 all-gather.4.cloned.1.call-update
  39.7 3.9 %collective-permute-start = (bf16[4,256,512]{2,1,0:T(8,128)(2,1)S(1)}, bf16[4,256,512]{2,1,0:T(8,128)(2,1)S(1)}, u32[]{:S(2)}, u32[]{:S(2)}) collective-permute-start(bf16[4,256,512]{2,1,0:T(8,128)(2,1)S(1)} %all-to-all-done.own_ref), channel_id=1, source_target_pairs={{0,16},{16,0},{1,17},{17,1},{2,18},{18,2},{3,19},{19,3},{4,20},{20... | collective-permute-start | bytes 3145736 | tf_op jit(solution)/shard_map/ppermute | solution.py:133
  43.7 0.1 pad_add_fusion.place_ref
  43.7 34.8 %all-gather = bf16[512,512]{1,0:T(8,128)(2,1)S(1)} all-gather(bf16[128,512]{1,0:T(8,128)(2,1)S(1)} %gather_fusion), channel_id=2, replica_groups=mesh['zh'=4,'zl'=4,'core'=2,'x'=4,'y'=4] {'zh'}, dimensions={0}, use_global_device_ids=true | all-gather | bytes 655360 | tf_op jit(solution)/shard_map/all_gather | solution.py:134
  78.5 0.0 collective-permute-done.other_ref
  78.6 2.0 shard_map.100
  80.5 32.4 %all_to_all.25 = bf16[16,512,128]{2,1,0:T(8,128)(2,1)S(1)} all-to-all(bf16[16,512,128]{2,1,0:T(8,128)(2,1)S(1)} %bitcast.23), channel_id=1, replica_groups=mesh['zh'=4,'zl'=4,'core'=2,'x'=4,'y'=4] {'x','y'}, dimensions={0} | all-to-all | bytes 4194304 | tf_op jit(solution)/shard_map/all_to_all | solution.py:155
  112.9 0.0 copy-start.2
  112.9 0.0 copy-start.5
  112.9 0.0 copy-start.3
  112.9 0.3 reduce_sum.41
  113.2 11.5 %all-gather.4.cloned.1.call-done = bf16[5120,512]{1,0:T(8,128)(2,1)} async-done(((bf16[160,512]{1,0:T(8,128)(2,1)}), bf16[5120,512]{1,0:T(8,128)(2,1)}) %all-gather.4.cloned.1.call-update) | async-done | bytes 5242896 | tf_op jit(solution)/shard_map/all_gather | solution.py:132
  124.7 0.7 collective-permute-start.1
  125.4 0.0 copy-done.2
  125.4 0.8 gather_fusion.1
  126.3 0.1 copy.13
  126.4 0.0 collective-permute-done.1.grad_ref
  126.4 0.0 copy-done.5
  126.4 0.2 fusion.6
  126.6 0.6 broadcast_in_dim.32
  127.2 22.6 %all-to-all-start.2 = ((f32[16,2,128]{2,1,0:T(2,128)}), f32[16,2,128]{2,1,0:T(2,128)S(1)}, u32[]{:S(2)}, u32[]{:S(2)}) async-start(f32[16,2,128]{2,1,0:T(2,128)} %broadcast_in_dim.32), calls=%async_computation.2 | async-start | bytes 32768 | tf_op jit(solution)/shard_map/all_to_all | solution.py:164
  149.8 0.0 copy-done.3
  149.8 0.8 gather_fusion.2
  150.7 0.1 copy.14
  150.8 0.1 copy.15.gain_ref
  150.9 5.3 %all-to-all-done.2.stat_ref = f32[16,2,128]{2,1,0:T(2,128)S(1)} async-done(((f32[16,2,128]{2,1,0:T(2,128)}), f32[16,2,128]{2,1,0:T(2,128)S(1)}, u32[]{:S(2)}, u32[]{:S(2)}) %all-to-all-start.2) | async-done | bytes 16416 | tf_op jit(solution)/shard_map/all_to_all | solution.py:164
  156.2 0.0 copy-start.1
  156.2 2.5 %copy-done.1 = bf16[5120,512]{1,0:T(8,128)(2,1)S(1)} copy-done((bf16[5120,512]{1,0:T(8,128)(2,1)S(1)}, bf16[5120,512]{1,0:T(8,128)(2,1)}, u32[]{:S(2)}) %copy-start.1) | copy-done | bytes 5242904
  158.7 2.7 %shard_map.101 = bf16[16,160,256]{2,1,0:T(8,128)(2,1)} custom-call(bf16[512,128]{1,0:T(8,128)(2,1)S(1)} %collective-permute-done.1.grad_ref, bf16[512,128]{1,0:T(8,128)(2,1)S(1)} %bitcast.26, bf16[512,128]{1,0:T(8,128)(2,1)S(1)} %bitcast.28, f32[512,1]{1,0:T(8,128)S(1)} %copy.15.gain_ref, f32[16,2,128]{2,1,0:T(2,128)S(1)} %all-to-all-done.2.stat_ref, ...), custom_call_target="tpu_custom_call" | custom-call | tf_op jit(solution)/shard_map/pallas_call | solution.py:76
  161.4 0.0 copy-start.6
  161.4 0.0 copy-start.4
  161.4 3.8 %all-to-all-start.3 = ((bf16[16,160,256]{2,1,0:T(8,128)(2,1)}), bf16[16,160,256]{2,1,0:T(8,128)(2,1)S(1)}, u32[]{:S(2)}, u32[]{:S(2)}) async-start(bf16[16,160,256]{2,1,0:T(8,128)(2,1)} %shard_map.101), calls=%async_computation.3 | async-start | bytes 2621440 | tf_op jit(solution)/shard_map/all_to_all | solution.py:170
  165.9 0.0 copy-done.6
  166.0 0.1 fusion.18
  166.1 0.2 reduce_window_sum.11
  166.2 0.2 select_reduce_fusion
  166.4 16.5 %all-to-all-done.3.hidden_ref = bf16[16,160,256]{2,1,0:T(8,128)(2,1)S(1)} async-done(((bf16[16,160,256]{2,1,0:T(8,128)(2,1)}), bf16[16,160,256]{2,1,0:T(8,128)(2,1)S(1)}, u32[]{:S(2)}, u32[]{:S(2)}) %all-to-all-start.3) | async-done | bytes 1310752 | tf_op jit(solution)/shard_map/all_to_all | solution.py:170
  182.9 1.0 shard_map.102
  183.9 13.7 %all-to-all-start.4 = ((bf16[32,8,384]{2,1,0:T(8,128)(2,1)}), bf16[32,8,384]{2,1,0:T(8,128)(2,1)S(1)}, u32[]{:S(2)}, u32[]{:S(2)}) async-start(bf16[32,8,384]{2,1,0:T(8,128)(2,1)} %bitcast.14), calls=%async_computation.4 | async-start | bytes 393216 | tf_op jit(solution)/shard_map/all_to_all | solution.py:177
  197.7 0.0 copy-done.4
  197.7 0.1 fusion.3.slope_ref
  197.8 18.4 %all-to-all-done.4 = bf16[32,8,384]{2,1,0:T(8,128)(2,1)S(1)} async-done(((bf16[32,8,384]{2,1,0:T(8,128)(2,1)}), bf16[32,8,384]{2,1,0:T(8,128)(2,1)S(1)}, u32[]{:S(2)}, u32[]{:S(2)}) %all-to-all-start.4) | async-done | bytes 196640 | tf_op jit(solution)/shard_map/all_to_all | solution.py:177
  216.2 1.0 shard_map.103
  (5 shorter events, 0.1 us)
Async XLA Ops:
  6.5 8.5 %copy-start = (bf16[256,512]{1,0:T(8,128)(2,1)S(1)}, bf16[256,512]{1,0:T(8,128)(2,1)}, u32[]{:S(2)}) copy-start(bf16[256,512]{1,0:T(8,128)(2,1)} %param.10) | copy-start | bytes 786436
  6.5 8.5 %copy-start.7 = (s32[1,128]{1,0:T(1,128)S(1)}, s32[1,128]{1,0:T(1,128)}, u32[]{:S(2)}) copy-start(s32[1,128]{1,0:T(1,128)} %param.15) | copy-start | bytes 1540
  8.6 31.1 %all-to-all-start = ((bf16[4,256,512]{2,1,0:T(8,128)(2,1)}), bf16[4,256,512]{2,1,0:T(8,128)(2,1)S(1)}, u32[]{:S(2)}, u32[]{:S(2)}) async-start(bf16[4,256,512]{2,1,0:T(8,128)(2,1)} %broadcast_in_dim.16), calls=%async_computation | async-start | bytes 2097152 | tf_op jit(solution)/shard_map/all_to_all | solution.py:127
  15.0 109.7 %all-gather.4.cloned.1.call-start = ((), (), s32[]{:S(2)}) async-start(), calls=%async_computation.5 | async-start | bytes 5406720 | tf_op jit(solution)/shard_map/all_gather | solution.py:132
  39.7 38.8 %collective-permute-start = (bf16[4,256,512]{2,1,0:T(8,128)(2,1)S(1)}, bf16[4,256,512]{2,1,0:T(8,128)(2,1)S(1)}, u32[]{:S(2)}, u32[]{:S(2)}) collective-permute-start(bf16[4,256,512]{2,1,0:T(8,128)(2,1)S(1)} %all-to-all-done.own_ref), channel_id=1, source_target_pairs={{0,16},{16,0},{1,17},{17,1},{2,18},{18,2},{3,19},{19,3},{4,20},{20... | collective-permute-start | bytes 3145736 | tf_op jit(solution)/shard_map/ppermute | solution.py:133
  112.9 12.5 %copy-start.2 = (bf16[256,512]{1,0:T(8,128)(2,1)S(1)}, bf16[256,512]{1,0:T(8,128)(2,1)}, u32[]{:S(2)}) copy-start(bf16[256,512]{1,0:T(8,128)(2,1)} %param.13) | copy-start | bytes 786436
  112.9 13.5 %copy-start.5 = (f32[512]{0:T(512)S(1)}, f32[512]{0:T(512)}, u32[]{:S(2)}) copy-start(f32[512]{0:T(512)} %param.14) | copy-start | bytes 6148
  112.9 36.9 %copy-start.3 = (bf16[256,512]{1,0:T(8,128)(2,1)S(1)}, bf16[256,512]{1,0:T(8,128)(2,1)}, u32[]{:S(2)}) copy-start(bf16[256,512]{1,0:T(8,128)(2,1)} %param.12) | copy-start | bytes 786436
  124.7 1.7 collective-permute-start.1
  127.2 29.1 %all-to-all-start.2 = ((f32[16,2,128]{2,1,0:T(2,128)}), f32[16,2,128]{2,1,0:T(2,128)S(1)}, u32[]{:S(2)}, u32[]{:S(2)}) async-start(f32[16,2,128]{2,1,0:T(2,128)} %broadcast_in_dim.32), calls=%async_computation.2 | async-start | bytes 32768 | tf_op jit(solution)/shard_map/all_to_all | solution.py:164
  156.2 2.5 %copy-start.1 = (bf16[5120,512]{1,0:T(8,128)(2,1)S(1)}, bf16[5120,512]{1,0:T(8,128)(2,1)}, u32[]{:S(2)}) copy-start(bf16[5120,512]{1,0:T(8,128)(2,1)} %all-gather.4.cloned.1.call-done) | copy-start | bytes 15728644
  161.4 4.5 %copy-start.6 = (s32[1,128]{1,0:T(1,128)S(1)}, s32[1,128]{1,0:T(1,128)}, u32[]{:S(2)}) copy-start(s32[1,128]{1,0:T(1,128)} %param.17) | copy-start | bytes 1540
  161.4 36.2 %copy-start.4 = (bf16[192,320]{1,0:T(8,128)(2,1)S(1)}, bf16[192,320]{1,0:T(8,128)(2,1)}, u32[]{:S(2)}) copy-start(bf16[192,320]{1,0:T(8,128)(2,1)} %param.19) | copy-start | bytes 368644
  161.4 21.5 %all-to-all-start.3 = ((bf16[16,160,256]{2,1,0:T(8,128)(2,1)}), bf16[16,160,256]{2,1,0:T(8,128)(2,1)S(1)}, u32[]{:S(2)}, u32[]{:S(2)}) async-start(bf16[16,160,256]{2,1,0:T(8,128)(2,1)} %shard_map.101), calls=%async_computation.3 | async-start | bytes 2621440 | tf_op jit(solution)/shard_map/all_to_all | solution.py:170
  183.9 32.3 %all-to-all-start.4 = ((bf16[32,8,384]{2,1,0:T(8,128)(2,1)}), bf16[32,8,384]{2,1,0:T(8,128)(2,1)S(1)}, u32[]{:S(2)}, u32[]{:S(2)}) async-start(bf16[32,8,384]{2,1,0:T(8,128)(2,1)} %bitcast.14), calls=%async_computation.4 | async-start | bytes 393216 | tf_op jit(solution)/shard_map/all_to_all | solution.py:177
Sparse Core Ops, SparseCore 0:
  39.8 84.8 all-gather.3

commit v12 on v6

v12 whole, which is shorter than its diff:
```python
import functools

import jax
import jax.numpy as jnp
from jax import lax
from jax.experimental import pallas as pl
from jax.experimental.pallas import tpu as pltpu
from jax.sharding import Mesh
from jax.sharding import PartitionSpec as P

D = 8192
NORM_EPS = 1e-06
MIB = 1024 * 1024
LANES = 128
DP = ("zh", "zl", "core")
TP = ("x", "y")


def gelu_slope(pre):
    value = pre.astype(jnp.float32)
    cdf_part = 0.5 * (1.0 + lax.erf(value * 0.7071067811865476))
    pdf_part = jnp.exp(-0.5 * value * value) * 0.3989422804014327
    return cdf_part + value * pdf_part


def own_kernel(rows_ref, weight_ref, out_ref, turned_ref):
    parts, count, depth = rows_ref.shape
    turned_ref[...] = rows_ref[...].reshape(parts * count, depth).T
    for block in range(weight_ref.shape[0]):
        product = jnp.dot(weight_ref[block], turned_ref[...], preferred_element_type=jnp.float32)
        out_ref[block] = product.astype(out_ref.dtype)


def join_kernel(place_ref, own_ref, turned_ref, weight_ref, out_ref):
    parts, blocks, _, count = out_ref.shape
    height = weight_ref.shape[1]
    core, shift = place_ref[0], place_ref[1]
    spots = [
        pl.ds(pl.multiple_of(place * height, height), height) for place in (core, 1 - core)
    ]
    for block in range(blocks):
        product = jnp.dot(weight_ref[block], turned_ref[...], preferred_element_type=jnp.float32)
        halves = (own_ref[block], product.astype(out_ref.dtype))
        for spot, half in zip(spots, halves):
            for part in range(parts):
                out_ref[lax.rem(part + shift, parts), block, spot] = half[
                    :, part * count : (part + 1) * count
                ]


def in_vmem(kernel, out_shape, *args, scalars=False):
    specs = [pl.BlockSpec(memory_space=pltpu.VMEM) for _ in args]
    if scalars:
        specs[0] = pl.BlockSpec(memory_space=pltpu.SMEM)
    return pl.pallas_call(
        kernel,
        in_specs=specs,
        out_specs=jax.tree.map(lambda _: pl.BlockSpec(memory_space=pltpu.VMEM), out_shape),
        out_shape=out_shape,
        compiler_params=pltpu.CompilerParams(vmem_limit_bytes=24 * MIB),
    )(*args)


def stat_kernel(grad_ref, scaled_ref, square_ref, out_ref):
    inner = jnp.sum(
        grad_ref[...].astype(jnp.float32) * scaled_ref[...], axis=0, keepdims=True
    )
    stats = jnp.concatenate([square_ref[...], inner], axis=0)
    for share in range(out_ref.shape[0]):
        out_ref[share] = stats


def handoff_kernel(capacity, grad_ref, input_ref, resid_ref, gain_ref, stat_ref, target_ref, out_ref):
    width, count = grad_ref.shape
    stats = jnp.sum(stat_ref[...], axis=0)
    inverse = lax.rsqrt(stats[0:1] / D + NORM_EPS)
    factor = inverse * inverse * inverse * stats[1:2] / D
    scaled = gain_ref[...] * grad_ref[...].astype(jnp.float32)
    handoff = (
        resid_ref[...].astype(jnp.float32)
        + inverse * scaled
        - input_ref[...].astype(jnp.float32) * factor
    ).astype(jnp.bfloat16)
    place = lax.broadcasted_iota(jnp.int32, (out_ref.shape[0], count), 0) - target_ref[...]
    total = jnp.zeros(out_ref.shape, jnp.float32)
    for block in range(width // LANES):
        hot = (place == block * capacity).astype(jnp.bfloat16)
        total += lax.dot_general(
            hot,
            handoff[block * LANES : (block + 1) * LANES],
            (((1,), (1,)), ((), ())),
            preferred_element_type=jnp.float32,
        )
    out_ref[...] = total.astype(out_ref.dtype)


def merge_kernel(capacity, box_ref, weight_ref, out_ref):
    width = weight_ref.shape[2]
    rows = out_ref.shape[2] // 2
    chunks = width // LANES
    box = box_ref[...]
    row = lax.broadcasted_iota(jnp.int32, (rows, box.shape[0]), 0)
    spot = lax.broadcasted_iota(jnp.int32, (rows, box.shape[0]), 1)
    source = (row * 10923) >> 16
    ahead = spot - (row + source * (capacity * (chunks - 1)))
    pieces = []
    for block in range(chunks):
        hot = (ahead == block * capacity).astype(jnp.bfloat16)
        piece = jnp.dot(hot, box, preferred_element_type=jnp.float32)
        pieces.append(piece.T.astype(jnp.bfloat16))
    turned = jnp.concatenate(pieces, axis=0)
    for share in range(out_ref.shape[0]):
        for half in range(2):
            product = jnp.dot(
                weight_ref[2 * share + half], turned, preferred_element_type=jnp.float32
            )
            out_ref[share, :, half * rows : (half + 1) * rows] = product.astype(out_ref.dtype)


def local(
    grad_query,
    query_weight,
    grad_resid,
    embeds,
    norm_gain,
    img_pos,
    img_count,
    img_dest,
    merge_weight,
    merge_pre,
):
    groups = lax.axis_size(DP)
    shares = lax.axis_size(TP)
    side = lax.axis_size("zh")
    rows, columns = merge_pre.shape
    capacity = rows // groups
    positions = img_pos[0]
    image_count = positions.shape[0]
    width = embeds.shape[1]

    own = lax.all_gather(query_weight, "zl", axis=0)
    picked = lax.all_gather(jnp.take(grad_query, positions, axis=0, mode="clip"), "zh", axis=0)
    merge_weight, picked = lax.optimization_barrier((merge_weight, picked))
    merge_full = lax.all_gather(merge_weight, DP, axis=0)
    inputs = jnp.take(embeds, positions, axis=0, mode="clip").T
    residual = jnp.take(grad_resid, positions, axis=0, mode="clip").T
    gain = norm_gain[:, None]
    wide = inputs.astype(jnp.float32)
    squares = jnp.sum(wide * wide, axis=0)
    is_live = jnp.arange(image_count, dtype=jnp.int32) < img_count[0]
    target_dev = img_dest[0]
    dest_hot = (
        (target_dev[:, None] == jnp.arange(groups, dtype=jnp.int32)[None, :]) & is_live[:, None]
    ).astype(jnp.int32)
    earlier = jnp.cumsum(dest_hot, axis=0) - dest_hot
    slot_index = jnp.sum(earlier * dest_hot, axis=1)
    pitch = capacity * (width // LANES)
    target = jnp.where(is_live, target_dev * pitch + slot_index, -groups * pitch)
    slope = gelu_slope(merge_pre)

    other = lax.ppermute(own, "core", [(0, 1), (1, 0)])
    place = jnp.stack([lax.axis_index("core"), lax.axis_index("zh")]).astype(jnp.int32)
    blocks, height, depth = own.shape
    own_value, turned = in_vmem(
        own_kernel,
        [
            jax.ShapeDtypeStruct((blocks, height, side * image_count), jnp.bfloat16),
            jax.ShapeDtypeStruct((depth, side * image_count), jnp.bfloat16),
        ],
        picked,
        own,
    )
    partial_value = in_vmem(
        join_kernel,
        jax.ShapeDtypeStruct((side, blocks, 2 * height, image_count), jnp.bfloat16),
        place,
        own_value,
        turned,
        other,
        scalars=True,
    )
    partial_value = partial_value.reshape(shares, width, image_count)
    swapped = lax.all_to_all(partial_value, TP, 0, 0, tiled=True)
    normal_grad = jnp.sum(swapped.astype(jnp.float32), axis=0).astype(jnp.bfloat16)
    exchange = [
        (h * side + (a + h) % side, a * side + h) for a in range(side) for h in range(side)
    ]
    normal_grad = lax.ppermute(normal_grad, ("zh", "x"), exchange)
    stats = in_vmem(
        stat_kernel,
        jax.ShapeDtypeStruct((shares, 2, image_count), jnp.float32),
        normal_grad,
        gain * wide,
        squares[None],
    )
    stats = lax.all_to_all(stats, TP, 0, 0, tiled=True)
    outbox = in_vmem(
        functools.partial(handoff_kernel, capacity),
        jax.ShapeDtypeStruct((groups * pitch, LANES), jnp.bfloat16),
        normal_grad,
        inputs,
        residual,
        gain,
        stats,
        target[None],
    )
    received = lax.all_to_all(outbox.reshape(groups, pitch, LANES), DP, 0, 0, tiled=True)
    partial_hidden = in_vmem(
        functools.partial(merge_kernel, capacity),
        jax.ShapeDtypeStruct((shares, merge_weight.shape[0], 2 * rows), jnp.bfloat16),
        received.reshape(groups * pitch, LANES),
        merge_full,
    )
    hidden = lax.all_to_all(partial_hidden, TP, 0, 0, tiled=True)
    hidden = jnp.sum(hidden.astype(jnp.float32), axis=0)
    hidden = jnp.concatenate([hidden[:, :rows].T, hidden[:, rows:].T], axis=1)
    return hidden * slope


def solution(mesh):
    split = Mesh(mesh.devices.reshape(4, 4, 2, 4, 4), DP + TP)
    in_specs = (
        P(DP, TP),
        P(DP, TP),
        P(DP, TP),
        P(DP, TP),
        P(TP),
        P(DP, None),
        P(DP),
        P(DP, None),
        P(DP, TP),
        P(DP, TP),
    )
    out_specs = P(DP, TP)
    return jax.shard_map(local, mesh=split, in_specs=in_specs, out_specs=out_specs, check_vma=False)
```

time: 219 us -> 206 us (0.941)
  waiting for transfers between devices: 86.4 us -> 52.2 us
  blocking collectives: 71.7 us -> 89.2 us
  starting transfers between devices: 27.3 us -> 32.6 us
    all_gather x1, waiting for transfers between devices: 49.5 us -> 18.4 us  [local(): own = lax.all_gather(query_weight, 'zl', axis=0)]
    all_gather x1, blocking collectives: 16.3 us -> 31.2 us  [local(): lax.all_gather(jnp.take(grad_query, positions, axis=0, mode='clip'), 'zh'...]
    all_to_all x1, starting transfers between devices: 17.5 us -> 22.5 us  [local(): stats = lax.all_to_all(stats, TP, 0, 0, tiled=True)]
    all_to_all x1, blocking collectives: 28.7 us -> 31.3 us  [local(): lax.all_to_all(outbox.reshape(groups, pitch, LANES), DP, 0, 0, tiled=True)]
    unnamed x15 -> x18, local copies, waits for them, and re-layouts: 4.77 us -> 4.24 us
    pallas_call x3 -> x5, Pallas kernels: 6.56 us -> 6.85 us  [in_vmem(): pl.pallas_call(kernel, in_specs=specs, out_specs=jax.tree.map(lambda _: p...]
  transfers between devices with their start and end apart: 6 -> 6, of which waited for: 4 -> 4; matrix products, arithmetic and copies ran while one was open for 3% -> 2% of each run, Pallas kernels for 2% -> 2%
where the time goes in v12:
time: 206 us; the launch traced here: 205 us
  blocking collectives  89.2 us (43%)
  waiting for transfers between devices  52.2 us (25%)
  starting transfers between devices  32.6 us (16%)
  between operations  14.3 us (7%)
  local copies, waits for them, and re-layouts  7.26 us (4%)
  Pallas kernels  6.85 us (3%)
  other arithmetic  2.78 us (1%)
    all_to_all x1, blocking collectives, local(): lax.all_to_all(outbox.reshape(groups, pitch, LANES), DP, 0, 0, tiled=True)  31.3 us
    all_gather x1, blocking collectives, local(): lax.all_gather(jnp.take(grad_query, positions, axis=0, mode='clip'), 'zh'...  31.2 us
    all_to_all x1, waiting for transfers between devices, local(): swapped = lax.all_to_all(partial_value, TP, 0, 0, tiled=True)  27.4 us
    all_to_all x1, blocking collectives, local(): hidden = lax.all_to_all(partial_hidden, TP, 0, 0, tiled=True)  26.8 us
    all_to_all x1, starting transfers between devices, local(): stats = lax.all_to_all(stats, TP, 0, 0, tiled=True)  22.5 us
    all_gather x1, waiting for transfers between devices, local(): own = lax.all_gather(query_weight, 'zl', axis=0)  18.4 us
    all_to_all x1, starting transfers between devices, local(): swapped = lax.all_to_all(partial_value, TP, 0, 0, tiled=True)  6.88 us
    pallas_call x5, Pallas kernels, in_vmem(): pl.pallas_call(kernel, in_specs=specs, out_specs=jax.tree.map(lambda _: p...  6.85 us
  transfers between devices with their start and end apart: 6, of which 4 were waited for; matrix products, arithmetic and copies ran while one was open for 2% of the time, Pallas kernels for 2%

profile of v12, /device:TPU:1, one launch (start us, length us, event | category | flops | bytes accessed | tf_op | source)
XLA Modules:
  0.0 205.1 jit_solution(6754226469486853252)
XLA Ops:
  6.5 0.0 copy-start
  6.5 0.0 all-gather.6.cloned.1.call-start
  6.5 0.7 all-gather.6.cloned.1.call-update
  7.3 0.0 all-gather.8.cloned.1.call-start
  7.3 0.7 pad_clamp_fusion
  8.0 0.0 copy-done
  8.0 0.8 gather_fusion
  8.8 31.2 %all-gather = bf16[512,512]{1,0:T(8,128)(2,1)S(1)} all-gather(bf16[128,512]{1,0:T(8,128)(2,1)S(1)} %gather_fusion), channel_id=2, replica_groups=mesh['zh'=4,'zl'=4,'core'=2,'x'=4,'y'=4] {'zh'}, dimensions={0}, use_global_device_ids=true | all-gather | bytes 655360 | tf_op jit(solution)/shard_map/all_gather | solution.py:142
  40.0 0.0 all-gather.8.cloned.1.call-update
  40.0 18.4 %all-gather.6.cloned.1.call-done = bf16[1024,512]{1,0:T(8,128)(2,1)} async-done(((bf16[256,512]{1,0:T(8,128)(2,1)}), bf16[1024,512]{1,0:T(8,128)(2,1)}) %all-gather.6.cloned.1.call-update) | async-done | bytes 1048592 | tf_op jit(solution)/shard_map/all_gather | solution.py:141
  58.4 2.5 %collective-permute-start = (bf16[4,256,512]{2,1,0:T(8,128)(2,1)}, bf16[4,256,512]{2,1,0:T(8,128)(2,1)S(1)}, u32[]{:S(2)}, u32[]{:S(2)}) collective-permute-start(bf16[4,256,512]{2,1,0:T(8,128)(2,1)} %bitcast.28), channel_id=1, source_target_pairs={{0,16},{16,0},{1,17},{17,1},{2,18},{18,2},{3,19},{19,3},{4,20},{20... | collective-permute-start | bytes 3145736 | tf_op jit(solution)/shard_map/ppermute | solution.py:161
  60.9 0.1 pad_add_fusion.place_ref
  61.0 0.0 copy-start.2
  61.0 1.2 copy-done.2
  62.2 0.8 shard_map.100
  63.0 0.4 collective-permute-done.weight_ref
  63.4 2.8 %shard_map.101 = bf16[4,4,512,128]{3,2,1,0:T(8,128)(2,1)} custom-call(s32[2]{0:T(128)S(1)} %pad_add_fusion.place_ref, bf16[4,256,512]{2,1,0:T(8,128)(2,1)S(1)} %get-tuple-element.10.own_ref, bf16[512,512]{1,0:T(8,128)(2,1)S(1)} %get-tuple-element.11.turned_ref, bf16[4,256,512]{2,1,0:T(8,128)(2,1)S(1)} %collective-permute-done.weight_ref), custom_call_target="tpu_custom_call" | custom-call | tf_op jit(solution)/shard_map/pallas_call | solution.py:55
  66.2 0.0 copy-start.3
  66.2 0.0 copy-start.6
  66.2 6.9 %all-to-all-start = ((bf16[16,512,128]{2,1,0:T(8,128)(2,1)}), bf16[16,512,128]{2,1,0:T(8,128)(2,1)S(1)}, u32[]{:S(2)}, u32[]{:S(2)}) async-start(bf16[16,512,128]{2,1,0:T(8,128)(2,1)} %bitcast.5), calls=%async_computation | async-start | bytes 4194304 | tf_op jit(solution)/shard_map/all_to_all | solution.py:183
  73.1 0.0 copy-done.3
  73.1 0.0 copy-start.7
  73.1 0.8 gather_fusion.1
  73.9 0.0 copy-start.4
  73.9 0.1 copy.21
  74.7 0.0 copy-done.6
  74.7 0.1 fusion.7
  74.9 27.4 %all-to-all-done = bf16[16,512,128]{2,1,0:T(8,128)(2,1)S(1)} async-done(((bf16[16,512,128]{2,1,0:T(8,128)(2,1)}), bf16[16,512,128]{2,1,0:T(8,128)(2,1)S(1)}, u32[]{:S(2)}, u32[]{:S(2)}) %all-to-all-start) | async-done | bytes 2097184 | tf_op jit(solution)/shard_map/all_to_all | solution.py:183
  102.3 0.3 reduce_sum.41
  102.5 0.7 collective-permute-start.1
  103.2 0.0 copy-done.7
  103.2 0.1 fusion.9
  103.3 0.2 reduce_window_sum.11
  103.5 0.2 select_reduce_fusion
  103.7 0.0 collective-permute-done.1.grad_ref
  103.7 0.7 shard_map.102
  104.4 22.5 %all-to-all-start.1 = ((f32[16,2,128]{2,1,0:T(2,128)}), f32[16,2,128]{2,1,0:T(2,128)S(1)}, u32[]{:S(2)}, u32[]{:S(2)}) async-start(f32[16,2,128]{2,1,0:T(2,128)} %shard_map.102), calls=%async_computation.1 | async-start | bytes 32768 | tf_op jit(solution)/shard_map/all_to_all | solution.py:196
  126.9 0.0 copy-done.4
  126.9 0.8 gather_fusion.2
  127.8 0.1 copy.22
  127.9 0.1 copy.23.gain_ref
  128.1 5.3 %all-to-all-done.1.stat_ref = f32[16,2,128]{2,1,0:T(2,128)S(1)} async-done(((f32[16,2,128]{2,1,0:T(2,128)}), f32[16,2,128]{2,1,0:T(2,128)S(1)}, u32[]{:S(2)}, u32[]{:S(2)}) %all-to-all-start.1) | async-done | bytes 16416 | tf_op jit(solution)/shard_map/all_to_all | solution.py:196
  133.4 0.5 shard_map.103
  133.8 31.3 %all_to_all.20 = bf16[32,24,128]{2,1,0:T(8,128)(2,1)S(1)} all-to-all(bf16[32,24,128]{2,1,0:T(8,128)(2,1)S(1)} %bitcast.30), channel_id=1, replica_groups=mesh['zh'=4,'zl'=4,'core'=2,'x'=4,'y'=4] {'zh','zl','core'}, dimensions={0} | all-to-all | bytes 393216 | tf_op jit(solution)/shard_map/all_to_all | solution.py:207
  165.1 0.0 all-gather.8.cloned.1.call-done
  165.1 0.0 copy-start.1
  165.1 2.5 %copy-done.1 = bf16[5120,512]{1,0:T(8,128)(2,1)S(1)} copy-done((bf16[5120,512]{1,0:T(8,128)(2,1)S(1)}, bf16[5120,512]{1,0:T(8,128)(2,1)}, u32[]{:S(2)}) %copy-start.1) | copy-done | bytes 5242904
  167.6 2.1 %shard_map.104 = bf16[16,160,384]{2,1,0:T(8,128)(2,1)S(1)} custom-call(bf16[768,128]{1,0:T(8,128)(2,1)S(1)} %bitcast.31, bf16[32,160,512]{2,1,0:T(8,128)(2,1)S(1)} %bitcast.25), custom_call_target="tpu_custom_call" | custom-call | tf_op jit(solution)/shard_map/pallas_call | solution.py:55
  169.7 26.8 %all_to_all.21 = bf16[16,160,384]{2,1,0:T(8,128)(2,1)S(1)} all-to-all(bf16[16,160,384]{2,1,0:T(8,128)(2,1)S(1)} %shard_map.104), channel_id=1, replica_groups=mesh['zh'=4,'zl'=4,'core'=2,'x'=4,'y'=4] {'x','y'}, dimensions={0} | all-to-all | bytes 3932160 | tf_op jit(solution)/shard_map/all_to_all | solution.py:214
  196.5 0.0 copy-start.5
  196.5 0.3 convert_reduce_fusion
  196.8 0.1 fusion.10
  196.9 0.1 copy.26
  197.0 0.1 copy.27
  197.1 0.3 copy-done.5
  197.4 0.9 fusion.4
  (2 shorter events, 0.0 us)
Async XLA Ops:
  6.5 1.4 copy-start
  6.5 51.9 %all-gather.6.cloned.1.call-start = ((), (), s32[]{:S(2)}) async-start(), calls=%async_computation.4 | async-start | bytes 1310720 | tf_op jit(solution)/shard_map/all_gather | solution.py:141
  7.3 157.8 %all-gather.8.cloned.1.call-start = ((), (), s32[]{:S(2)}) async-start(), calls=%async_computation.5 | async-start | bytes 5406720 | tf_op jit(solution)/shard_map/all_gather | solution.py:144
  58.4 4.9 %collective-permute-start = (bf16[4,256,512]{2,1,0:T(8,128)(2,1)}, bf16[4,256,512]{2,1,0:T(8,128)(2,1)S(1)}, u32[]{:S(2)}, u32[]{:S(2)}) collective-permute-start(bf16[4,256,512]{2,1,0:T(8,128)(2,1)} %bitcast.28), channel_id=1, source_target_pairs={{0,16},{16,0},{1,17},{17,1},{2,18},{18,2},{3,19},{19,3},{4,20},{20... | collective-permute-start | bytes 3145736 | tf_op jit(solution)/shard_map/ppermute | solution.py:161
  61.0 1.2 copy-start.2
  66.2 6.9 %copy-start.3 = (bf16[256,512]{1,0:T(8,128)(2,1)S(1)}, bf16[256,512]{1,0:T(8,128)(2,1)}, u32[]{:S(2)}) copy-start(bf16[256,512]{1,0:T(8,128)(2,1)} %param.13) | copy-start | bytes 786436
  66.2 8.6 %copy-start.6 = (f32[512]{0:T(512)S(1)}, f32[512]{0:T(512)}, u32[]{:S(2)}) copy-start(f32[512]{0:T(512)} %param.14) | copy-start | bytes 6148
  66.2 36.1 %all-to-all-start = ((bf16[16,512,128]{2,1,0:T(8,128)(2,1)}), bf16[16,512,128]{2,1,0:T(8,128)(2,1)S(1)}, u32[]{:S(2)}, u32[]{:S(2)}) async-start(bf16[16,512,128]{2,1,0:T(8,128)(2,1)} %bitcast.5), calls=%async_computation | async-start | bytes 4194304 | tf_op jit(solution)/shard_map/all_to_all | solution.py:183
  73.1 30.2 %copy-start.7 = (s32[1,128]{1,0:T(1,128)S(1)}, s32[1,128]{1,0:T(1,128)}, u32[]{:S(2)}) copy-start(s32[1,128]{1,0:T(1,128)} %param.17) | copy-start | bytes 1540
  73.9 53.0 %copy-start.4 = (bf16[256,512]{1,0:T(8,128)(2,1)S(1)}, bf16[256,512]{1,0:T(8,128)(2,1)}, u32[]{:S(2)}) copy-start(bf16[256,512]{1,0:T(8,128)(2,1)} %param.12) | copy-start | bytes 786436
  102.5 1.1 collective-permute-start.1
  104.4 29.0 %all-to-all-start.1 = ((f32[16,2,128]{2,1,0:T(2,128)}), f32[16,2,128]{2,1,0:T(2,128)S(1)}, u32[]{:S(2)}, u32[]{:S(2)}) async-start(f32[16,2,128]{2,1,0:T(2,128)} %shard_map.102), calls=%async_computation.1 | async-start | bytes 32768 | tf_op jit(solution)/shard_map/all_to_all | solution.py:196
  165.1 2.5 %copy-start.1 = (bf16[5120,512]{1,0:T(8,128)(2,1)S(1)}, bf16[5120,512]{1,0:T(8,128)(2,1)}, u32[]{:S(2)}) copy-start(bf16[5120,512]{1,0:T(8,128)(2,1)} %all-gather.8.cloned.1.call-done) | copy-start | bytes 15728644
  196.5 0.9 copy-start.5
Sparse Core Ops, SparseCore 0:
  9.5 48.9 all-gather.5
  60.6 74.8 all-gather.7

commit v13 on v12

--- a/solution.py
+++ b/solution.py
@@ -140,7 +140,9 @@
 
     own = lax.all_gather(query_weight, "zl", axis=0)
     picked = lax.all_gather(jnp.take(grad_query, positions, axis=0, mode="clip"), "zh", axis=0)
-    merge_weight, picked = lax.optimization_barrier((merge_weight, picked))
+    merge_weight, embeds, grad_resid, img_dest, merge_pre, picked = lax.optimization_barrier(
+        (merge_weight, embeds, grad_resid, img_dest, merge_pre, picked)
+    )
     merge_full = lax.all_gather(merge_weight, DP, axis=0)
     inputs = jnp.take(embeds, positions, axis=0, mode="clip").T
     residual = jnp.take(grad_resid, positions, axis=0, mode="clip").T
@@ -158,6 +160,12 @@
     target = jnp.where(is_live, target_dev * pitch + slot_index, -groups * pitch)
     slope = gelu_slope(merge_pre)
 
+    scaled_input = gain * wide
+    own, picked, inputs, residual, gain, squares, scaled_input, target, slope = (
+        lax.optimization_barrier(
+            (own, picked, inputs, residual, gain, squares, scaled_input, target, slope)
+        )
+    )
     other = lax.ppermute(own, "core", [(0, 1), (1, 0)])
     place = jnp.stack([lax.axis_index("core"), lax.axis_index("zh")]).astype(jnp.int32)
     blocks, height, depth = own.shape
@@ -190,7 +198,7 @@
         stat_kernel,
         jax.ShapeDtypeStruct((shares, 2, image_count), jnp.float32),
         normal_grad,
-        gain * wide,
+        scaled_input,
         squares[None],
     )
     stats = lax.all_to_all(stats, TP, 0, 0, tiled=True)

time: 206 us -> 204 us (level)
  blocking collectives: 89.2 us -> 123 us
  waiting for transfers between devices: 52.2 us -> 21.5 us
  starting transfers between devices: 32.6 us -> 26.7 us
    all_to_all x0 -> x1, blocking collectives: none -> 33.8 us  [local(): swapped = lax.all_to_all(partial_value, TP, 0, 0, tiled=True)]
    all_to_all x1 -> x0, waiting for transfers between devices: 27.4 us -> none  [local(): swapped = lax.all_to_all(partial_value, TP, 0, 0, tiled=True)]
    all_to_all x1 -> x0, starting transfers between devices: 6.88 us -> none  [local(): swapped = lax.all_to_all(partial_value, TP, 0, 0, tiled=True)]
    all_gather x1, waiting for transfers between devices: 18.4 us -> 14.2 us  [local(): own = lax.all_gather(query_weight, 'zl', axis=0)]
  transfers between devices with their start and end apart: 6 -> 5, of which waited for: 4 -> 3; matrix products, arithmetic and copies ran while one was open for 2% -> 3% of each run, Pallas kernels for 2% -> 2%
where the time goes in v13:
time: 204 us; the launch traced here: 202 us
  blocking collectives  123 us (60%)
  starting transfers between devices  26.7 us (13%)
  waiting for transfers between devices  21.5 us (11%)
  between operations  14.3 us (7%)
  local copies, waits for them, and re-layouts  8.33 us (4%)
  Pallas kernels  5.47 us (3%)
  other arithmetic  2.81 us (1%)
    all_to_all x1, blocking collectives, local(): swapped = lax.all_to_all(partial_value, TP, 0, 0, tiled=True)  33.8 us
    all_gather x1, blocking collectives, local(): lax.all_gather(jnp.take(grad_query, positions, axis=0, mode='clip'), 'zh'...  31.3 us
    all_to_all x1, blocking collectives, local(): lax.all_to_all(outbox.reshape(groups, pitch, LANES), DP, 0, 0, tiled=True)  31.3 us
    all_to_all x1, blocking collectives, local(): hidden = lax.all_to_all(partial_hidden, TP, 0, 0, tiled=True)  26.7 us
    all_to_all x1, starting transfers between devices, local(): stats = lax.all_to_all(stats, TP, 0, 0, tiled=True)  23.6 us
    all_gather x1, waiting for transfers between devices, local(): own = lax.all_gather(query_weight, 'zl', axis=0)  14.2 us
    all_to_all x1, waiting for transfers between devices, local(): stats = lax.all_to_all(stats, TP, 0, 0, tiled=True)  6.29 us
    pallas_call x5, Pallas kernels, in_vmem(): pl.pallas_call(kernel, in_specs=specs, out_specs=jax.tree.map(lambda _: p...  5.47 us
  transfers between devices with their start and end apart: 5, of which 3 were waited for; matrix products, arithmetic and copies ran while one was open for 3% of the time, Pallas kernels for 2%

profile of v13, /device:TPU:1, one launch (start us, length us, event | category | flops | bytes accessed | tf_op | source)
XLA Modules:
  0.0 202.3 jit_solution(6642275363696537257)
XLA Ops:
  6.5 0.0 copy-start
  6.5 0.0 copy-start.3
  6.5 0.0 copy-start.4
  6.5 0.0 all-gather.6.cloned.1.call-start
  6.5 0.7 all-gather.6.cloned.1.call-update
  7.3 0.0 all-gather.8.cloned.1.call-start
  7.3 0.7 pad_clamp_fusion
  8.0 0.0 copy-done
  8.0 0.8 gather_fusion
  8.8 0.0 copy-start.6
  8.8 0.0 copy-start.8
  8.8 0.0 copy-start.7
  8.9 31.3 %all-gather.1 = bf16[512,512]{1,0:T(8,128)(2,1)S(1)} all-gather(bf16[128,512]{1,0:T(8,128)(2,1)S(1)} %gather_fusion), channel_id=3, replica_groups=mesh['zh'=4,'zl'=4,'core'=2,'x'=4,'y'=4] {'zh'}, dimensions={0}, use_global_device_ids=true | all-gather | bytes 655360 | tf_op jit(solution)/shard_map/all_gather | solution.py:142
  40.2 0.0 all-gather.8.cloned.1.call-update
  40.2 0.0 copy-done.3
  40.2 0.8 gather_fusion.1
  41.1 0.1 copy.16
  41.2 0.0 copy-done.4
  41.2 0.8 gather_fusion.2
  42.0 0.1 copy.17
  42.8 0.0 copy-done.6
  42.8 0.1 copy.18
  43.0 0.0 copy-done.8
  43.0 0.1 fusion.8
  43.1 0.2 reduce_window_sum.11
  43.3 0.2 select_reduce_fusion
  43.5 0.0 copy-done.7
  43.5 0.1 convert_multiply_fusion.4
  43.6 0.9 fusion.3
  44.5 14.2 %all-gather.6.cloned.1.call-done = bf16[1024,512]{1,0:T(8,128)(2,1)} async-done(((bf16[256,512]{1,0:T(8,128)(2,1)}), bf16[1024,512]{1,0:T(8,128)(2,1)}) %all-gather.6.cloned.1.call-update) | async-done | bytes 1048592 | tf_op jit(solution)/shard_map/all_gather | solution.py:141
  58.6 2.5 %collective-permute-start = (bf16[4,256,512]{2,1,0:T(8,128)(2,1)}, bf16[4,256,512]{2,1,0:T(8,128)(2,1)S(1)}, u32[]{:S(2)}, u32[]{:S(2)}) collective-permute-start(bf16[4,256,512]{2,1,0:T(8,128)(2,1)} %bitcast.29), channel_id=1, source_target_pairs={{0,16},{16,0},{1,17},{17,1},{2,18},{18,2},{3,19},{19,3},{4,20},{20... | collective-permute-start | bytes 3145736 | tf_op jit(solution)/shard_map/ppermute | solution.py:169
  61.1 0.1 pad_add_fusion.place_ref
  61.2 0.0 copy-start.2
  61.2 1.2 copy-done.2
  62.4 0.8 shard_map.100
  63.2 0.4 collective-permute-done.weight_ref
  63.6 1.4 shard_map.101
  65.0 33.8 %all_to_all.20 = bf16[16,512,128]{2,1,0:T(8,128)(2,1)S(1)} all-to-all(bf16[16,512,128]{2,1,0:T(8,128)(2,1)S(1)} %bitcast.25), channel_id=1, replica_groups=mesh['zh'=4,'zl'=4,'core'=2,'x'=4,'y'=4] {'x','y'}, dimensions={0} | all-to-all | bytes 4194304 | tf_op jit(solution)/shard_map/all_to_all | solution.py:191
  98.7 0.3 reduce_sum.41
  99.0 0.7 collective-permute-start.1
  99.7 0.0 collective-permute-done.1.grad_ref
  99.7 0.7 shard_map.102
  100.4 23.6 %all-to-all-start.1 = ((f32[16,2,128]{2,1,0:T(2,128)}), f32[16,2,128]{2,1,0:T(2,128)S(1)}, u32[]{:S(2)}, u32[]{:S(2)}) async-start(f32[16,2,128]{2,1,0:T(2,128)} %shard_map.102), calls=%async_computation.1 | async-start | bytes 32768 | tf_op jit(solution)/shard_map/all_to_all | solution.py:204
  124.0 0.1 copy.19.gain_ref
  124.1 6.3 %all-to-all-done.1.stat_ref = f32[16,2,128]{2,1,0:T(2,128)S(1)} async-done(((f32[16,2,128]{2,1,0:T(2,128)}), f32[16,2,128]{2,1,0:T(2,128)S(1)}, u32[]{:S(2)}, u32[]{:S(2)}) %all-to-all-start.1) | async-done | bytes 16416 | tf_op jit(solution)/shard_map/all_to_all | solution.py:204
  130.4 0.5 shard_map.103
  130.9 31.3 %all_to_all.21 = bf16[32,24,128]{2,1,0:T(8,128)(2,1)S(1)} all-to-all(bf16[32,24,128]{2,1,0:T(8,128)(2,1)S(1)} %bitcast.31), channel_id=1, replica_groups=mesh['zh'=4,'zl'=4,'core'=2,'x'=4,'y'=4] {'zh','zl','core'}, dimensions={0} | all-to-all | bytes 393216 | tf_op jit(solution)/shard_map/all_to_all | solution.py:215
  162.2 0.0 all-gather.8.cloned.1.call-done
  162.2 0.0 copy-start.1
  162.2 2.5 %copy-done.1 = bf16[5120,512]{1,0:T(8,128)(2,1)S(1)} copy-done((bf16[5120,512]{1,0:T(8,128)(2,1)S(1)}, bf16[5120,512]{1,0:T(8,128)(2,1)}, u32[]{:S(2)}) %copy-start.1) | copy-done | bytes 5242904
  164.7 2.1 %shard_map.104 = bf16[16,160,384]{2,1,0:T(8,128)(2,1)S(1)} custom-call(bf16[768,128]{1,0:T(8,128)(2,1)S(1)} %bitcast.32, bf16[32,160,512]{2,1,0:T(8,128)(2,1)S(1)} %bitcast.26), custom_call_target="tpu_custom_call" | custom-call | tf_op jit(solution)/shard_map/pallas_call | solution.py:55
  166.8 26.7 %all_to_all.22 = bf16[16,160,384]{2,1,0:T(8,128)(2,1)S(1)} all-to-all(bf16[16,160,384]{2,1,0:T(8,128)(2,1)S(1)} %shard_map.104), channel_id=1, replica_groups=mesh['zh'=4,'zl'=4,'core'=2,'x'=4,'y'=4] {'x','y'}, dimensions={0} | all-to-all | bytes 3932160 | tf_op jit(solution)/shard_map/all_to_all | solution.py:222
  193.5 0.0 copy-start.5
  193.5 0.3 convert_reduce_fusion
  193.8 0.1 slice_bitcast_fusion.1
  193.9 0.6 copy-done.5
  194.5 0.9 copy.20
  (3 shorter events, 0.1 us)
Async XLA Ops:
  6.5 1.4 copy-start
  6.5 33.7 %copy-start.3 = (bf16[256,512]{1,0:T(8,128)(2,1)S(1)}, bf16[256,512]{1,0:T(8,128)(2,1)}, u32[]{:S(2)}) copy-start(bf16[256,512]{1,0:T(8,128)(2,1)} %param.13) | copy-start | bytes 786436
  6.5 34.7 %copy-start.4 = (bf16[256,512]{1,0:T(8,128)(2,1)S(1)}, bf16[256,512]{1,0:T(8,128)(2,1)}, u32[]{:S(2)}) copy-start(bf16[256,512]{1,0:T(8,128)(2,1)} %param.12) | copy-start | bytes 786436
  6.5 52.1 %all-gather.6.cloned.1.call-start = ((), (), s32[]{:S(2)}) async-start(), calls=%async_computation.4 | async-start | bytes 1310720 | tf_op jit(solution)/shard_map/all_gather | solution.py:141
  7.3 154.9 %all-gather.8.cloned.1.call-start = ((), (), s32[]{:S(2)}) async-start(), calls=%async_computation.5 | async-start | bytes 5406720 | tf_op jit(solution)/shard_map/all_gather | solution.py:146
  8.8 34.0 %copy-start.6 = (bf16[192,320]{1,0:T(8,128)(2,1)S(1)}, bf16[192,320]{1,0:T(8,128)(2,1)}, u32[]{:S(2)}) copy-start(bf16[192,320]{1,0:T(8,128)(2,1)} %param.19) | copy-start | bytes 368644
  8.8 34.2 %copy-start.8 = (s32[1,128]{1,0:T(1,128)S(1)}, s32[1,128]{1,0:T(1,128)}, u32[]{:S(2)}) copy-start(s32[1,128]{1,0:T(1,128)} %param.17) | copy-start | bytes 1540
  8.8 34.6 %copy-start.7 = (f32[512]{0:T(512)S(1)}, f32[512]{0:T(512)}, u32[]{:S(2)}) copy-start(f32[512]{0:T(512)} %param.14) | copy-start | bytes 6148
  58.6 4.9 %collective-permute-start = (bf16[4,256,512]{2,1,0:T(8,128)(2,1)}, bf16[4,256,512]{2,1,0:T(8,128)(2,1)S(1)}, u32[]{:S(2)}, u32[]{:S(2)}) collective-permute-start(bf16[4,256,512]{2,1,0:T(8,128)(2,1)} %bitcast.29), channel_id=1, source_target_pairs={{0,16},{16,0},{1,17},{17,1},{2,18},{18,2},{3,19},{19,3},{4,20},{20... | collective-permute-start | bytes 3145736 | tf_op jit(solution)/shard_map/ppermute | solution.py:169
  61.2 1.2 copy-start.2
  99.0 0.7 collective-permute-start.1
  100.4 30.0 %all-to-all-start.1 = ((f32[16,2,128]{2,1,0:T(2,128)}), f32[16,2,128]{2,1,0:T(2,128)S(1)}, u32[]{:S(2)}, u32[]{:S(2)}) async-start(f32[16,2,128]{2,1,0:T(2,128)} %shard_map.102), calls=%async_computation.1 | async-start | bytes 32768 | tf_op jit(solution)/shard_map/all_to_all | solution.py:204
  162.2 2.5 %copy-start.1 = (bf16[5120,512]{1,0:T(8,128)(2,1)S(1)}, bf16[5120,512]{1,0:T(8,128)(2,1)}, u32[]{:S(2)}) copy-start(bf16[5120,512]{1,0:T(8,128)(2,1)} %all-gather.8.cloned.1.call-done) | copy-start | bytes 15728644
  193.5 1.0 copy-start.5
Sparse Core Ops, SparseCore 0:
  9.5 49.1 all-gather.5
  60.7 75.7 all-gather.7

commit v14 on v13

--- a/solution.py
+++ b/solution.py
@@ -59,6 +59,27 @@
         out_shape=out_shape,
         compiler_params=pltpu.CompilerParams(vmem_limit_bytes=24 * MIB),
     )(*args)
+
+
+def pick_kernel(position_ref, source_ref, out_ref):
+    count = position_ref.shape[1]
+    token = lax.broadcasted_iota(jnp.int32, (source_ref.shape[0], count), 0)
+    hot = (token == position_ref[...]).astype(jnp.bfloat16)
+    out_ref[...] = lax.dot_general(
+        hot, source_ref[...], (((0,), (0,)), ((), ())), preferred_element_type=jnp.float32
+    ).astype(out_ref.dtype)
+
+
+def finish_kernel(hidden_ref, slope_ref, out_ref):
+    _, height, double = hidden_ref.shape
+    rows = double // 2
+    total = hidden_ref[0].astype(jnp.float32)
+    for share in range(1, hidden_ref.shape[0]):
+        total += hidden_ref[share].astype(jnp.float32)
+    for half in range(2):
+        piece = total[:, half * rows : (half + 1) * rows].T
+        spot = slice(half * height, (half + 1) * height)
+        out_ref[:, spot] = piece * slope_ref[:, spot]
 
 
 def stat_kernel(grad_ref, scaled_ref, square_ref, out_ref):
@@ -139,9 +160,15 @@
     width = embeds.shape[1]
 
     own = lax.all_gather(query_weight, "zl", axis=0)
-    picked = lax.all_gather(jnp.take(grad_query, positions, axis=0, mode="clip"), "zh", axis=0)
-    merge_weight, embeds, grad_resid, img_dest, merge_pre, picked = lax.optimization_barrier(
-        (merge_weight, embeds, grad_resid, img_dest, merge_pre, picked)
+    picked = in_vmem(
+        pick_kernel,
+        jax.ShapeDtypeStruct((image_count, grad_query.shape[1]), jnp.bfloat16),
+        img_pos,
+        grad_query,
+    )
+    picked = lax.all_gather(picked, "zh", axis=0)
+    merge_weight, embeds, grad_resid, img_dest, picked = lax.optimization_barrier(
+        (merge_weight, embeds, grad_resid, img_dest, picked)
     )
     merge_full = lax.all_gather(merge_weight, DP, axis=0)
     inputs = jnp.take(embeds, positions, axis=0, mode="clip").T
@@ -158,12 +185,11 @@
     slot_index = jnp.sum(earlier * dest_hot, axis=1)
     pitch = capacity * (width // LANES)
     target = jnp.where(is_live, target_dev * pitch + slot_index, -groups * pitch)
-    slope = gelu_slope(merge_pre)
 
     scaled_input = gain * wide
-    own, picked, inputs, residual, gain, squares, scaled_input, target, slope = (
+    own, picked, inputs, residual, gain, squares, scaled_input, target = (
         lax.optimization_barrier(
-            (own, picked, inputs, residual, gain, squares, scaled_input, target, slope)
+            (own, picked, inputs, residual, gain, squares, scaled_input, target)
         )
     )
     other = lax.ppermute(own, "core", [(0, 1), (1, 0)])
@@ -212,7 +238,10 @@
         stats,
         target[None],
     )
+    outbox, merge_pre = lax.optimization_barrier((outbox, merge_pre))
+    slope = gelu_slope(merge_pre)
     received = lax.all_to_all(outbox.reshape(groups, pitch, LANES), DP, 0, 0, tiled=True)
+    received, slope = lax.optimization_barrier((received, slope))
     partial_hidden = in_vmem(
         functools.partial(merge_kernel, capacity),
         jax.ShapeDtypeStruct((shares, merge_weight.shape[0], 2 * rows), jnp.bfloat16),
@@ -220,9 +249,12 @@
         merge_full,
     )
     hidden = lax.all_to_all(partial_hidden, TP, 0, 0, tiled=True)
-    hidden = jnp.sum(hidden.astype(jnp.float32), axis=0)
-    hidden = jnp.concatenate([hidden[:, :rows].T, hidden[:, rows:].T], axis=1)
-    return hidden * slope
+    return in_vmem(
+        finish_kernel,
+        jax.ShapeDtypeStruct((rows, columns), jnp.float32),
+        hidden,
+        slope,
+    )
 
 
 def solution(mesh):

time: 204 us -> 204 us (level)
  blocking collectives: 123 us -> 91.7 us
  waiting for transfers between devices: 21.5 us -> 39.5 us
  starting transfers between devices: 26.7 us -> 39.7 us
  Pallas kernels: 5.47 us -> 7.62 us
    all_to_all x1 -> x0, blocking collectives: 31.3 us -> none  [local(): lax.all_to_all(outbox.reshape(groups, pitch, LANES), DP, 0, 0, tiled=True)]
    all_to_all x0 -> x1, waiting for transfers between devices: none -> 17.6 us  [local(): lax.all_to_all(outbox.reshape(groups, pitch, LANES), DP, 0, 0, tiled=True)]
    all_to_all x0 -> x1, starting transfers between devices: none -> 13.1 us  [local(): lax.all_to_all(outbox.reshape(groups, pitch, LANES), DP, 0, 0, tiled=True)]
    pallas_call x5 -> x7, Pallas kernels: 5.47 us -> 7.62 us  [in_vmem(): pl.pallas_call(kernel, in_specs=specs, out_specs=jax.tree.map(lambda _: p...]
    unnamed x18 -> x16, local copies, waits for them, and re-layouts: 4.32 us -> 5.32 us
  transfers between devices with their start and end apart: 5 -> 6, of which waited for: 3 -> 4; matrix products, arithmetic and copies ran while one was open for 3% -> 2% of each run, Pallas kernels for 2% -> 2%
where the time goes in v14:
time: 204 us; the launch traced here: 203 us
  blocking collectives  91.7 us (45%)
  starting transfers between devices  39.7 us (19%)
  waiting for transfers between devices  39.5 us (19%)
  between operations  14.2 us (7%)
  Pallas kernels  7.62 us (4%)
  local copies, waits for them, and re-layouts  7.4 us (4%)
  other arithmetic  2.66 us (1%)
    all_to_all x1, blocking collectives, local(): swapped = lax.all_to_all(partial_value, TP, 0, 0, tiled=True)  33.8 us
    all_gather x1, blocking collectives, local(): picked = lax.all_gather(picked, 'zh', axis=0)  31.2 us
    all_to_all x1, blocking collectives, local(): hidden = lax.all_to_all(partial_hidden, TP, 0, 0, tiled=True)  26.7 us
    all_to_all x1, starting transfers between devices, local(): stats = lax.all_to_all(stats, TP, 0, 0, tiled=True)  23.4 us
    all_to_all x1, waiting for transfers between devices, local(): lax.all_to_all(outbox.reshape(groups, pitch, LANES), DP, 0, 0, tiled=True)  17.6 us
    all_gather x1, waiting for transfers between devices, local(): own = lax.all_gather(query_weight, 'zl', axis=0)  14.5 us
    all_to_all x1, starting transfers between devices, local(): lax.all_to_all(outbox.reshape(groups, pitch, LANES), DP, 0, 0, tiled=True)  13.1 us
    pallas_call x7, Pallas kernels, in_vmem(): pl.pallas_call(kernel, in_specs=specs, out_specs=jax.tree.map(lambda _: p...  7.62 us
  transfers between devices with their start and end apart: 6, of which 4 were waited for; matrix products, arithmetic and copies ran while one was open for 2% of the time, Pallas kernels for 2%

profile of v14, /device:TPU:1, one launch (start us, length us, event | category | flops | bytes accessed | tf_op | source)
XLA Modules:
  0.0 202.7 jit_solution(18057537403434837026)
XLA Ops:
  6.5 0.0 copy-start
  6.5 0.0 copy-start.5
  6.5 0.0 all-gather.6.cloned.1.call-start
  6.5 0.7 all-gather.6.cloned.1.call-update
  7.3 0.0 all-gather.8.cloned.1.call-start
  7.3 0.0 copy-start.3
  7.3 0.9 copy-done.3
  8.3 0.0 copy-start.4
  8.3 0.7 copy-done.4
  8.9 0.0 copy-start.7
  8.9 0.0 copy-start.6
  8.9 0.2 shard_map.100
  9.1 31.2 %all-gather.1 = bf16[512,512]{1,0:T(8,128)(2,1)S(1)} all-gather(bf16[128,512]{1,0:T(8,128)(2,1)S(1)} %shard_map.100), channel_id=3, replica_groups=mesh['zh'=4,'zl'=4,'core'=2,'x'=4,'y'=4] {'zh'}, dimensions={0}, use_global_device_ids=true | all-gather | bytes 655360 | tf_op jit(solution)/shard_map/all_gather | solution.py:169
  40.3 0.0 all-gather.8.cloned.1.call-update
  41.0 0.7 pad_clamp_fusion
  41.7 0.0 copy-done
  41.7 0.8 gather_fusion
  42.5 0.1 copy.13
  42.6 0.0 copy-done.5
  42.7 0.8 gather_fusion.1
  43.5 0.1 copy.14
  43.6 0.0 copy-done.7
  43.7 0.1 fusion.8
  43.8 0.2 reduce_window_sum.11
  43.9 0.2 select_reduce_fusion
  44.1 0.0 copy-done.6
  44.1 0.1 convert_multiply_fusion.4
  44.3 14.5 %all-gather.6.cloned.1.call-done = bf16[1024,512]{1,0:T(8,128)(2,1)} async-done(((bf16[256,512]{1,0:T(8,128)(2,1)}), bf16[1024,512]{1,0:T(8,128)(2,1)}) %all-gather.6.cloned.1.call-update) | async-done | bytes 1048592 | tf_op jit(solution)/shard_map/all_gather | solution.py:162
  58.8 2.5 %collective-permute-start = (bf16[4,256,512]{2,1,0:T(8,128)(2,1)}, bf16[4,256,512]{2,1,0:T(8,128)(2,1)S(1)}, u32[]{:S(2)}, u32[]{:S(2)}) collective-permute-start(bf16[4,256,512]{2,1,0:T(8,128)(2,1)} %bitcast.25), channel_id=1, source_target_pairs={{0,16},{16,0},{1,17},{17,1},{2,18},{18,2},{3,19},{19,3},{4,20},{20... | collective-permute-start | bytes 3145736 | tf_op jit(solution)/shard_map/ppermute | solution.py:195
  61.2 0.1 pad_add_fusion.place_ref
  61.3 0.0 copy-start.2
  61.3 1.2 copy-done.2
  62.5 0.8 shard_map.101
  63.3 0.4 collective-permute-done.weight_ref
  63.7 1.4 shard_map.102
  65.1 33.8 %all_to_all.20 = bf16[16,512,128]{2,1,0:T(8,128)(2,1)S(1)} all-to-all(bf16[16,512,128]{2,1,0:T(8,128)(2,1)S(1)} %bitcast.21), channel_id=1, replica_groups=mesh['zh'=4,'zl'=4,'core'=2,'x'=4,'y'=4] {'x','y'}, dimensions={0} | all-to-all | bytes 4194304 | tf_op jit(solution)/shard_map/all_to_all | solution.py:217
  98.9 0.3 reduce_sum.32
  99.2 0.7 collective-permute-start.1
  99.9 0.0 collective-permute-done.1.grad_ref
  99.9 0.7 shard_map.103
  100.6 23.4 %all-to-all-start.1 = ((f32[16,2,128]{2,1,0:T(2,128)}), f32[16,2,128]{2,1,0:T(2,128)S(1)}, u32[]{:S(2)}, u32[]{:S(2)}) async-start(f32[16,2,128]{2,1,0:T(2,128)} %shard_map.103), calls=%async_computation.1 | async-start | bytes 32768 | tf_op jit(solution)/shard_map/all_to_all | solution.py:230
  124.0 0.1 copy.15.gain_ref
  124.2 6.3 %all-to-all-done.1.stat_ref = f32[16,2,128]{2,1,0:T(2,128)S(1)} async-done(((f32[16,2,128]{2,1,0:T(2,128)}), f32[16,2,128]{2,1,0:T(2,128)S(1)}, u32[]{:S(2)}, u32[]{:S(2)}) %all-to-all-start.1) | async-done | bytes 16416 | tf_op jit(solution)/shard_map/all_to_all | solution.py:230
  130.5 1.1 shard_map.104
  131.6 13.1 %all-to-all-start.2 = ((bf16[32,24,128]{2,1,0:T(8,128)(2,1)}), bf16[32,24,128]{2,1,0:T(8,128)(2,1)S(1)}, u32[]{:S(2)}, u32[]{:S(2)}) async-start(bf16[32,24,128]{2,1,0:T(8,128)(2,1)} %bitcast.13), calls=%async_computation.2 | async-start | bytes 393216 | tf_op jit(solution)/shard_map/all_to_all | solution.py:243
  144.7 1.0 fusion.3.slope_ref
  145.7 17.6 %all-to-all-done.2 = bf16[32,24,128]{2,1,0:T(8,128)(2,1)S(1)} async-done(((bf16[32,24,128]{2,1,0:T(8,128)(2,1)}), bf16[32,24,128]{2,1,0:T(8,128)(2,1)S(1)}, u32[]{:S(2)}, u32[]{:S(2)}) %all-to-all-start.2) | async-done | bytes 196640 | tf_op jit(solution)/shard_map/all_to_all | solution.py:243
  163.3 0.0 all-gather.8.cloned.1.call-done
  163.3 0.0 copy-start.1
  163.3 2.5 %copy-done.1 = bf16[5120,512]{1,0:T(8,128)(2,1)S(1)} copy-done((bf16[5120,512]{1,0:T(8,128)(2,1)S(1)}, bf16[5120,512]{1,0:T(8,128)(2,1)}, u32[]{:S(2)}) %copy-start.1) | copy-done | bytes 5242904
  165.8 2.1 %shard_map.105 = bf16[16,160,384]{2,1,0:T(8,128)(2,1)S(1)} custom-call(bf16[768,128]{1,0:T(8,128)(2,1)S(1)} %bitcast.27, bf16[32,160,512]{2,1,0:T(8,128)(2,1)S(1)} %bitcast.22), custom_call_target="tpu_custom_call" | custom-call | tf_op jit(solution)/shard_map/pallas_call | solution.py:55
  167.9 26.7 %all_to_all.21.hidden_ref = bf16[16,160,384]{2,1,0:T(8,128)(2,1)S(1)} all-to-all(bf16[16,160,384]{2,1,0:T(8,128)(2,1)S(1)} %shard_map.105), channel_id=1, replica_groups=mesh['zh'=4,'zl'=4,'core'=2,'x'=4,'y'=4] {'x','y'}, dimensions={0} | all-to-all | bytes 3932160 | tf_op jit(solution)/shard_map/all_to_all | solution.py:251
  194.6 1.3 shard_map.106
  (2 shorter events, 0.0 us)
Async XLA Ops:
  6.5 35.1 %copy-start = (bf16[256,512]{1,0:T(8,128)(2,1)S(1)}, bf16[256,512]{1,0:T(8,128)(2,1)}, u32[]{:S(2)}) copy-start(bf16[256,512]{1,0:T(8,128)(2,1)} %param.13) | copy-start | bytes 786436
  6.5 36.1 %copy-start.5 = (bf16[256,512]{1,0:T(8,128)(2,1)S(1)}, bf16[256,512]{1,0:T(8,128)(2,1)}, u32[]{:S(2)}) copy-start(bf16[256,512]{1,0:T(8,128)(2,1)} %param.12) | copy-start | bytes 786436
  6.5 52.2 %all-gather.6.cloned.1.call-start = ((), (), s32[]{:S(2)}) async-start(), calls=%async_computation.4 | async-start | bytes 1310720 | tf_op jit(solution)/shard_map/all_gather | solution.py:162
  7.3 156.0 %all-gather.8.cloned.1.call-start = ((), (), s32[]{:S(2)}) async-start(), calls=%async_computation.5 | async-start | bytes 5406720 | tf_op jit(solution)/shard_map/all_gather | solution.py:173
  7.3 1.0 copy-start.3
  8.3 0.7 copy-start.4
  8.9 34.7 %copy-start.7 = (s32[1,128]{1,0:T(1,128)S(1)}, s32[1,128]{1,0:T(1,128)}, u32[]{:S(2)}) copy-start(s32[1,128]{1,0:T(1,128)} %param.17) | copy-start | bytes 1540
  8.9 35.2 %copy-start.6 = (f32[512]{0:T(512)S(1)}, f32[512]{0:T(512)}, u32[]{:S(2)}) copy-start(f32[512]{0:T(512)} %param.14) | copy-start | bytes 6148
  58.8 4.9 %collective-permute-start = (bf16[4,256,512]{2,1,0:T(8,128)(2,1)}, bf16[4,256,512]{2,1,0:T(8,128)(2,1)S(1)}, u32[]{:S(2)}, u32[]{:S(2)}) collective-permute-start(bf16[4,256,512]{2,1,0:T(8,128)(2,1)} %bitcast.25), channel_id=1, source_target_pairs={{0,16},{16,0},{1,17},{17,1},{2,18},{18,2},{3,19},{19,3},{4,20},{20... | collective-permute-start | bytes 3145736 | tf_op jit(solution)/shard_map/ppermute | solution.py:195
  61.3 1.2 copy-start.2
  99.2 0.7 collective-permute-start.1
  100.6 29.9 %all-to-all-start.1 = ((f32[16,2,128]{2,1,0:T(2,128)}), f32[16,2,128]{2,1,0:T(2,128)S(1)}, u32[]{:S(2)}, u32[]{:S(2)}) async-start(f32[16,2,128]{2,1,0:T(2,128)} %shard_map.103), calls=%async_computation.1 | async-start | bytes 32768 | tf_op jit(solution)/shard_map/all_to_all | solution.py:230
  131.6 31.7 %all-to-all-start.2 = ((bf16[32,24,128]{2,1,0:T(8,128)(2,1)}), bf16[32,24,128]{2,1,0:T(8,128)(2,1)S(1)}, u32[]{:S(2)}, u32[]{:S(2)}) async-start(bf16[32,24,128]{2,1,0:T(8,128)(2,1)} %bitcast.13), calls=%async_computation.2 | async-start | bytes 393216 | tf_op jit(solution)/shard_map/all_to_all | solution.py:243
  163.3 2.5 %copy-start.1 = (bf16[5120,512]{1,0:T(8,128)(2,1)S(1)}, bf16[5120,512]{1,0:T(8,128)(2,1)}, u32[]{:S(2)}) copy-start(bf16[5120,512]{1,0:T(8,128)(2,1)} %all-gather.8.cloned.1.call-done) | copy-start | bytes 15728644
Sparse Core Ops, SparseCore 0:
  9.5 49.2 all-gather.5
  60.9 76.0 all-gather.7

commit v15 on v14

--- a/solution.py
+++ b/solution.py
@@ -61,15 +61,6 @@
     )(*args)
 
 
-def pick_kernel(position_ref, source_ref, out_ref):
-    count = position_ref.shape[1]
-    token = lax.broadcasted_iota(jnp.int32, (source_ref.shape[0], count), 0)
-    hot = (token == position_ref[...]).astype(jnp.bfloat16)
-    out_ref[...] = lax.dot_general(
-        hot, source_ref[...], (((0,), (0,)), ((), ())), preferred_element_type=jnp.float32
-    ).astype(out_ref.dtype)
-
-
 def finish_kernel(hidden_ref, slope_ref, out_ref):
     _, height, double = hidden_ref.shape
     rows = double // 2
@@ -96,7 +87,19 @@
     stats = jnp.sum(stat_ref[...], axis=0)
     inverse = lax.rsqrt(stats[0:1] / D + NORM_EPS)
     factor = inverse * inverse * inverse * stats[1:2] / D
-    scaled = gain_ref[...] * grad_ref[...].astype(jnp.float32)
+    equal = lax.broadcasted_iota(jnp.int32, (LANES, LANES), 0) == lax.broadcasted_iota(
+        jnp.int32, (LANES, LANES), 1
+    )
+    gain = jnp.concatenate(
+        [
+            jnp.sum(
+                jnp.where(equal, gain_ref[:, at : at + LANES], 0.0), axis=1, keepdims=True
+            )
+            for at in range(0, width, LANES)
+        ],
+        axis=0,
+    )
+    scaled = gain * grad_ref[...].astype(jnp.float32)
     handoff = (
         resid_ref[...].astype(jnp.float32)
         + inverse * scaled
@@ -159,13 +162,9 @@
     image_count = positions.shape[0]
     width = embeds.shape[1]
 
+    picked = jnp.take(grad_query, positions, axis=0, mode="clip")
+    query_weight, picked = lax.optimization_barrier((query_weight, picked))
     own = lax.all_gather(query_weight, "zl", axis=0)
-    picked = in_vmem(
-        pick_kernel,
-        jax.ShapeDtypeStruct((image_count, grad_query.shape[1]), jnp.bfloat16),
-        img_pos,
-        grad_query,
-    )
     picked = lax.all_gather(picked, "zh", axis=0)
     merge_weight, embeds, grad_resid, img_dest, picked = lax.optimization_barrier(
         (merge_weight, embeds, grad_resid, img_dest, picked)
@@ -187,9 +186,9 @@
     target = jnp.where(is_live, target_dev * pitch + slot_index, -groups * pitch)
 
     scaled_input = gain * wide
-    own, picked, inputs, residual, gain, squares, scaled_input, target = (
+    own, picked, inputs, residual, norm_gain, squares, scaled_input, target = (
         lax.optimization_barrier(
-            (own, picked, inputs, residual, gain, squares, scaled_input, target)
+            (own, picked, inputs, residual, norm_gain, squares, scaled_input, target)
         )
     )
     other = lax.ppermute(own, "core", [(0, 1), (1, 0)])
@@ -234,7 +233,7 @@
         normal_grad,
         inputs,
         residual,
-        gain,
+        norm_gain[None],
         stats,
         target[None],
     )

time: 204 us -> 203 us (level)
  blocking collectives: 91.7 us -> 121 us
  starting transfers between devices: 39.7 us -> 15.9 us
  waiting for transfers between devices: 39.5 us -> 34 us
    all_to_all x0 -> x1, blocking collectives: none -> 29.8 us  [local(): stats = lax.all_to_all(stats, TP, 0, 0, tiled=True)]
    all_to_all x1 -> x0, starting transfers between devices: 23.4 us -> none  [local(): stats = lax.all_to_all(stats, TP, 0, 0, tiled=True)]
    all_to_all x1 -> x0, waiting for transfers between devices: 6.29 us -> none  [local(): stats = lax.all_to_all(stats, TP, 0, 0, tiled=True)]
    pallas_call x7 -> x6, Pallas kernels: 7.62 us -> 6.97 us  [in_vmem(): pl.pallas_call(kernel, in_specs=specs, out_specs=jax.tree.map(lambda _: p...]
  transfers between devices with their start and end apart: 6 -> 5, of which waited for: 4 -> 3; matrix products, arithmetic and copies ran while one was open for 2% -> 2% of each run, Pallas kernels for 2% -> 2%
where the time goes in v15:
time: 203 us; the launch traced here: 201 us
  blocking collectives  121 us (60%)
  waiting for transfers between devices  34 us (17%)
  starting transfers between devices  15.9 us (8%)
  between operations  14.2 us (7%)
  Pallas kernels  6.97 us (3%)
  local copies, waits for them, and re-layouts  6.81 us (3%)
    all_to_all x1, blocking collectives, local(): swapped = lax.all_to_all(partial_value, TP, 0, 0, tiled=True)  33.7 us
    all_gather x1, blocking collectives, local(): picked = lax.all_gather(picked, 'zh', axis=0)  31.2 us
    all_to_all x1, blocking collectives, local(): stats = lax.all_to_all(stats, TP, 0, 0, tiled=True)  29.8 us
    all_to_all x1, blocking collectives, local(): hidden = lax.all_to_all(partial_hidden, TP, 0, 0, tiled=True)  26.7 us
    all_to_all x1, waiting for transfers between devices, local(): lax.all_to_all(outbox.reshape(groups, pitch, LANES), DP, 0, 0, tiled=True)  18.5 us
    all_gather x1, waiting for transfers between devices, local(): own = lax.all_gather(query_weight, 'zl', axis=0)  15.2 us
    all_to_all x1, starting transfers between devices, local(): lax.all_to_all(outbox.reshape(groups, pitch, LANES), DP, 0, 0, tiled=True)  12.7 us
    pallas_call x6, Pallas kernels, in_vmem(): pl.pallas_call(kernel, in_specs=specs, out_specs=jax.tree.map(lambda _: p...  6.97 us
  transfers between devices with their start and end apart: 5, of which 3 were waited for; matrix products, arithmetic and copies ran while one was open for 2% of the time, Pallas kernels for 2%

profile of v15, /device:TPU:1, one launch (start us, length us, event | category | flops | bytes accessed | tf_op | source)
XLA Modules:
  0.0 201.2 jit_solution(9096648552384881815)
XLA Ops:
  6.5 0.0 copy-start
  6.5 0.0 copy-start.5
  6.5 0.0 copy-start.4
  6.5 0.0 all-gather.6.cloned.1.call-start
  6.5 0.7 pad_clamp_fusion
  7.3 0.3 copy-done
  7.6 0.8 gather_fusion
  8.4 0.0 copy-start.7
  8.4 0.0 copy-start.3
  8.5 0.0 all-gather.6.cloned.1.call-update
  8.5 0.0 all-gather.8.cloned.1.call-start
  8.5 31.2 %all-gather.1 = bf16[512,512]{1,0:T(8,128)(2,1)S(1)} all-gather(bf16[128,512]{1,0:T(8,128)(2,1)S(1)} %gather_fusion), channel_id=3, replica_groups=mesh['zh'=4,'zl'=4,'core'=2,'x'=4,'y'=4] {'zh'}, dimensions={0}, use_global_device_ids=true | all-gather | bytes 655360 | tf_op jit(solution)/shard_map/all_gather | solution.py:168
  39.7 0.0 all-gather.8.cloned.1.call-update
  40.4 0.0 copy-done.4
  40.4 0.8 gather_fusion.1
  41.2 0.1 copy.11
  41.4 0.0 copy-done.5
  41.4 0.8 gather_fusion.2
  42.2 0.1 copy.12
  42.4 0.0 copy-done.7
  42.4 0.1 fusion.8
  42.5 0.2 reduce_window_sum.11
  42.7 0.2 select_reduce_fusion
  42.8 0.0 copy-done.3
  42.9 0.1 convert_multiply_fusion.4
  43.0 15.2 %all-gather.6.cloned.1.call-done = bf16[1024,512]{1,0:T(8,128)(2,1)} async-done(((bf16[256,512]{1,0:T(8,128)(2,1)}), bf16[1024,512]{1,0:T(8,128)(2,1)}) %all-gather.6.cloned.1.call-update) | async-done | bytes 1048592 | tf_op jit(solution)/shard_map/all_gather | solution.py:167
  58.2 2.5 %collective-permute-start = (bf16[4,256,512]{2,1,0:T(8,128)(2,1)}, bf16[4,256,512]{2,1,0:T(8,128)(2,1)S(1)}, u32[]{:S(2)}, u32[]{:S(2)}) collective-permute-start(bf16[4,256,512]{2,1,0:T(8,128)(2,1)} %bitcast.25), channel_id=1, source_target_pairs={{0,16},{16,0},{1,17},{17,1},{2,18},{18,2},{3,19},{19,3},{4,20},{20... | collective-permute-start | bytes 3145736 | tf_op jit(solution)/shard_map/ppermute | solution.py:194
  60.6 0.1 pad_add_fusion.place_ref
  60.7 0.0 copy-start.2
  60.7 1.2 copy-done.2
  61.9 0.8 shard_map.100
  62.7 0.4 collective-permute-done.weight_ref
  63.1 1.4 shard_map.101
  64.5 33.7 %all_to_all.20 = bf16[16,512,128]{2,1,0:T(8,128)(2,1)S(1)} all-to-all(bf16[16,512,128]{2,1,0:T(8,128)(2,1)S(1)} %bitcast.21), channel_id=1, replica_groups=mesh['zh'=4,'zl'=4,'core'=2,'x'=4,'y'=4] {'x','y'}, dimensions={0} | all-to-all | bytes 4194304 | tf_op jit(solution)/shard_map/all_to_all | solution.py:216
  98.3 0.0 copy-start.6
  98.3 0.3 reduce_sum.32
  98.5 0.7 collective-permute-start.1
  99.2 0.0 collective-permute-done.1.grad_ref
  99.2 0.1 shard_map.102
  99.3 29.8 %all_to_all.21.stat_ref = f32[16,2,128]{2,1,0:T(2,128)S(1)} all-to-all(f32[16,2,128]{2,1,0:T(2,128)S(1)} %shard_map.102), channel_id=1, replica_groups=mesh['zh'=4,'zl'=4,'core'=2,'x'=4,'y'=4] {'x','y'}, dimensions={0} | all-to-all | bytes 32768 | tf_op jit(solution)/shard_map/all_to_all | solution.py:229
  129.1 1.3 shard_map.103
  130.4 12.7 %all-to-all-start.2 = ((bf16[32,24,128]{2,1,0:T(8,128)(2,1)}), bf16[32,24,128]{2,1,0:T(8,128)(2,1)S(1)}, u32[]{:S(2)}, u32[]{:S(2)}) async-start(bf16[32,24,128]{2,1,0:T(8,128)(2,1)} %bitcast.13), calls=%async_computation.2 | async-start | bytes 393216 | tf_op jit(solution)/shard_map/all_to_all | solution.py:242
  143.1 0.0 copy-done.6
  143.1 0.1 fusion.3.slope_ref
  143.3 18.5 %all-to-all-done.2 = bf16[32,24,128]{2,1,0:T(8,128)(2,1)S(1)} async-done(((bf16[32,24,128]{2,1,0:T(8,128)(2,1)}), bf16[32,24,128]{2,1,0:T(8,128)(2,1)S(1)}, u32[]{:S(2)}, u32[]{:S(2)}) %all-to-all-start.2) | async-done | bytes 196640 | tf_op jit(solution)/shard_map/all_to_all | solution.py:242
  161.8 0.0 all-gather.8.cloned.1.call-done
  161.8 0.0 copy-start.1
  161.8 2.5 %copy-done.1 = bf16[5120,512]{1,0:T(8,128)(2,1)S(1)} copy-done((bf16[5120,512]{1,0:T(8,128)(2,1)S(1)}, bf16[5120,512]{1,0:T(8,128)(2,1)}, u32[]{:S(2)}) %copy-start.1) | copy-done | bytes 5242904
  164.3 2.1 %shard_map.104 = bf16[16,160,384]{2,1,0:T(8,128)(2,1)S(1)} custom-call(bf16[768,128]{1,0:T(8,128)(2,1)S(1)} %bitcast.27, bf16[32,160,512]{2,1,0:T(8,128)(2,1)S(1)} %bitcast.22), custom_call_target="tpu_custom_call" | custom-call | tf_op jit(solution)/shard_map/pallas_call | solution.py:55
  166.4 26.7 %all_to_all.22.hidden_ref = bf16[16,160,384]{2,1,0:T(8,128)(2,1)S(1)} all-to-all(bf16[16,160,384]{2,1,0:T(8,128)(2,1)S(1)} %shard_map.104), channel_id=1, replica_groups=mesh['zh'=4,'zl'=4,'core'=2,'x'=4,'y'=4] {'x','y'}, dimensions={0} | all-to-all | bytes 3932160 | tf_op jit(solution)/shard_map/all_to_all | solution.py:250
  193.1 1.3 shard_map.105
  (2 shorter events, 0.0 us)
Async XLA Ops:
  6.5 1.0 copy-start
  6.5 34.8 %copy-start.5 = (bf16[256,512]{1,0:T(8,128)(2,1)S(1)}, bf16[256,512]{1,0:T(8,128)(2,1)}, u32[]{:S(2)}) copy-start(bf16[256,512]{1,0:T(8,128)(2,1)} %param.12) | copy-start | bytes 786436
  6.5 33.9 %copy-start.4 = (bf16[256,512]{1,0:T(8,128)(2,1)S(1)}, bf16[256,512]{1,0:T(8,128)(2,1)}, u32[]{:S(2)}) copy-start(bf16[256,512]{1,0:T(8,128)(2,1)} %param.13) | copy-start | bytes 786436
  6.5 51.6 %all-gather.6.cloned.1.call-start = ((), (), s32[]{:S(2)}) async-start(), calls=%async_computation.4 | async-start | bytes 1310720 | tf_op jit(solution)/shard_map/all_gather | solution.py:167
  8.4 33.9 %copy-start.7 = (s32[1,128]{1,0:T(1,128)S(1)}, s32[1,128]{1,0:T(1,128)}, u32[]{:S(2)}) copy-start(s32[1,128]{1,0:T(1,128)} %param.17) | copy-start | bytes 1540
  8.4 34.4 %copy-start.3 = (f32[512]{0:T(512)S(1)}, f32[512]{0:T(512)}, u32[]{:S(2)}) copy-start(f32[512]{0:T(512)} %param.14) | copy-start | bytes 6148
  8.5 153.3 %all-gather.8.cloned.1.call-start = ((), (), s32[]{:S(2)}) async-start(), calls=%async_computation.5 | async-start | bytes 5406720 | tf_op jit(solution)/shard_map/all_gather | solution.py:172
  58.2 4.9 %collective-permute-start = (bf16[4,256,512]{2,1,0:T(8,128)(2,1)}, bf16[4,256,512]{2,1,0:T(8,128)(2,1)S(1)}, u32[]{:S(2)}, u32[]{:S(2)}) collective-permute-start(bf16[4,256,512]{2,1,0:T(8,128)(2,1)} %bitcast.25), channel_id=1, source_target_pairs={{0,16},{16,0},{1,17},{17,1},{2,18},{18,2},{3,19},{19,3},{4,20},{20... | collective-permute-start | bytes 3145736 | tf_op jit(solution)/shard_map/ppermute | solution.py:194
  60.7 1.2 copy-start.2
  98.3 44.9 %copy-start.6 = (bf16[192,320]{1,0:T(8,128)(2,1)S(1)}, bf16[192,320]{1,0:T(8,128)(2,1)}, u32[]{:S(2)}) copy-start(bf16[192,320]{1,0:T(8,128)(2,1)} %param.19) | copy-start | bytes 368644
  98.5 0.7 collective-permute-start.1
  130.4 31.4 %all-to-all-start.2 = ((bf16[32,24,128]{2,1,0:T(8,128)(2,1)}), bf16[32,24,128]{2,1,0:T(8,128)(2,1)S(1)}, u32[]{:S(2)}, u32[]{:S(2)}) async-start(bf16[32,24,128]{2,1,0:T(8,128)(2,1)} %bitcast.13), calls=%async_computation.2 | async-start | bytes 393216 | tf_op jit(solution)/shard_map/all_to_all | solution.py:242
  161.8 2.5 %copy-start.1 = (bf16[5120,512]{1,0:T(8,128)(2,1)S(1)}, bf16[5120,512]{1,0:T(8,128)(2,1)}, u32[]{:S(2)}) copy-start(bf16[5120,512]{1,0:T(8,128)(2,1)} %all-gather.8.cloned.1.call-done) | copy-start | bytes 15728644
Sparse Core Ops, SparseCore 0:
  9.5 48.6 all-gather.5
  60.3 76.0 all-gather.7

commit v16 on v15

--- a/solution.py
+++ b/solution.py
@@ -82,7 +82,7 @@
         out_ref[share] = stats
 
 
-def handoff_kernel(capacity, grad_ref, input_ref, resid_ref, gain_ref, stat_ref, target_ref, out_ref):
+def handoff_kernel(capacity, grad_ref, input_ref, resid_ref, gain_ref, stat_ref, target_ref, *out_refs):
     width, count = grad_ref.shape
     stats = jnp.sum(stat_ref[...], axis=0)
     inverse = lax.rsqrt(stats[0:1] / D + NORM_EPS)
@@ -105,20 +105,22 @@
         + inverse * scaled
         - input_ref[...].astype(jnp.float32) * factor
     ).astype(jnp.bfloat16)
-    place = lax.broadcasted_iota(jnp.int32, (out_ref.shape[0], count), 0) - target_ref[...]
-    total = jnp.zeros(out_ref.shape, jnp.float32)
-    for block in range(width // LANES):
-        hot = (place == block * capacity).astype(jnp.bfloat16)
-        total += lax.dot_general(
-            hot,
-            handoff[block * LANES : (block + 1) * LANES],
-            (((1,), (1,)), ((), ())),
-            preferred_element_type=jnp.float32,
-        )
-    out_ref[...] = total.astype(out_ref.dtype)
-
-
-def merge_kernel(capacity, box_ref, weight_ref, out_ref):
+    for number, out_ref in enumerate(out_refs):
+        place = lax.broadcasted_iota(jnp.int32, (out_ref.shape[0], count), 0)
+        place = place - target_ref[number : number + 1]
+        total = jnp.zeros(out_ref.shape, jnp.float32)
+        for block in range(width // LANES):
+            hot = (place == block * capacity).astype(jnp.bfloat16)
+            total += lax.dot_general(
+                hot,
+                handoff[block * LANES : (block + 1) * LANES],
+                (((1,), (1,)), ((), ())),
+                preferred_element_type=jnp.float32,
+            )
+        out_ref[...] = total.astype(out_ref.dtype)
+
+
+def merge_kernel(capacity, place_ref, box_ref, weight_ref, out_ref):
     width = weight_ref.shape[2]
     rows = out_ref.shape[2] // 2
     chunks = width // LANES
@@ -126,7 +128,9 @@
     row = lax.broadcasted_iota(jnp.int32, (rows, box.shape[0]), 0)
     spot = lax.broadcasted_iota(jnp.int32, (rows, box.shape[0]), 1)
     source = (row * 10923) >> 16
-    ahead = spot - (row + source * (capacity * (chunks - 1)))
+    pitch = capacity * chunks
+    crossed = (source & 1) ^ place_ref[0]
+    ahead = spot - (((source >> 1) * 2 + crossed) * pitch + row - source * capacity)
     pieces = []
     for block in range(chunks):
         hot = (ahead == block * capacity).astype(jnp.bfloat16)
@@ -183,7 +187,15 @@
     earlier = jnp.cumsum(dest_hot, axis=0) - dest_hot
     slot_index = jnp.sum(earlier * dest_hot, axis=1)
     pitch = capacity * (width // LANES)
-    target = jnp.where(is_live, target_dev * pitch + slot_index, -groups * pitch)
+    planes = groups // 2
+    crosses = target_dev % 2 != lax.axis_index("core")
+    target = (target_dev // 2) * pitch + slot_index
+    target = jnp.stack(
+        [
+            jnp.where(is_live & ~crosses, target, -planes * pitch),
+            jnp.where(is_live & crosses, target, -planes * pitch),
+        ]
+    )
 
     scaled_input = gain * wide
     own, picked, inputs, residual, norm_gain, squares, scaled_input, target = (
@@ -227,25 +239,31 @@
         squares[None],
     )
     stats = lax.all_to_all(stats, TP, 0, 0, tiled=True)
-    outbox = in_vmem(
+    outbox, across = in_vmem(
         functools.partial(handoff_kernel, capacity),
-        jax.ShapeDtypeStruct((groups * pitch, LANES), jnp.bfloat16),
+        [jax.ShapeDtypeStruct((planes * pitch, LANES), jnp.bfloat16)] * 2,
         normal_grad,
         inputs,
         residual,
         norm_gain[None],
         stats,
-        target[None],
+        target,
     )
     outbox, merge_pre = lax.optimization_barrier((outbox, merge_pre))
     slope = gelu_slope(merge_pre)
-    received = lax.all_to_all(outbox.reshape(groups, pitch, LANES), DP, 0, 0, tiled=True)
+    across = lax.ppermute(across, "core", [(0, 1), (1, 0)])
+    outbox = jnp.concatenate(
+        [box.reshape(planes, pitch, LANES) for box in (outbox, across)], axis=1
+    )
+    received = lax.all_to_all(outbox, ("zh", "zl"), 0, 0, tiled=True)
     received, slope = lax.optimization_barrier((received, slope))
     partial_hidden = in_vmem(
         functools.partial(merge_kernel, capacity),
         jax.ShapeDtypeStruct((shares, merge_weight.shape[0], 2 * rows), jnp.bfloat16),
+        place,
         received.reshape(groups * pitch, LANES),
         merge_full,
+        scalars=True,
     )
     hidden = lax.all_to_all(partial_hidden, TP, 0, 0, tiled=True)
     return in_vmem(

time: 203 us -> 204 us (level)
  the two profiles are of different devices: /device:TPU:1 before, /device:TPU:32 now
where the time goes in v16:
time: 204 us
  blocking collectives  131 us (64%)
  waiting for transfers between devices  27.3 us (13%)
  starting transfers between devices  14.3 us (7%)
  between operations  14.2 us (7%)
  Pallas kernels  6.92 us (3%)
  local copies, waits for them, and re-layouts  6.81 us (3%)
  other arithmetic  3.46 us (2%)
    all_to_all x1, blocking collectives, local(): swapped = lax.all_to_all(partial_value, TP, 0, 0, tiled=True)  35.5 us
    all_gather x1, blocking collectives, local(): picked = lax.all_gather(picked, 'zh', axis=0)  34 us
    all_to_all x1, blocking collectives, local(): stats = lax.all_to_all(stats, TP, 0, 0, tiled=True)  31.8 us
    all_to_all x1, blocking collectives, local(): hidden = lax.all_to_all(partial_hidden, TP, 0, 0, tiled=True)  29.3 us
    all_to_all x1, waiting for transfers between devices, local(): received = lax.all_to_all(outbox, ('zh', 'zl'), 0, 0, tiled=True)  15.2 us
    all_gather x1, waiting for transfers between devices, local(): own = lax.all_gather(query_weight, 'zl', axis=0)  10.1 us
    all_to_all x1, starting transfers between devices, local(): received = lax.all_to_all(outbox, ('zh', 'zl'), 0, 0, tiled=True)  9.76 us
    pallas_call x6, Pallas kernels, in_vmem(): pl.pallas_call(kernel, in_specs=specs, out_specs=jax.tree.map(lambda _: p...  6.92 us
  transfers between devices with their start and end apart: 6, of which 4 were waited for; matrix products, arithmetic and copies ran while one was open for 2% of the time, Pallas kernels for 1%

profile of v16, /device:TPU:32, one launch (start us, length us, event | category | flops | bytes accessed | tf_op | source)
XLA Modules:
  0.0 203.7 jit_solution(13065174655986703263)
XLA Ops:
  6.5 0.0 copy-start
  6.5 0.0 copy-start.5
  6.5 0.0 copy-start.4
  6.5 0.0 all-gather.6.cloned.1.call-start
  6.5 0.7 pad_clamp_fusion
  7.3 0.3 copy-done
  7.6 0.8 gather_fusion
  8.4 0.0 copy-start.6
  8.4 0.0 copy-start.3
  8.5 0.0 all-gather.6.cloned.1.call-update
  8.5 0.0 all-gather.8.cloned.1.call-start
  8.5 34.0 %all-gather.1 = bf16[512,512]{1,0:T(8,128)(2,1)S(1)} all-gather(bf16[128,512]{1,0:T(8,128)(2,1)S(1)} %gather_fusion), channel_id=3, replica_groups=mesh['zh'=4,'zl'=4,'core'=2,'x'=4,'y'=4] {'zh'}, dimensions={0}, use_global_device_ids=true | all-gather | bytes 655360 | tf_op jit(solution)/shard_map/all_gather | solution.py:172
  42.6 0.0 all-gather.8.cloned.1.call-update
  43.2 0.0 copy-done.4
  43.2 0.8 gather_fusion.1
  44.1 0.1 copy.11
  44.2 0.0 copy-done.5
  44.2 0.8 gather_fusion.2
  45.1 0.1 copy.12
  45.2 0.0 copy-done.6
  45.2 0.1 fusion.8
  45.3 0.2 reduce_window_sum.11
  45.5 0.2 select_reduce_fusion
  45.7 0.0 copy-done.3
  45.8 0.1 convert_multiply_fusion.4
  45.9 10.1 %all-gather.6.cloned.1.call-done = bf16[1024,512]{1,0:T(8,128)(2,1)} async-done(((bf16[256,512]{1,0:T(8,128)(2,1)}), bf16[1024,512]{1,0:T(8,128)(2,1)}) %all-gather.6.cloned.1.call-update) | async-done | bytes 1048592 | tf_op jit(solution)/shard_map/all_gather | solution.py:171
  56.0 2.0 collective-permute-start
  58.0 0.1 pad_add_fusion.1.place_ref
  58.0 0.0 copy-start.2
  58.1 1.2 copy-done.2
  59.3 0.8 shard_map.100
  60.1 0.7 collective-permute-done.weight_ref
  60.8 1.4 shard_map.101
  62.2 35.5 %all_to_all.20 = bf16[16,512,128]{2,1,0:T(8,128)(2,1)S(1)} all-to-all(bf16[16,512,128]{2,1,0:T(8,128)(2,1)S(1)} %bitcast.24), channel_id=1, replica_groups=mesh['zh'=4,'zl'=4,'core'=2,'x'=4,'y'=4] {'x','y'}, dimensions={0} | all-to-all | bytes 4194304 | tf_op jit(solution)/shard_map/all_to_all | solution.py:228
  97.7 0.3 reduce_sum.35
  98.0 0.7 collective-permute-start.1
  98.6 0.0 collective-permute-done.1.grad_ref
  98.6 0.1 shard_map.102
  98.7 31.8 %all_to_all.21.stat_ref = f32[16,2,128]{2,1,0:T(2,128)S(1)} all-to-all(f32[16,2,128]{2,1,0:T(2,128)S(1)} %shard_map.102), channel_id=1, replica_groups=mesh['zh'=4,'zl'=4,'core'=2,'x'=4,'y'=4] {'x','y'}, dimensions={0} | all-to-all | bytes 32768 | tf_op jit(solution)/shard_map/all_to_all | solution.py:241
  130.6 0.7 shard_map.103
  131.2 1.9 collective-permute-start.2
  133.2 1.3 collective-permute-done.2
  134.4 0.7 pad_maximum_fusion
  135.1 9.8 %all-to-all-start.2 = ((bf16[16,48,128]{2,1,0:T(8,128)(2,1)}), bf16[16,48,128]{2,1,0:T(8,128)(2,1)S(1)}, u32[]{:S(2)}, u32[]{:S(2)}) async-start(bf16[16,48,128]{2,1,0:T(8,128)(2,1)} %pad_maximum_fusion), calls=%async_computation.2 | async-start | bytes 393216 | tf_op jit(solution)/shard_map/all_to_all | solution.py:258
  144.9 1.0 fusion.3.slope_ref
  145.9 15.2 %all-to-all-done.2 = bf16[16,48,128]{2,1,0:T(8,128)(2,1)S(1)} async-done(((bf16[16,48,128]{2,1,0:T(8,128)(2,1)}), bf16[16,48,128]{2,1,0:T(8,128)(2,1)S(1)}, u32[]{:S(2)}, u32[]{:S(2)}) %all-to-all-start.2) | async-done | bytes 196640 | tf_op jit(solution)/shard_map/all_to_all | solution.py:258
  161.1 0.0 all-gather.8.cloned.1.call-done
  161.1 0.0 copy-start.1
  161.1 2.5 %copy-done.1 = bf16[5120,512]{1,0:T(8,128)(2,1)S(1)} copy-done((bf16[5120,512]{1,0:T(8,128)(2,1)S(1)}, bf16[5120,512]{1,0:T(8,128)(2,1)}, u32[]{:S(2)}) %copy-start.1) | copy-done | bytes 5242904
  163.6 2.7 %shard_map.104 = bf16[16,160,384]{2,1,0:T(8,128)(2,1)S(1)} custom-call(s32[2]{0:T(128)S(1)} %pad_add_fusion.1.place_ref, bf16[768,128]{1,0:T(8,128)(2,1)S(1)} %bitcast.30, bf16[32,160,512]{2,1,0:T(8,128)(2,1)S(1)} %bitcast.25), custom_call_target="tpu_custom_call" | custom-call | tf_op jit(solution)/shard_map/pallas_call | solution.py:55
  166.3 29.3 %all_to_all.22.hidden_ref = bf16[16,160,384]{2,1,0:T(8,128)(2,1)S(1)} all-to-all(bf16[16,160,384]{2,1,0:T(8,128)(2,1)S(1)} %shard_map.104), channel_id=1, replica_groups=mesh['zh'=4,'zl'=4,'core'=2,'x'=4,'y'=4] {'x','y'}, dimensions={0} | all-to-all | bytes 3932160 | tf_op jit(solution)/shard_map/all_to_all | solution.py:268
  195.6 1.3 shard_map.105
  (4 shorter events, 0.0 us)
Async XLA Ops:
  6.5 1.0 copy-start
  6.5 37.7 %copy-start.5 = (bf16[256,512]{1,0:T(8,128)(2,1)S(1)}, bf16[256,512]{1,0:T(8,128)(2,1)}, u32[]{:S(2)}) copy-start(bf16[256,512]{1,0:T(8,128)(2,1)} %param.12) | copy-start | bytes 786436
  6.5 36.7 %copy-start.4 = (bf16[256,512]{1,0:T(8,128)(2,1)S(1)}, bf16[256,512]{1,0:T(8,128)(2,1)}, u32[]{:S(2)}) copy-start(bf16[256,512]{1,0:T(8,128)(2,1)} %param.13) | copy-start | bytes 786436
  6.5 49.5 %all-gather.6.cloned.1.call-start = ((), (), s32[]{:S(2)}) async-start(), calls=%async_computation.4 | async-start | bytes 1310720 | tf_op jit(solution)/shard_map/all_gather | solution.py:171
  8.4 36.8 %copy-start.6 = (s32[1,128]{1,0:T(1,128)S(1)}, s32[1,128]{1,0:T(1,128)}, u32[]{:S(2)}) copy-start(s32[1,128]{1,0:T(1,128)} %param.17) | copy-start | bytes 1540
  8.4 37.3 %copy-start.3 = (f32[512]{0:T(512)S(1)}, f32[512]{0:T(512)}, u32[]{:S(2)}) copy-start(f32[512]{0:T(512)} %param.14) | copy-start | bytes 6148
  8.5 152.6 %all-gather.8.cloned.1.call-start = ((), (), s32[]{:S(2)}) async-start(), calls=%async_computation.5 | async-start | bytes 5406720 | tf_op jit(solution)/shard_map/all_gather | solution.py:176
  56.0 4.8 %collective-permute-start = (bf16[4,256,512]{2,1,0:T(8,128)(2,1)}, bf16[4,256,512]{2,1,0:T(8,128)(2,1)S(1)}, u32[]{:S(2)}, u32[]{:S(2)}) collective-permute-start(bf16[4,256,512]{2,1,0:T(8,128)(2,1)} %bitcast.28), channel_id=1, source_target_pairs={{0,16},{16,0},{1,17},{17,1},{2,18},{18,2},{3,19},{19,3},{4,20},{20... | collective-permute-start | bytes 3145736 | tf_op jit(solution)/shard_map/ppermute | solution.py:206
  58.0 1.2 copy-start.2
  98.0 0.7 collective-permute-start.1
  131.2 3.2 %collective-permute-start.2 = (bf16[384,128]{1,0:T(8,128)(2,1)S(1)}, bf16[384,128]{1,0:T(8,128)(2,1)S(1)}, u32[]{:S(2)}, u32[]{:S(2)}) collective-permute-start(bf16[384,128]{1,0:T(8,128)(2,1)S(1)} %get-tuple-element.46), channel_id=1, source_target_pairs={{0,16},{16,0},{1,17},{17,1},{2,18},{18,2},{3,19},{19,3},{4,20},{20... | collective-permute-start | bytes 294920 | tf_op jit(solution)/shard_map/ppermute | solution.py:254
  135.1 26.0 %all-to-all-start.2 = ((bf16[16,48,128]{2,1,0:T(8,128)(2,1)}), bf16[16,48,128]{2,1,0:T(8,128)(2,1)S(1)}, u32[]{:S(2)}, u32[]{:S(2)}) async-start(bf16[16,48,128]{2,1,0:T(8,128)(2,1)} %pad_maximum_fusion), calls=%async_computation.2 | async-start | bytes 393216 | tf_op jit(solution)/shard_map/all_to_all | solution.py:258
  161.1 2.5 %copy-start.1 = (bf16[5120,512]{1,0:T(8,128)(2,1)S(1)}, bf16[5120,512]{1,0:T(8,128)(2,1)}, u32[]{:S(2)}) copy-start(bf16[5120,512]{1,0:T(8,128)(2,1)} %all-gather.8.cloned.1.call-done) | copy-start | bytes 15728644
Sparse Core Ops, SparseCore 0:
  9.5 46.5 all-gather.5
  58.1 75.9 all-gather.7

commit v17 on v15

--- a/solution.py
+++ b/solution.py
@@ -1,5 +1,3 @@
-import functools
-
 import jax
 import jax.numpy as jnp
 from jax import lax
@@ -12,6 +10,7 @@
 NORM_EPS = 1e-06
 MIB = 1024 * 1024
 LANES = 128
+SLOT_PITCH = 8
 DP = ("zh", "zl", "core")
 TP = ("x", "y")
 
@@ -61,16 +60,26 @@
     )(*args)
 
 
-def finish_kernel(hidden_ref, slope_ref, out_ref):
-    _, height, double = hidden_ref.shape
-    rows = double // 2
-    total = hidden_ref[0].astype(jnp.float32)
-    for share in range(1, hidden_ref.shape[0]):
-        total += hidden_ref[share].astype(jnp.float32)
-    for half in range(2):
-        piece = total[:, half * rows : (half + 1) * rows].T
-        spot = slice(half * height, (half + 1) * height)
-        out_ref[:, spot] = piece * slope_ref[:, spot]
+def send_kernel(hidden_ref, target_ref, out_ref):
+    count = target_ref.shape[1]
+    total = jnp.sum(hidden_ref[...].astype(jnp.float32), axis=0).astype(jnp.bfloat16)
+    spare = out_ref.shape[1] - 2 * total.shape[0]
+    columns = jnp.concatenate(
+        [total[:, :count], total[:, count:], jnp.zeros((spare, count), jnp.bfloat16)], axis=0
+    )
+    row = lax.broadcasted_iota(jnp.int32, (out_ref.shape[0], count), 0)
+    hot = (row == target_ref[...]).astype(jnp.bfloat16)
+    out_ref[...] = lax.dot_general(
+        hot, columns, (((1,), (1,)), ((), ())), preferred_element_type=jnp.float32
+    ).astype(out_ref.dtype)
+
+
+def finish_kernel(box_ref, spot_ref, slope_ref, out_ref):
+    rows, columns = out_ref.shape
+    spot = lax.broadcasted_iota(jnp.int32, (rows, box_ref.shape[0]), 1)
+    hot = (spot == spot_ref[...]).astype(jnp.bfloat16)
+    hidden = jnp.dot(hot, box_ref[...], preferred_element_type=jnp.float32)
+    out_ref[...] = hidden[:, :columns] * slope_ref[...]
 
 
 def stat_kernel(grad_ref, scaled_ref, square_ref, out_ref):
@@ -82,7 +91,7 @@
         out_ref[share] = stats
 
 
-def handoff_kernel(capacity, grad_ref, input_ref, resid_ref, gain_ref, stat_ref, target_ref, out_ref):
+def merge_kernel(grad_ref, input_ref, resid_ref, gain_ref, stat_ref, weight_ref, out_ref):
     width, count = grad_ref.shape
     stats = jnp.sum(stat_ref[...], axis=0)
     inverse = lax.rsqrt(stats[0:1] / D + NORM_EPS)
@@ -105,40 +114,12 @@
         + inverse * scaled
         - input_ref[...].astype(jnp.float32) * factor
     ).astype(jnp.bfloat16)
-    place = lax.broadcasted_iota(jnp.int32, (out_ref.shape[0], count), 0) - target_ref[...]
-    total = jnp.zeros(out_ref.shape, jnp.float32)
-    for block in range(width // LANES):
-        hot = (place == block * capacity).astype(jnp.bfloat16)
-        total += lax.dot_general(
-            hot,
-            handoff[block * LANES : (block + 1) * LANES],
-            (((1,), (1,)), ((), ())),
-            preferred_element_type=jnp.float32,
-        )
-    out_ref[...] = total.astype(out_ref.dtype)
-
-
-def merge_kernel(capacity, box_ref, weight_ref, out_ref):
-    width = weight_ref.shape[2]
-    rows = out_ref.shape[2] // 2
-    chunks = width // LANES
-    box = box_ref[...]
-    row = lax.broadcasted_iota(jnp.int32, (rows, box.shape[0]), 0)
-    spot = lax.broadcasted_iota(jnp.int32, (rows, box.shape[0]), 1)
-    source = (row * 10923) >> 16
-    ahead = spot - (row + source * (capacity * (chunks - 1)))
-    pieces = []
-    for block in range(chunks):
-        hot = (ahead == block * capacity).astype(jnp.bfloat16)
-        piece = jnp.dot(hot, box, preferred_element_type=jnp.float32)
-        pieces.append(piece.T.astype(jnp.bfloat16))
-    turned = jnp.concatenate(pieces, axis=0)
     for share in range(out_ref.shape[0]):
         for half in range(2):
             product = jnp.dot(
-                weight_ref[2 * share + half], turned, preferred_element_type=jnp.float32
+                weight_ref[2 * share + half], handoff, preferred_element_type=jnp.float32
             )
-            out_ref[share, :, half * rows : (half + 1) * rows] = product.astype(out_ref.dtype)
+            out_ref[share, :, half * count : (half + 1) * count] = product.astype(out_ref.dtype)
 
 
 def local(
@@ -182,13 +163,13 @@
     ).astype(jnp.int32)
     earlier = jnp.cumsum(dest_hot, axis=0) - dest_hot
     slot_index = jnp.sum(earlier * dest_hot, axis=1)
-    pitch = capacity * (width // LANES)
-    target = jnp.where(is_live, target_dev * pitch + slot_index, -groups * pitch)
-
+    target = jnp.where(is_live, target_dev * SLOT_PITCH + slot_index, -1)
+    number = jnp.arange(rows, dtype=jnp.int32)
+    spot = number // capacity * SLOT_PITCH + number % capacity
     scaled_input = gain * wide
-    own, picked, inputs, residual, norm_gain, squares, scaled_input, target = (
+    own, picked, inputs, residual, norm_gain, squares, scaled_input, target, spot = (
         lax.optimization_barrier(
-            (own, picked, inputs, residual, norm_gain, squares, scaled_input, target)
+            (own, picked, inputs, residual, norm_gain, squares, scaled_input, target, spot)
         )
     )
     other = lax.ppermute(own, "core", [(0, 1), (1, 0)])
@@ -227,31 +208,32 @@
         squares[None],
     )
     stats = lax.all_to_all(stats, TP, 0, 0, tiled=True)
-    outbox = in_vmem(
-        functools.partial(handoff_kernel, capacity),
-        jax.ShapeDtypeStruct((groups * pitch, LANES), jnp.bfloat16),
+    partial_hidden = in_vmem(
+        merge_kernel,
+        jax.ShapeDtypeStruct((shares, merge_weight.shape[0], 2 * image_count), jnp.bfloat16),
         normal_grad,
         inputs,
         residual,
         norm_gain[None],
         stats,
+        merge_full,
+    )
+    hidden = lax.all_to_all(partial_hidden, TP, 0, 0, tiled=True)
+    lanes = -(-columns // LANES) * LANES
+    outbox = in_vmem(
+        send_kernel,
+        jax.ShapeDtypeStruct((groups * SLOT_PITCH, lanes), jnp.bfloat16),
+        hidden,
         target[None],
     )
     outbox, merge_pre = lax.optimization_barrier((outbox, merge_pre))
     slope = gelu_slope(merge_pre)
-    received = lax.all_to_all(outbox.reshape(groups, pitch, LANES), DP, 0, 0, tiled=True)
-    received, slope = lax.optimization_barrier((received, slope))
-    partial_hidden = in_vmem(
-        functools.partial(merge_kernel, capacity),
-        jax.ShapeDtypeStruct((shares, merge_weight.shape[0], 2 * rows), jnp.bfloat16),
-        received.reshape(groups * pitch, LANES),
-        merge_full,
-    )
-    hidden = lax.all_to_all(partial_hidden, TP, 0, 0, tiled=True)
+    received = lax.all_to_all(outbox.reshape(groups, SLOT_PITCH, lanes), DP, 0, 0, tiled=True)
     return in_vmem(
         finish_kernel,
         jax.ShapeDtypeStruct((rows, columns), jnp.float32),
-        hidden,
+        received.reshape(groups * SLOT_PITCH, lanes),
+        spot[:, None],
         slope,
     )
 

time: 203 us -> 207 us (1.020)
  waiting for transfers between devices: 34 us -> 41.1 us
  starting transfers between devices: 15.9 us -> 12 us
  blocking collectives: 121 us -> 124 us
    all_gather x1, waiting for transfers between devices: 0.01 us -> 7.22 us  [local(): merge_full = lax.all_gather(merge_weight, DP, axis=0)]
    all_to_all x1, starting transfers between devices: 12.7 us -> 8.83 us  [local(): lax.all_to_all(outbox.reshape(groups, SLOT_PITCH, lanes), DP, 0, 0, tiled...]
    all_to_all x1, blocking collectives: 26.7 us -> 29.5 us  [local(): hidden = lax.all_to_all(partial_hidden, TP, 0, 0, tiled=True)]
  transfers between devices with their start and end apart: 5 -> 5, of which waited for: 3 -> 4; matrix products, arithmetic and copies ran while one was open for 2% -> 2% of each run, Pallas kernels for 2% -> 1%
where the time goes in v17:
time: 207 us; the launch traced here: 206 us
  blocking collectives  124 us (60%)
  waiting for transfers between devices  41.1 us (20%)
  between operations  14.2 us (7%)
  starting transfers between devices  12 us (6%)
  local copies, waits for them, and re-layouts  6.93 us (3%)
  Pallas kernels  6.05 us (3%)
    all_to_all x1, blocking collectives, local(): swapped = lax.all_to_all(partial_value, TP, 0, 0, tiled=True)  33.7 us
    all_gather x1, blocking collectives, local(): picked = lax.all_gather(picked, 'zh', axis=0)  31.2 us
    all_to_all x1, blocking collectives, local(): stats = lax.all_to_all(stats, TP, 0, 0, tiled=True)  29.8 us
    all_to_all x1, blocking collectives, local(): hidden = lax.all_to_all(partial_hidden, TP, 0, 0, tiled=True)  29.5 us
    all_to_all x1, waiting for transfers between devices, local(): lax.all_to_all(outbox.reshape(groups, SLOT_PITCH, lanes), DP, 0, 0, tiled...  18.4 us
    all_gather x1, waiting for transfers between devices, local(): own = lax.all_gather(query_weight, 'zl', axis=0)  15.1 us
    all_to_all x1, starting transfers between devices, local(): lax.all_to_all(outbox.reshape(groups, SLOT_PITCH, lanes), DP, 0, 0, tiled...  8.83 us
    all_gather x1, waiting for transfers between devices, local(): merge_full = lax.all_gather(merge_weight, DP, axis=0)  7.22 us
  transfers between devices with their start and end apart: 5, of which 4 were waited for; matrix products, arithmetic and copies ran while one was open for 2% of the time, Pallas kernels for 1%

profile of v17, /device:TPU:1, one launch (start us, length us, event | category | flops | bytes accessed | tf_op | source)
XLA Modules:
  0.0 206.4 jit_solution(12910453263065918630)
XLA Ops:
  6.5 0.0 copy-start
  6.5 0.0 copy-start.5
  6.5 0.0 copy-start.4
  6.5 0.0 all-gather.6.cloned.1.call-start
  6.5 0.7 pad_clamp_fusion
  7.3 0.3 copy-done
  7.6 0.8 gather_fusion
  8.4 0.0 copy-start.7
  8.4 0.0 copy-start.3
  8.5 0.0 all-gather.6.cloned.1.call-update
  8.5 0.0 all-gather.8.cloned.1.call-start
  8.5 31.2 %all-gather.1 = bf16[512,512]{1,0:T(8,128)(2,1)S(1)} all-gather(bf16[128,512]{1,0:T(8,128)(2,1)S(1)} %gather_fusion), channel_id=3, replica_groups=mesh['zh'=4,'zl'=4,'core'=2,'x'=4,'y'=4] {'zh'}, dimensions={0}, use_global_device_ids=true | all-gather | bytes 655360 | tf_op jit(solution)/shard_map/all_gather | solution.py:149
  39.7 0.0 all-gather.8.cloned.1.call-update
  40.4 0.0 copy-done.4
  40.4 0.8 gather_fusion.1
  41.2 0.1 copy.13
  41.4 0.0 copy-done.5
  41.4 0.8 gather_fusion.2
  42.2 0.1 copy.14
  42.4 0.0 copy-done.7
  42.4 0.1 fusion.8
  42.5 0.2 reduce_window_sum.11
  42.7 0.2 select_reduce_fusion
  42.9 0.0 copy-done.3
  42.9 0.1 convert_multiply_fusion.4
  43.0 15.1 %all-gather.6.cloned.1.call-done = bf16[1024,512]{1,0:T(8,128)(2,1)} async-done(((bf16[256,512]{1,0:T(8,128)(2,1)}), bf16[1024,512]{1,0:T(8,128)(2,1)}) %all-gather.6.cloned.1.call-update) | async-done | bytes 1048592 | tf_op jit(solution)/shard_map/all_gather | solution.py:148
  58.2 2.5 %collective-permute-start = (bf16[4,256,512]{2,1,0:T(8,128)(2,1)}, bf16[4,256,512]{2,1,0:T(8,128)(2,1)S(1)}, u32[]{:S(2)}, u32[]{:S(2)}) collective-permute-start(bf16[4,256,512]{2,1,0:T(8,128)(2,1)} %bitcast.26), channel_id=1, source_target_pairs={{0,16},{16,0},{1,17},{17,1},{2,18},{18,2},{3,19},{19,3},{4,20},{20... | collective-permute-start | bytes 3145736 | tf_op jit(solution)/shard_map/ppermute | solution.py:175
  60.6 0.1 pad_add_fusion.place_ref
  60.7 0.0 copy-start.2
  60.7 1.2 copy-done.2
  61.9 0.8 shard_map.100
  62.7 0.4 collective-permute-done.weight_ref
  63.1 1.4 shard_map.101
  64.5 33.7 %all_to_all.20 = bf16[16,512,128]{2,1,0:T(8,128)(2,1)S(1)} all-to-all(bf16[16,512,128]{2,1,0:T(8,128)(2,1)S(1)} %bitcast.22), channel_id=1, replica_groups=mesh['zh'=4,'zl'=4,'core'=2,'x'=4,'y'=4] {'x','y'}, dimensions={0} | all-to-all | bytes 4194304 | tf_op jit(solution)/shard_map/all_to_all | solution.py:197
  98.3 0.3 reduce_sum.32
  98.5 0.7 collective-permute-start.1
  99.2 0.0 collective-permute-done.1.grad_ref
  99.2 0.1 shard_map.102
  99.3 29.8 %all_to_all.21.stat_ref = f32[16,2,128]{2,1,0:T(2,128)S(1)} all-to-all(f32[16,2,128]{2,1,0:T(2,128)S(1)} %shard_map.102), channel_id=1, replica_groups=mesh['zh'=4,'zl'=4,'core'=2,'x'=4,'y'=4] {'x','y'}, dimensions={0} | all-to-all | bytes 32768 | tf_op jit(solution)/shard_map/all_to_all | solution.py:210
  129.1 7.2 %all-gather.8.cloned.1.call-done = bf16[5120,512]{1,0:T(8,128)(2,1)} async-done(((bf16[160,512]{1,0:T(8,128)(2,1)}), bf16[5120,512]{1,0:T(8,128)(2,1)}) %all-gather.8.cloned.1.call-update) | async-done | bytes 5242896 | tf_op jit(solution)/shard_map/all_gather | solution.py:153
  136.3 0.0 copy-start.1
  136.3 2.5 %copy-done.1 = bf16[5120,512]{1,0:T(8,128)(2,1)S(1)} copy-done((bf16[5120,512]{1,0:T(8,128)(2,1)S(1)}, bf16[5120,512]{1,0:T(8,128)(2,1)}, u32[]{:S(2)}) %copy-start.1) | copy-done | bytes 5242904
  138.8 1.8 shard_map.103
  140.6 0.0 copy-start.6
  140.6 29.5 %all_to_all.22.hidden_ref = bf16[16,160,256]{2,1,0:T(8,128)(2,1)S(1)} all-to-all(bf16[16,160,256]{2,1,0:T(8,128)(2,1)S(1)} %shard_map.103), channel_id=1, replica_groups=mesh['zh'=4,'zl'=4,'core'=2,'x'=4,'y'=4] {'x','y'}, dimensions={0} | all-to-all | bytes 2621440 | tf_op jit(solution)/shard_map/all_to_all | solution.py:221
  170.0 1.0 shard_map.104
  171.1 8.8 %all-to-all-start.3 = ((bf16[32,8,384]{2,1,0:T(8,128)(2,1)}), bf16[32,8,384]{2,1,0:T(8,128)(2,1)S(1)}, u32[]{:S(2)}, u32[]{:S(2)}) async-start(bf16[32,8,384]{2,1,0:T(8,128)(2,1)} %bitcast.14), calls=%async_computation.3 | async-start | bytes 393216 | tf_op jit(solution)/shard_map/all_to_all | solution.py:231
  179.9 0.1 copy.15.spot_ref
  180.1 0.0 copy-done.6
  180.1 0.1 fusion.3.slope_ref
  180.2 18.4 %all-to-all-done.3 = bf16[32,8,384]{2,1,0:T(8,128)(2,1)S(1)} async-done(((bf16[32,8,384]{2,1,0:T(8,128)(2,1)}), bf16[32,8,384]{2,1,0:T(8,128)(2,1)S(1)}, u32[]{:S(2)}, u32[]{:S(2)}) %all-to-all-start.3) | async-done | bytes 196640 | tf_op jit(solution)/shard_map/all_to_all | solution.py:231
  198.6 1.0 shard_map.105
  (3 shorter events, 0.0 us)
Async XLA Ops:
  6.5 1.0 copy-start
  6.5 34.8 %copy-start.5 = (bf16[256,512]{1,0:T(8,128)(2,1)S(1)}, bf16[256,512]{1,0:T(8,128)(2,1)}, u32[]{:S(2)}) copy-start(bf16[256,512]{1,0:T(8,128)(2,1)} %param.12) | copy-start | bytes 786436
  6.5 33.9 %copy-start.4 = (bf16[256,512]{1,0:T(8,128)(2,1)S(1)}, bf16[256,512]{1,0:T(8,128)(2,1)}, u32[]{:S(2)}) copy-start(bf16[256,512]{1,0:T(8,128)(2,1)} %param.13) | copy-start | bytes 786436
  6.5 51.6 %all-gather.6.cloned.1.call-start = ((), (), s32[]{:S(2)}) async-start(), calls=%async_computation.4 | async-start | bytes 1310720 | tf_op jit(solution)/shard_map/all_gather | solution.py:148
  8.4 33.9 %copy-start.7 = (s32[1,128]{1,0:T(1,128)S(1)}, s32[1,128]{1,0:T(1,128)}, u32[]{:S(2)}) copy-start(s32[1,128]{1,0:T(1,128)} %param.17) | copy-start | bytes 1540
  8.4 34.4 %copy-start.3 = (f32[512]{0:T(512)S(1)}, f32[512]{0:T(512)}, u32[]{:S(2)}) copy-start(f32[512]{0:T(512)} %param.14) | copy-start | bytes 6148
  8.5 127.9 %all-gather.8.cloned.1.call-start = ((), (), s32[]{:S(2)}) async-start(), calls=%async_computation.5 | async-start | bytes 5406720 | tf_op jit(solution)/shard_map/all_gather | solution.py:153
  58.2 4.9 %collective-permute-start = (bf16[4,256,512]{2,1,0:T(8,128)(2,1)}, bf16[4,256,512]{2,1,0:T(8,128)(2,1)S(1)}, u32[]{:S(2)}, u32[]{:S(2)}) collective-permute-start(bf16[4,256,512]{2,1,0:T(8,128)(2,1)} %bitcast.26), channel_id=1, source_target_pairs={{0,16},{16,0},{1,17},{17,1},{2,18},{18,2},{3,19},{19,3},{4,20},{20... | collective-permute-start | bytes 3145736 | tf_op jit(solution)/shard_map/ppermute | solution.py:175
  60.7 1.2 copy-start.2
  98.5 0.7 collective-permute-start.1
  136.3 2.5 %copy-start.1 = (bf16[5120,512]{1,0:T(8,128)(2,1)S(1)}, bf16[5120,512]{1,0:T(8,128)(2,1)}, u32[]{:S(2)}) copy-start(bf16[5120,512]{1,0:T(8,128)(2,1)} %all-gather.8.cloned.1.call-done) | copy-start | bytes 15728644
  140.6 39.5 %copy-start.6 = (bf16[192,320]{1,0:T(8,128)(2,1)S(1)}, bf16[192,320]{1,0:T(8,128)(2,1)}, u32[]{:S(2)}) copy-start(bf16[192,320]{1,0:T(8,128)(2,1)} %param.19) | copy-start | bytes 368644
  171.1 27.5 %all-to-all-start.3 = ((bf16[32,8,384]{2,1,0:T(8,128)(2,1)}), bf16[32,8,384]{2,1,0:T(8,128)(2,1)S(1)}, u32[]{:S(2)}, u32[]{:S(2)}) async-start(bf16[32,8,384]{2,1,0:T(8,128)(2,1)} %bitcast.14), calls=%async_computation.3 | async-start | bytes 393216 | tf_op jit(solution)/shard_map/all_to_all | solution.py:231
Sparse Core Ops, SparseCore 0:
  9.5 48.6 all-gather.5
  60.3 76.0 all-gather.7
